TPU v7x, 512 devices: a whole 4x4x16 slice. The times are simulated.
512 devices in a mesh: col: 32 (over x, z_lo, core), row: 16 (over z_hi, y).
Axes of the slice: x: 4, y: 4, z: 16 (z_hi: 4, z_lo: 4; z = z_hi * 4 + z_lo), core: 2. Of those that a mesh axis runs over, the one named last changes fastest.
Arguments:
- features: bfloat16 [65536, 256], P(('col', 'row')), may hold values from -6 to 6
- grad_out: bfloat16 [65536, 256], P(('col', 'row')), may hold values from -6 to 6
- weight: bfloat16 [256, 256], replicated, may hold values from -4 to 4
- bias: float32 [256], replicated, may hold values from -3 to 3
- tile_rows: int32 [32, 16, 32], P('col', 'row'), may hold values from 0 to 15
- tile_cols: int32 [32, 16, 32], P('col', 'row'), may hold values from 0 to 31
- tile_weights: bfloat16 [32, 16, 32, 128, 128], P('col', 'row'), may hold values from 0 to 0.051, as said below
- tile_count: int32 [32, 16], P('col', 'row'), may hold values from 8 to 32, as said below
Outputs:
- node_out: bfloat16 [65536, 256], P(('col', 'row'))
- grad_features: bfloat16 [65536, 256], P(('col', 'row'))
- grad_weight: float32 [256, 256], replicated
- grad_bias: float32 [256], replicated
Inputs may be any that keep to these rules, and one draw needn't show every extreme that they name: `tile_rows`: tile slots may repeat a position; their entries add up. `tile_weights`: nonnegative edge weights; most entries are zero. `tile_count`: some device uses all 32 slots.
All inputs are finite; a program needn't handle non-finite values.
Results may differ from a plain program's by a relative error of at most 0.017.
Values may be sent and summed in bfloat16 or wider, within the bound.
No kernel may reach another device: no remote copies, remote signals or barrier semaphores. Data moves between devices by JAX's collectives and lax.ppermute only.
A program may use at most 64 MiB of HBM per device.

v0:
```python
import jax
import jax.numpy as jnp
from jax import lax
from jax.sharding import PartitionSpec as P

TILE = 128


def silu_slope(pre):
    sigmoid_val = jax.nn.sigmoid(pre)
    return sigmoid_val * (1.0 + pre * (1.0 - sigmoid_val))


def segment_rows(index_list, products, first_block, block_count):
    local = index_list - first_block
    inside = jnp.logical_and(local >= 0, local < block_count)
    target = jnp.where(inside, local, block_count)
    empty = jnp.zeros((block_count, products.shape[1], products.shape[2]), jnp.float32)
    summed = empty.at[target].add(products, mode="drop")
    return summed.reshape(block_count * products.shape[1], products.shape[2])


def shards(features, grad_out, weight, bias, tile_rows, tile_cols, tile_weights, tile_count):
    width = features.shape[1]
    node_rows = features.shape[0]
    slot_total = tile_rows.shape[2]
    row_tiles = lax.axis_size("row") * node_rows // TILE
    col_tiles = lax.axis_size("col") * node_rows // TILE
    all_nodes = node_rows * lax.axis_size("col") * lax.axis_size("row")
    row_index = tile_rows[0, 0]
    col_index = tile_cols[0, 0]
    slot_live = (jnp.arange(slot_total) < tile_count[0, 0]).astype(jnp.bfloat16)
    live_tiles = tile_weights[0, 0] * slot_live[:, None, None]
    gathered = lax.all_gather(features, "col", axis=0, tiled=True)
    blocks = gathered.reshape(col_tiles, TILE, width)[col_index]
    products = jnp.einsum("tij,tjf->tif", live_tiles, blocks, preferred_element_type=jnp.float32)
    row_mass = jnp.sum(live_tiles, axis=2, dtype=jnp.float32)
    hits = (row_index[None, :] == jnp.arange(row_tiles)[:, None]).astype(jnp.float32)
    mass_partial = jnp.einsum("rt,ti->ri", hits, row_mass, precision=lax.Precision.HIGHEST).reshape(
        -1
    )
    degree = 1.0 + lax.psum_scatter(mass_partial, "row", scatter_dimension=0, tiled=True)
    partial_sum = segment_rows(row_index, products, 0, row_tiles)
    neighbor = lax.psum_scatter(
        partial_sum.astype(jnp.bfloat16), "row", scatter_dimension=0, tiled=True
    ).astype(jnp.float32)
    aggregate = ((features.astype(jnp.float32) + neighbor) / degree[:, None]).astype(jnp.bfloat16)
    pre = jnp.dot(aggregate, weight, preferred_element_type=jnp.float32) + bias
    node_out = jax.nn.silu(pre).astype(jnp.bfloat16)
    grad_pre = (grad_out.astype(jnp.float32) * silu_slope(pre)).astype(jnp.bfloat16)
    weight_term = lax.dot_general(
        aggregate, grad_pre, (((0,), (0,)), ((), ())), preferred_element_type=jnp.float32
    )
    bias_term = jnp.sum(grad_pre, axis=0, dtype=jnp.float32)
    weight_sum, bias_sum = lax.psum((weight_term, bias_term), ("col", "row"))
    norm_scale = 1.0 / jnp.sqrt(jnp.float32(all_nodes))
    grad_weight = weight_sum * norm_scale
    grad_bias = bias_sum * norm_scale
    back_proj = lax.dot_general(
        grad_pre, weight, (((1,), (1,)), ((), ())), preferred_element_type=jnp.float32
    )
    spread = (back_proj / degree[:, None]).astype(jnp.bfloat16)
    owned = lax.all_gather(spread, "row", axis=0, tiled=True)
    spread_blocks = owned.reshape(row_tiles, TILE, width)[row_index]
    back_products = jnp.einsum(
        "tij,tif->tjf", live_tiles, spread_blocks, preferred_element_type=jnp.float32
    )
    back_term = segment_rows(col_index, back_products, 0, col_tiles)
    back_sum = lax.psum_scatter(
        back_term.astype(jnp.bfloat16), "col", scatter_dimension=0, tiled=True
    ).astype(jnp.float32)
    grad_features = (spread.astype(jnp.float32) + back_sum).astype(jnp.bfloat16)
    return (node_out, grad_features, grad_weight, grad_bias)


def solution(mesh):
    return jax.shard_map(
        shards,
        mesh=mesh,
        in_specs=(
            P(("col", "row"), None),
            P(("col", "row"), None),
            P(),
            P(),
            P("col", "row", None),
            P("col", "row", None),
            P("col", "row", None, None, None),
            P("col", "row"),
        ),
        out_specs=(P(("col", "row"), None), P(("col", "row"), None), P(), P()),
        check_vma=False,
    )
```

profile of v0, /device:TPU:1, one launch (start us, length us, event | category | flops | bytes accessed | tf_op | source)
XLA Modules:
  0.0 895.9 jit_solution(401037207562873109)
XLA Ops:
  7.2 0.0 copy-start
  7.2 0.0 all-gather.3.cloned.1.call-start
  7.2 0.7 all-gather.3.cloned.1.call-update
  7.9 0.0 reduce-scatter.3.cloned.1.call-start
  8.6 0.7 fusion.8
  9.3 0.7 fusion.9
  10.0 71.2 %all-gather.3.cloned.1.call-done = bf16[4096,256]{1,0:T(8,128)(2,1)} async-done(((bf16[128,256]{1,0:T(8,128)(2,1)}), bf16[4096,256]{1,0:T(8,128)(2,1)}) %all-gather.3.cloned.1.call-update) | async-done | bytes 2097168 | tf_op jit(solution)/shard_map/all_gather | solution.py:34
  81.2 0.0 copy-start.1
  81.2 2.4 gather_fusion
  83.6 0.0 copy-done.1
  83.6 2.7 fusion.2
  86.2 0.2 broadcast_in_dim.7
  86.5 6.5 scatter_fusion
  92.9 0.0 copy-start.4
  93.0 0.0 copy-start.3
  93.0 0.0 copy-start.5
  93.0 0.0 copy-start.7
  93.0 1.1 convert_element_type.58
  94.1 0.0 reduce-scatter.3.cloned.1.call-update
  94.1 0.0 all-gather.5.cloned.1.call-start
  94.2 1.3 dynamic-slice
  96.1 1.1 convert_reduce_fusion
  97.2 0.0 copy-done.4
  97.2 0.1 convolution_bitcast_fusion
  97.3 47.1 %all-reduce = f32[2048]{0:T(1024)S(1)} all-reduce(f32[2048]{0:T(1024)S(1)} %convolution_bitcast_fusion), channel_id=3, replica_groups=mesh['col'=32,'row'=16] {'row'}, use_global_device_ids=true, to_apply=%region_3.4.clone | all-reduce | flops 2048 | bytes 16384
  144.5 0.1 dynamic-slice_add_fusion
  144.6 61.6 %reduce-scatter.3.cloned.1.call-done = bf16[128,256]{1,0:T(8,128)(2,1)} async-done(((bf16[2048,256]{1,0:T(8,128)(2,1)}), bf16[128,256]{1,0:T(8,128)(2,1)}) %reduce-scatter.3.cloned.1.call-update) | async-done | bytes 65552 | tf_op jit(solution)/shard_map/reduce_scatter | solution.py:44
  206.2 0.0 copy-done
  206.2 0.0 copy-done.3
  206.2 0.0 copy-done.5
  206.2 0.0 copy-done.7
  206.2 0.0 copy-start.6
  206.2 1.8 convert_reduce_fusion.1
  208.0 0.8 fusion
  208.8 0.0 all-gather.5.cloned.1.call-update
  208.8 0.0 all-reduce.3.cloned.1.call-start
  208.9 0.0 copy-done.6
  208.9 1.0 fusion.10
  209.9 0.0 all-reduce.3.cloned.1.call-update
  209.9 0.0 reduce-scatter.5.cloned.1.call-start
  210.0 72.8 %all-gather.5.cloned.1.call-done = bf16[2048,256]{1,0:T(8,128)(2,1)} async-done(((bf16[128,256]{1,0:T(8,128)(2,1)}), bf16[2048,256]{1,0:T(8,128)(2,1)}) %all-gather.5.cloned.1.call-update) | async-done | bytes 1048592 | tf_op jit(solution)/shard_map/all_gather | solution.py:63
  282.8 1.9 gather_fusion.1
  284.7 3.1 fusion.1
  287.8 2.4 broadcast_in_dim.8
  290.2 9.8 %scatter_fusion.1 = f32[32,128,256]{2,1,0:T(8,128)} fusion(f32[32,128,256]{2,1,0:T(8,128)} %broadcast_in_dim.8, s32[32]{0:T(128)S(1)} %get-tuple-element.9, f32[32,128,256]{2,1,0:T(8,128)} %fusion.1), kind=kCustom, calls=%fused_computation.3 | custom fusion | flops 1048576 | bytes 12583040 | tf_op jit(solution)/shard_map/scatter-add | solution.py:19
  300.0 3.8 convert_element_type.68
  303.8 0.0 copy-start.2
  303.8 0.0 reduce-scatter.5.cloned.1.call-update
  303.9 102.1 %psum.15 = f32[256]{0:T(256)S(1)} all-reduce(f32[256]{0:T(256)S(1)} %get-tuple-element.4), channel_id=1, replica_groups=mesh['col'=32,'row'=16] {'col','row'}, use_global_device_ids=true, to_apply=%region_8.9 | all-reduce | flops 256 | bytes 2048 | tf_op jit(solution)/shard_map/psum | solution.py:55
  406.0 0.6 broadcast_multiply_fusion.1
  406.5 333.7 %all-reduce.3.cloned.1.call-done = f32[256,256]{1,0:T(8,128)} async-done(((f32[256,256]{1,0:T(8,128)}), f32[256,256]{1,0:T(8,128)}) %all-reduce.3.cloned.1.call-update) | async-done | bytes 262160 | tf_op jit(solution)/shard_map/psum | solution.py:55
  740.3 1.7 broadcast_multiply_fusion
  741.9 146.0 %reduce-scatter.5.cloned.1.call-done = bf16[128,256]{1,0:T(8,128)(2,1)} async-done(((bf16[4096,256]{1,0:T(8,128)(2,1)}), bf16[128,256]{1,0:T(8,128)(2,1)}) %reduce-scatter.5.cloned.1.call-update) | async-done | bytes 65552 | tf_op jit(solution)/shard_map/reduce_scatter | solution.py:69
  887.9 0.0 copy-done.2
  887.9 1.5 add_convert_fusion
  (3 shorter events, 0.0 us)
Async XLA Ops:
  7.2 199.0 %copy-start = (bf16[256,256]{1,0:T(8,128)(2,1)S(1)}, bf16[256,256]{1,0:T(8,128)(2,1)}, u32[]{:S(2)}) copy-start(bf16[256,256]{1,0:T(8,128)(2,1)} %param.10) | copy-start | bytes 393220
  7.2 74.0 %all-gather.3.cloned.1.call-start = ((), (), s32[]{:S(2)}) async-start(), calls=%async_computation.2 | async-start | bytes 2162688 | tf_op jit(solution)/shard_map/all_gather | solution.py:34
  7.9 198.2 %reduce-scatter.3.cloned.1.call-start = ((), (), s32[]{:S(2)}) async-start(), calls=%async_computation.3 | async-start | bytes 1114112 | tf_op jit(solution)/shard_map/reduce_scatter | solution.py:44
  81.2 2.4 copy-start.1
  92.9 4.3 copy-start.4
  93.0 113.2 %copy-start.3 = (bf16[128,256]{1,0:T(8,128)(2,1)S(1)}, bf16[128,256]{1,0:T(8,128)(2,1)}, u32[]{:S(2)}) copy-start(bf16[128,256]{1,0:T(8,128)(2,1)} %param.8) | copy-start | bytes 196612
  93.0 113.2 %copy-start.5 = (bf16[128,256]{1,0:T(8,128)(2,1)S(1)}, bf16[128,256]{1,0:T(8,128)(2,1)}, u32[]{:S(2)}) copy-start(bf16[128,256]{1,0:T(8,128)(2,1)} %param.9) | copy-start | bytes 196612
  93.0 113.2 %copy-start.7 = (f32[256]{0:T(256)S(1)}, f32[256]{0:T(256)}, u32[]{:S(2)}) copy-start(f32[256]{0:T(256)} %param.11) | copy-start | bytes 3076
  94.1 188.6 %all-gather.5.cloned.1.call-start = ((), (), s32[]{:S(2)}) async-start(), calls=%async_computation.4 | async-start | bytes 1114112 | tf_op jit(solution)/shard_map/all_gather | solution.py:63
  206.2 2.7 copy-start.6
  208.8 531.4 %all-reduce.3.cloned.1.call-start = ((), (), s32[]{:S(2)}) async-start(), calls=%async_computation.6 | async-start | bytes 524288 | tf_op jit(solution)/shard_map/psum | solution.py:55
  209.9 677.9 %reduce-scatter.5.cloned.1.call-start = ((), (), s32[]{:S(2)}) async-start(), calls=%async_computation.5 | async-start | bytes 2162688 | tf_op jit(solution)/shard_map/reduce_scatter | solution.py:69
  303.8 584.1 %copy-start.2 = (bf16[128,256]{1,0:T(8,128)(2,1)S(1)}, bf16[128,256]{1,0:T(8,128)(2,1)}, u32[]{:S(2)}) copy-start(bf16[128,256]{1,0:T(8,128)(2,1)} %fusion) | copy-start | bytes 196612
Sparse Core Ops, SparseCore 0:
  10.2 70.9 all-gather.2
  94.3 111.8 reduce-scatter.2
  210.2 72.5 all-gather.4
  289.5 450.6 all-reduce.2
  742.9 144.9 reduce-scatter.4
where the time goes:
time: 900 us; the launch traced here: 896 us
  waiting for transfers between devices  686 us (76%)
  blocking collectives  149 us (17%)
  other arithmetic  27.5 us (3%)
  between operations  15.2 us (2%)
  matrix products  9.52 us (1%)
    psum x1, waiting for transfers between devices, shards(): weight_sum, bias_sum = lax.psum((weight_term, bias_term), ('col', 'row'))  334 us
    reduce_scatter x1, waiting for transfers between devices, shards(): lax.psum_scatter(back_term.astype(jnp.bfloat16), 'col', scatter_dimension...  146 us
    psum x1, blocking collectives, shards(): weight_sum, bias_sum = lax.psum((weight_term, bias_term), ('col', 'row'))  102 us
    all_gather x1, waiting for transfers between devices, shards(): owned = lax.all_gather(spread, 'row', axis=0, tiled=True)  72.8 us
    all_gather x1, waiting for transfers between devices, shards(): gathered = lax.all_gather(features, 'col', axis=0, tiled=True)  71.2 us
    reduce_scatter x1, waiting for transfers between devices, shards(): lax.psum_scatter(partial_sum.astype(jnp.bfloat16), 'row', scatter_dimensi...  61.6 us
    unnamed x1, blocking collectives  47.1 us
  transfers between devices with their start and end apart: 5, of which 5 were waited for; matrix products, arithmetic and copies ran while one was open for 3% of the time, Pallas kernels for 0%

commit v1 on v0

v1 whole, which is shorter than its diff:
```python
import functools

import jax
import jax.numpy as jnp
from jax import lax
from jax.experimental import pallas as pl
from jax.experimental.pallas import tpu as pltpu
from jax.sharding import Mesh, PartitionSpec as P

AXES = ("x", "zl", "k", "zh", "y")
SIZES = (4, 4, 2, 4, 4)
COL, ROW = ("x", "zl", "k"), ("zh", "y")
TILE, H, EXTRA = 128, 256, 16
PIECE = H // 4
TAIL = PIECE + EXTRA
NORM = 1.0 / 256.0
BF, F32 = jnp.bfloat16, jnp.float32


def call(kernel, outs, in_smem, n_in, scratch=(), flops=1000000):
    vmem = pl.BlockSpec(memory_space=pltpu.VMEM)
    smem = pl.BlockSpec(memory_space=pltpu.SMEM)
    return pl.pallas_call(
        kernel,
        out_shape=outs,
        in_specs=[smem] * in_smem + [vmem] * n_in,
        out_specs=jax.tree.map(lambda _: vmem, outs),
        scratch_shapes=list(scratch),
        compiler_params=pltpu.CompilerParams(vmem_limit_bytes=40 * 1024 * 1024),
        cost_estimate=pl.CostEstimate(flops=flops, bytes_accessed=4000000, transcendentals=0),
    )


def split_rows(total):
    high = total.astype(BF).astype(F32)
    low = total - high
    row = lax.broadcasted_iota(jnp.int32, (EXTRA, H), 0)
    return jnp.where(row == 0, high, jnp.where(row == 1, low, 0.0)).astype(BF)


def sum_ref(ref, count, rows):
    total = ref[0, rows, :].astype(F32)
    for i in range(1, count):
        total += ref[i, rows, :].astype(F32)
    return total


def mass_rows(mass):
    high = mass.astype(BF)
    low = (mass - high.astype(F32)).astype(BF)
    return jnp.concatenate([high, low], axis=1)


def each_slot(count, step):
    def pair(i, carry):
        step(2 * i)
        step(2 * i + 1)
        return carry

    lax.fori_loop(0, count // 2, pair, 0)

    @pl.when(lax.rem(count, 2) == 1)
    def _():
        step(count - 1)


def forward_kernel(rows, cols, count, core, tiles, own, other, out, acc, mass):
    acc[...] = jnp.zeros_like(acc)
    mass[...] = jnp.zeros_like(mass)
    ones = jnp.ones((EXTRA, TILE), BF)

    def step(t):
        tile = tiles[t]
        c, r = cols[0, t], rows[0, t]
        block = jnp.where(lax.rem(c, 2) == core[0], own[c // 2], other[c // 2])
        acc[r] += jnp.dot(tile, block, preferred_element_type=F32)
        mass[r] += lax.dot_general(ones, tile, (((1,), (1,)), ((), ())), preferred_element_type=F32)

    each_slot(count[0, 0], step)
    for r in range(16):
        out[r % 4, r // 4, 0:TILE, :] = acc[r].astype(BF)
        out[r % 4, r // 4, TILE : TILE + EXTRA, :] = mass_rows(mass[r])


def sum_y_kernel(recv, out):
    for z in range(4):
        total = recv[0, z].astype(F32)
        for i in range(1, 4):
            total += recv[i, z].astype(F32)
        out[z, 0:TILE, :] = total[0:TILE].astype(BF)
        ends = total[TILE:]
        out[z, TILE : TILE + EXTRA, :] = mass_rows(ends[:, 0:TILE] + ends[:, TILE:])


def node_kernel(recv, features, grad_out, weight, bias, node_out, spread_out, send):
    total = recv[0].astype(F32) + recv[1].astype(F32) + recv[2].astype(F32) + recv[3].astype(F32)
    ends = total[TILE:]
    mass = 1.0 + ends[0:1, 0:TILE] + ends[0:1, TILE:]
    on_diagonal = lax.broadcasted_iota(jnp.int32, (TILE, TILE), 0) == lax.broadcasted_iota(
        jnp.int32, (TILE, TILE), 1
    )
    degree = jnp.sum(jnp.where(on_diagonal, mass, 0.0), axis=1, keepdims=True)
    aggregate = ((features[...].astype(F32) + total[0:TILE]) / degree).astype(BF)
    w = weight[...]
    pre = jnp.dot(aggregate, w, preferred_element_type=F32) + bias[...]
    sig = jax.nn.sigmoid(pre)
    node_out[...] = (pre * sig).astype(BF)
    grad_pre = (grad_out[...].astype(F32) * (sig * (1.0 + pre * (1.0 - sig)))).astype(BF)
    term = lax.dot_general(
        aggregate, grad_pre, (((0,), (0,)), ((), ())), preferred_element_type=F32
    ).astype(BF)
    bias_rows = split_rows(jnp.sum(grad_pre.astype(F32), axis=0, keepdims=True))
    back = lax.dot_general(grad_pre, w, (((1,), (1,)), ((), ())), preferred_element_type=F32)
    spread = (back / degree).astype(BF)
    spread_out[...] = spread
    for z in range(4):
        send[z, 0:TILE, :] = spread
        send[z, TILE : TILE + PIECE, :] = term[PIECE * z : PIECE * (z + 1)]
        send[z, TILE + PIECE :, :] = bias_rows


def tail_sum(total):
    ends = split_rows(total[PIECE : PIECE + 1] + total[PIECE + 1 : PIECE + 2])
    return jnp.concatenate([total[0:PIECE].astype(BF), ends], axis=0)


def sum_zh_kernel(recv, out):
    tail = tail_sum(sum_ref(recv, 4, slice(TILE, TILE + TAIL)))
    for y in range(4):
        for z in range(4):
            out[y, z * TILE : (z + 1) * TILE, :] = recv[z, 0:TILE, :]
        out[y, 4 * TILE :, :] = tail


def backward_kernel(rows, cols, count, core, tiles, spread, keep, send, acc):
    acc[...] = jnp.zeros_like(acc)

    def step(t):
        c, r = cols[0, t], rows[0, t]
        block = spread[lax.rem(r, 4), pl.ds(pl.multiple_of((r // 4) * TILE, TILE), TILE), :]
        acc[c] += lax.dot_general(
            tiles[t], block, (((0,), (0,)), ((), ())), preferred_element_type=F32
        )

    each_slot(count[0, 0], step)
    me = core[0]
    for i in range(16):
        keep[i * TILE : (i + 1) * TILE, :] = acc[2 * i + me].astype(BF)
        send[i * TILE : (i + 1) * TILE, :] = acc[2 * i + 1 - me].astype(BF)
    tail = tail_sum(sum_ref(spread, 4, slice(4 * TILE, 4 * TILE + TAIL)))
    keep[16 * TILE :, :] = tail
    send[16 * TILE :, :] = tail


def sum_k_kernel(keep, recv, out):
    def both(rows):
        return keep[rows, :].astype(F32) + recv[rows, :].astype(F32)

    tail = tail_sum(both(slice(16 * TILE, 16 * TILE + TAIL)))
    for x in range(4):
        out[x, 0 : 4 * TILE, :] = both(slice(4 * TILE * x, 4 * TILE * (x + 1))).astype(BF)
        out[x, 4 * TILE :, :] = tail


def sum_x_kernel(recv, out):
    tail = tail_sum(sum_ref(recv, 4, slice(4 * TILE, 4 * TILE + TAIL)))
    for z in range(4):
        out[z, 0:TILE, :] = sum_ref(recv, 4, slice(z * TILE, (z + 1) * TILE)).astype(BF)
        out[z, TILE:, :] = tail


def last_kernel(recv, spread, grad_features, piece, grad_bias):
    total = sum_ref(recv, 4, slice(0, TILE))
    grad_features[...] = (spread[...].astype(F32) + total).astype(BF)
    ends = sum_ref(recv, 4, slice(TILE, TILE + TAIL))
    part = ends[0:PIECE].astype(BF)
    for z in range(4):
        piece[z] = part
    grad_bias[...] = (ends[PIECE : PIECE + 1] + ends[PIECE + 1 : PIECE + 2]) * NORM


def exchange(value, axis):
    return lax.all_to_all(value, axis, 0, 0)


def copies(value):
    return jnp.broadcast_to(value[None], (4,) + value.shape)


def shards(features, grad_out, weight, bias, tile_rows, tile_cols, tile_weights, tile_count):
    shape = jax.ShapeDtypeStruct
    rows, cols = tile_rows[0], tile_cols[0]
    tiles = tile_weights[0, 0]
    core = lax.axis_index("k").astype(jnp.int32).reshape(1)
    swap = [(0, 1), (1, 0)]

    own = exchange(copies(features), "zl")
    own = exchange(copies(own), "x").reshape(16, TILE, H)
    other = lax.ppermute(own, "k", swap)
    part = call(
        forward_kernel,
        shape((4, 4, TILE + EXTRA, H), BF),
        4,
        3,
        (pltpu.VMEM((16, TILE, H), F32), pltpu.VMEM((16, EXTRA, TILE), F32)),
        600000000,
    )(rows, cols, tile_count, core, tiles, own, other)
    part = exchange(part, "y")
    part = call(sum_y_kernel, shape((4, TILE + EXTRA, H), BF), 0, 1)(part)
    part = exchange(part, "zh")
    node_out, spread, send = call(
        node_kernel,
        (shape((TILE, H), BF), shape((TILE, H), BF), shape((4, TILE + TAIL, H), BF)),
        0,
        5,
    )(part, features, grad_out, weight, bias.reshape(1, H))
    send = exchange(send, "zh")
    send = call(sum_zh_kernel, shape((4, 4 * TILE + TAIL, H), BF), 0, 1)(send)
    send = exchange(send, "y")
    flat = shape((16 * TILE + TAIL, H), BF)
    keep, away = call(
        backward_kernel, (flat, flat), 4, 2, (pltpu.VMEM((32, TILE, H), F32),), 600000000
    )(rows, cols, tile_count, core, tiles, send)
    back = lax.ppermute(away, "k", swap)
    back = call(sum_k_kernel, shape((4, 4 * TILE + TAIL, H), BF), 0, 2)(keep, back)
    back = exchange(back, "x")
    back = call(sum_x_kernel, shape((4, TILE + TAIL, H), BF), 0, 1)(back)
    back = exchange(back, "zl")
    grad_features, piece, grad_bias = call(
        last_kernel, (shape((TILE, H), BF), shape((4, PIECE, H), BF), shape((1, H), F32)), 0, 2
    )(back, spread)
    grad_weight = exchange(piece, "zh").reshape(H, H).astype(F32) * NORM
    return (node_out, grad_features, grad_weight, grad_bias.reshape(H))


def solution(mesh):
    grid = Mesh(mesh.devices.reshape(SIZES), AXES)
    nodes = P(COL + ROW, None)
    return jax.shard_map(
        shards,
        mesh=grid,
        in_specs=(
            nodes,
            nodes,
            P(),
            P(),
            P(COL, ROW, None),
            P(COL, ROW, None),
            P(COL, ROW, None, None, None),
            P(COL, ROW),
        ),
        out_specs=(nodes, nodes, P(), P()),
        check_vma=False,
    )
```

time: 900 us -> 207 us (0.23)
  waiting for transfers between devices: 686 us -> 3.94 us
  other arithmetic: 27.5 us -> 0.73 us
  blocking collectives: 149 us -> 175 us
  starting transfers between devices: 0.2 us -> 14.1 us
  between operations: 15.2 us -> 1.38 us
  Pallas kernels: 0 us -> 9.82 us
  matrix products: 9.52 us -> 0 us
    psum x1 -> x0, waiting for transfers between devices: 334 us -> none  [shards(): weight_sum, bias_sum = lax.psum((weight_term, bias_term), ('col', 'row'))]
    reduce_scatter x2 -> x0, waiting for transfers between devices: 208 us -> none  [the longest x1 146 us: shards(): lax.psum_scatter(back_term.astype(jnp.bfloat16), 'col', scatter_dimension...]
    all_to_all x0 -> x9, blocking collectives: none -> 175 us  [exchange(): return lax.all_to_all(value, axis, 0, 0)]
    all_gather x2 -> x0, waiting for transfers between devices: 144 us -> none  [the longest x1 72.8 us: shards(): owned = lax.all_gather(spread, 'row', axis=0, tiled=True)]
    psum x1 -> x0, blocking collectives: 102 us -> none  [shards(): weight_sum, bias_sum = lax.psum((weight_term, bias_term), ('col', 'row'))]
    unnamed x1 -> x0, blocking collectives: 47.1 us -> none
    scatter-add x2 -> x0, other arithmetic: 16.3 us -> none  [segment_rows(): summed = empty.at[target].add(products, mode='drop')]
    ppermute x0 -> x2, starting transfers between devices: none -> 14.1 us  [the longest x1 8.08 us: shards(): back = lax.ppermute(away, 'k', swap)]
  transfers between devices with their start and end apart: 5 -> 2, of which waited for: 5 -> 2; matrix products, arithmetic and copies ran while one was open for 3% -> 0% of each run, Pallas kernels for 0% -> 0%
where the time goes in v1:
time: 207 us; the launch traced here: 206 us
  blocking collectives  175 us (85%)
  starting transfers between devices  14.1 us (7%)
  Pallas kernels  9.82 us (5%)
  waiting for transfers between devices  3.94 us (2%)
    all_to_all x9, blocking collectives, exchange(): return lax.all_to_all(value, axis, 0, 0)  175 us
    ppermute x1, starting transfers between devices, shards(): back = lax.ppermute(away, 'k', swap)  8.08 us
    ppermute x1, starting transfers between devices, shards(): other = lax.ppermute(own, 'k', swap)  6.04 us
  transfers between devices with their start and end apart: 2, of which 2 were waited for; matrix products, arithmetic and copies ran while one was open for 0% of the time, Pallas kernels for 0%

profile of v1, /device:TPU:1, one launch (start us, length us, event | category | flops | bytes accessed | tf_op | source)
XLA Modules:
  0.0 205.7 jit_solution(2579692428256196227)
XLA Ops:
  0.6 0.9 broadcast_in_dim.4
  1.5 12.2 %all_to_all.45 = bf16[4,128,256]{2,1,0:T(8,128)(2,1)S(1)} all-to-all(bf16[4,128,256]{2,1,0:T(8,128)(2,1)S(1)} %broadcast_in_dim.4), channel_id=1, replica_groups=mesh['x'=4,'zl'=4,'k'=2,'zh'=4,'y'=4] {'zl'}, dimensions={0} | all-to-all | bytes 524288 | tf_op jit(solution)/shard_map/all_to_all | solution.py:183
  13.7 0.1 broadcast_in_dim.5
  13.8 0.0 copy-start
  13.8 0.0 copy-start.4
  13.8 0.0 copy-start.5
  13.9 16.8 %all_to_all.46 = bf16[4,4,128,256]{3,2,1,0:T(8,128)(2,1)S(1)} all-to-all(bf16[4,4,128,256]{3,2,1,0:T(8,128)(2,1)S(1)} %broadcast_in_dim.5), channel_id=1, replica_groups=mesh['x'=4,'zl'=4,'k'=2,'zh'=4,'y'=4] {'x'}, dimensions={0} | all-to-all | bytes 2097152 | tf_op jit(solution)/shard_map/all_to_all | solution.py:183
  30.6 6.0 %collective-permute-start = (bf16[16,128,256]{2,1,0:T(8,128)(2,1)S(1)}, bf16[16,128,256]{2,1,0:T(8,128)(2,1)S(1)}, u32[]{:S(2)}, u32[]{:S(2)}) collective-permute-start(bf16[16,128,256]{2,1,0:T(8,128)(2,1)S(1)} %bitcast.10), channel_id=1, source_target_pairs={{0,16},{16,0},{1,17},{17,1},{2,18},{18,2},{3,19},{19,3},{4,20},{20... | collective-permute-start | bytes 3145736 | tf_op jit(solution)/shard_map/ppermute | solution.py:199
  37.3 1.6 collective-permute-done.other
  38.9 0.0 copy-done
  38.9 0.0 copy-done.4
  38.9 0.0 copy-done.5
  38.9 3.6 %shard_map.111 = bf16[4,4,144,256]{3,2,1,0:T(8,128)(2,1)S(1)} custom-call(s32[1,32]{1,0:T(1,128)S(1)} %bitcast.12, s32[1,32]{1,0:T(1,128)S(1)} %bitcast.14, s32[1,1]{1,0:T(1,128)S(6)} %copy.12.count, s32[1]{0:T(128)} %bitcast.2.core, bf16[32,128,128]{2,1,0:T(8,128)(2,1)S(1)} %bitcast.8, bf16[16,128,256]{2,1,0:T(8,128)(2,1)S(1)} %bitcast.11, ...), custom_call_target="tpu_custom_call" | custom-call | flops 600000000 | bytes 4000000 | tf_op jit(solution)/shard_map/pallas_call | solution.py:200
  42.6 20.4 %all_to_all.47.recv = bf16[4,4,144,256]{3,2,1,0:T(8,128)(2,1)S(1)} all-to-all(bf16[4,4,144,256]{3,2,1,0:T(8,128)(2,1)S(1)} %shard_map.111), channel_id=1, replica_groups=mesh['x'=4,'zl'=4,'k'=2,'zh'=4,'y'=4] {'y'}, dimensions={0} | all-to-all | bytes 2359296 | tf_op jit(solution)/shard_map/all_to_all | solution.py:183
  62.9 0.0 copy-start.1
  62.9 0.0 copy-start.2
  62.9 0.0 copy-start.3
  62.9 0.0 copy-start.6
  62.9 0.2 shard_map.112
  63.1 29.3 %all_to_all.48.recv = bf16[4,144,256]{2,1,0:T(8,128)(2,1)S(1)} all-to-all(bf16[4,144,256]{2,1,0:T(8,128)(2,1)S(1)} %shard_map.112), channel_id=1, replica_groups=mesh['x'=4,'zl'=4,'k'=2,'zh'=4,'y'=4] {'zh'}, dimensions={0} | all-to-all | bytes 589824 | tf_op jit(solution)/shard_map/all_to_all | solution.py:183
  92.4 0.0 copy-done.1
  92.4 0.0 copy-done.2
  92.4 0.0 copy-done.3
  92.4 0.0 copy-done.6
  92.4 0.9 shard_map.113
  93.3 25.4 %all_to_all.49.recv = bf16[4,208,256]{2,1,0:T(8,128)(2,1)S(1)} all-to-all(bf16[4,208,256]{2,1,0:T(8,128)(2,1)S(1)} %get-tuple-element.13), channel_id=1, replica_groups=mesh['x'=4,'zl'=4,'k'=2,'zh'=4,'y'=4] {'zh'}, dimensions={0} | all-to-all | bytes 851968 | tf_op jit(solution)/shard_map/all_to_all | solution.py:183
  118.7 0.1 shard_map.114
  118.8 13.7 %all_to_all.50.spread = bf16[4,592,256]{2,1,0:T(8,128)(2,1)S(1)} all-to-all(bf16[4,592,256]{2,1,0:T(8,128)(2,1)S(1)} %shard_map.114), channel_id=1, replica_groups=mesh['x'=4,'zl'=4,'k'=2,'zh'=4,'y'=4] {'y'}, dimensions={0} | all-to-all | bytes 2424832 | tf_op jit(solution)/shard_map/all_to_all | solution.py:183
  132.5 3.9 %shard_map.115 = (bf16[2128,256]{1,0:T(8,128)(2,1)S(1)}, bf16[2128,256]{1,0:T(8,128)(2,1)S(1)}) custom-call(s32[1,32]{1,0:T(1,128)S(1)} %bitcast.13, s32[1,32]{1,0:T(1,128)S(1)} %bitcast.15, s32[1,1]{1,0:T(1,128)S(6)} %copy.12.count, s32[1]{0:T(128)} %bitcast.2.core, bf16[32,128,128]{2,1,0:T(8,128)(2,1)S(1)} %bitcast.9, ...), custom_call_target="tpu_custom_call" | custom-call | flops 600000000 | bytes 4000000 | tf_op jit(solution)/shard_map/pallas_call | solution.py:221
  136.5 8.1 %collective-permute-start.1 = (bf16[2128,256]{1,0:T(8,128)(2,1)S(1)}, bf16[2128,256]{1,0:T(8,128)(2,1)S(1)}, u32[]{:S(2)}, u32[]{:S(2)}) collective-permute-start(bf16[2128,256]{1,0:T(8,128)(2,1)S(1)} %get-tuple-element.15), channel_id=1, source_target_pairs={{0,16},{16,0},{1,17},{17,1},{2,18},{18,2},{3,19},{19,3},{4,20},{20... | collective-permute-start | bytes 3268616 | tf_op jit(solution)/shard_map/ppermute | solution.py:224
  144.6 2.3 %collective-permute-done.1.recv = bf16[2128,256]{1,0:T(8,128)(2,1)S(1)} collective-permute-done((bf16[2128,256]{1,0:T(8,128)(2,1)S(1)}, bf16[2128,256]{1,0:T(8,128)(2,1)S(1)}, u32[]{:S(2)}, u32[]{:S(2)}) %collective-permute-start.1) | collective-permute-done | bytes 1089568 | tf_op jit(solution)/shard_map/ppermute | solution.py:224
  146.9 0.3 shard_map.116
  147.2 18.9 %all_to_all.51.recv = bf16[4,592,256]{2,1,0:T(8,128)(2,1)S(1)} all-to-all(bf16[4,592,256]{2,1,0:T(8,128)(2,1)S(1)} %shard_map.116), channel_id=1, replica_groups=mesh['x'=4,'zl'=4,'k'=2,'zh'=4,'y'=4] {'x'}, dimensions={0} | all-to-all | bytes 2424832 | tf_op jit(solution)/shard_map/all_to_all | solution.py:183
  166.0 0.2 shard_map.117
  166.2 21.5 %all_to_all.52.recv = bf16[4,208,256]{2,1,0:T(8,128)(2,1)S(1)} all-to-all(bf16[4,208,256]{2,1,0:T(8,128)(2,1)S(1)} %shard_map.117), channel_id=1, replica_groups=mesh['x'=4,'zl'=4,'k'=2,'zh'=4,'y'=4] {'zl'}, dimensions={0} | all-to-all | bytes 851968 | tf_op jit(solution)/shard_map/all_to_all | solution.py:183
  187.7 0.7 shard_map.118
  188.4 16.6 %all_to_all.53 = bf16[4,64,256]{2,1,0:T(8,128)(2,1)S(1)} all-to-all(bf16[4,64,256]{2,1,0:T(8,128)(2,1)S(1)} %get-tuple-element.18), channel_id=1, replica_groups=mesh['x'=4,'zl'=4,'k'=2,'zh'=4,'y'=4] {'zh'}, dimensions={0} | all-to-all | bytes 262144 | tf_op jit(solution)/shard_map/all_to_all | solution.py:183
  205.0 0.7 convert_multiply_fusion
Async XLA Ops:
  13.8 25.1 %copy-start = (bf16[1,1,32,128,128]{4,3,2,1,0:T(8,128)(2,1)S(1)}, bf16[1,1,32,128,128]{4,3,2,1,0:T(8,128)(2,1)}, u32[]{:S(2)}) copy-start(bf16[1,1,32,128,128]{4,3,2,1,0:T(8,128)(2,1)} %param.14) | copy-start | bytes 3145732
  13.8 25.1 %copy-start.4 = (s32[1,1,32]{2,1,0:T(1,128)S(1)}, s32[1,1,32]{2,1,0:T(1,128)}, u32[]{:S(2)}) copy-start(s32[1,1,32]{2,1,0:T(1,128)} %param.12) | copy-start | bytes 388
  13.8 25.1 %copy-start.5 = (s32[1,1,32]{2,1,0:T(1,128)S(1)}, s32[1,1,32]{2,1,0:T(1,128)}, u32[]{:S(2)}) copy-start(s32[1,1,32]{2,1,0:T(1,128)} %param.13) | copy-start | bytes 388
  30.6 8.3 %collective-permute-start = (bf16[16,128,256]{2,1,0:T(8,128)(2,1)S(1)}, bf16[16,128,256]{2,1,0:T(8,128)(2,1)S(1)}, u32[]{:S(2)}, u32[]{:S(2)}) collective-permute-start(bf16[16,128,256]{2,1,0:T(8,128)(2,1)S(1)} %bitcast.10), channel_id=1, source_target_pairs={{0,16},{16,0},{1,17},{17,1},{2,18},{18,2},{3,19},{19,3},{4,20},{20... | collective-permute-start | bytes 3145736 | tf_op jit(solution)/shard_map/ppermute | solution.py:199
  62.9 29.5 %copy-start.1 = (bf16[128,256]{1,0:T(8,128)(2,1)S(1)}, bf16[128,256]{1,0:T(8,128)(2,1)}, u32[]{:S(2)}) copy-start(bf16[128,256]{1,0:T(8,128)(2,1)} %features.1) | copy-start | bytes 196612
  62.9 29.5 %copy-start.2 = (bf16[256,256]{1,0:T(8,128)(2,1)S(1)}, bf16[256,256]{1,0:T(8,128)(2,1)}, u32[]{:S(2)}) copy-start(bf16[256,256]{1,0:T(8,128)(2,1)} %weight.1) | copy-start | bytes 393220
  62.9 29.5 %copy-start.3 = (bf16[128,256]{1,0:T(8,128)(2,1)S(1)}, bf16[128,256]{1,0:T(8,128)(2,1)}, u32[]{:S(2)}) copy-start(bf16[128,256]{1,0:T(8,128)(2,1)} %grad_out.1) | copy-start | bytes 196612
  62.9 29.5 %copy-start.6 = (f32[256]{0:T(256)S(1)}, f32[256]{0:T(256)}, u32[]{:S(2)}) copy-start(f32[256]{0:T(256)} %param.11) | copy-start | bytes 3076
  136.5 10.4 %collective-permute-start.1 = (bf16[2128,256]{1,0:T(8,128)(2,1)S(1)}, bf16[2128,256]{1,0:T(8,128)(2,1)S(1)}, u32[]{:S(2)}, u32[]{:S(2)}) collective-permute-start(bf16[2128,256]{1,0:T(8,128)(2,1)S(1)} %get-tuple-element.15), channel_id=1, source_target_pairs={{0,16},{16,0},{1,17},{17,1},{2,18},{18,2},{3,19},{19,3},{4,20},{20... | collective-permute-start | bytes 3268616 | tf_op jit(solution)/shard_map/ppermute | solution.py:224

commit v2 on v1

--- a/solution.py
+++ b/solution.py
@@ -64,8 +64,18 @@
         step(count - 1)
 
 
-def forward_kernel(rows, cols, count, core, tiles, own, other, out, acc, mass):
-    acc[...] = jnp.zeros_like(acc)
+def add_block(acc, seen, i, product):
+    acc[i] = jnp.where(seen[i] == 1, acc[i], 0.0) + product
+    seen[i] = 1
+
+
+def clear(seen, count):
+    for i in range(count):
+        seen[i] = 0
+
+
+def forward_kernel(rows, cols, count, core, tiles, own, other, out, acc, mass, seen):
+    clear(seen, 16)
     mass[...] = jnp.zeros_like(mass)
     ones = jnp.ones((EXTRA, TILE), BF)
 
@@ -73,12 +83,12 @@
         tile = tiles[t]
         c, r = cols[0, t], rows[0, t]
         block = jnp.where(lax.rem(c, 2) == core[0], own[c // 2], other[c // 2])
-        acc[r] += jnp.dot(tile, block, preferred_element_type=F32)
+        add_block(acc, seen, r, jnp.dot(tile, block, preferred_element_type=F32))
         mass[r] += lax.dot_general(ones, tile, (((1,), (1,)), ((), ())), preferred_element_type=F32)
 
     each_slot(count[0, 0], step)
     for r in range(16):
-        out[r % 4, r // 4, 0:TILE, :] = acc[r].astype(BF)
+        out[r % 4, r // 4, 0:TILE, :] = jnp.where(seen[r] == 1, acc[r], 0.0).astype(BF)
         out[r % 4, r // 4, TILE : TILE + EXTRA, :] = mass_rows(mass[r])
 
 
@@ -92,31 +102,54 @@
         out[z, TILE : TILE + EXTRA, :] = mass_rows(ends[:, 0:TILE] + ends[:, TILE:])
 
 
+def column(lanes):
+    on_diagonal = lax.broadcasted_iota(jnp.int32, (TILE, TILE), 0) == lax.broadcasted_iota(
+        jnp.int32, (TILE, TILE), 1
+    )
+    return jnp.sum(jnp.where(on_diagonal, lanes, 0.0), axis=1, keepdims=True)
+
+
 def node_kernel(recv, features, grad_out, weight, bias, node_out, spread_out, send):
     total = recv[0].astype(F32) + recv[1].astype(F32) + recv[2].astype(F32) + recv[3].astype(F32)
     ends = total[TILE:]
-    mass = 1.0 + ends[0:1, 0:TILE] + ends[0:1, TILE:]
-    on_diagonal = lax.broadcasted_iota(jnp.int32, (TILE, TILE), 0) == lax.broadcasted_iota(
-        jnp.int32, (TILE, TILE), 1
-    )
-    degree = jnp.sum(jnp.where(on_diagonal, mass, 0.0), axis=1, keepdims=True)
+    degrees = 1.0 + ends[:, 0:TILE] + ends[:, TILE:]
+    degree = column(degrees[0:1])
     aggregate = ((features[...].astype(F32) + total[0:TILE]) / degree).astype(BF)
     w = weight[...]
     pre = jnp.dot(aggregate, w, preferred_element_type=F32) + bias[...]
     sig = jax.nn.sigmoid(pre)
     node_out[...] = (pre * sig).astype(BF)
     grad_pre = (grad_out[...].astype(F32) * (sig * (1.0 + pre * (1.0 - sig)))).astype(BF)
-    term = lax.dot_general(
-        aggregate, grad_pre, (((0,), (0,)), ((), ())), preferred_element_type=F32
-    ).astype(BF)
-    bias_rows = split_rows(jnp.sum(grad_pre.astype(F32), axis=0, keepdims=True))
     back = lax.dot_general(grad_pre, w, (((1,), (1,)), ((), ())), preferred_element_type=F32)
-    spread = (back / degree).astype(BF)
-    spread_out[...] = spread
+    spread_out[...] = (back / degree).astype(BF)
+    degree_rows = mass_rows(degrees)
     for z in range(4):
-        send[z, 0:TILE, :] = spread
-        send[z, TILE : TILE + PIECE, :] = term[PIECE * z : PIECE * (z + 1)]
-        send[z, TILE + PIECE :, :] = bias_rows
+        send[z, 0:TILE, :] = grad_pre
+        send[z, TILE : 2 * TILE, :] = aggregate
+        send[z, 2 * TILE :, :] = degree_rows
+
+
+def four_kernel(recv, weight, out):
+    w = weight[...]
+    term = jnp.zeros((H, H), F32)
+    bias_term = jnp.zeros((1, H), F32)
+    for z in range(4):
+        grad_pre = recv[z, 0:TILE, :]
+        aggregate = recv[z, TILE : 2 * TILE, :]
+        ends = recv[z, 2 * TILE :, :].astype(F32)
+        degree = column(ends[0:1, 0:TILE] + ends[0:1, TILE:])
+        back = lax.dot_general(grad_pre, w, (((1,), (1,)), ((), ())), preferred_element_type=F32)
+        spread = (back / degree).astype(BF)
+        for y in range(4):
+            out[y, z * TILE : (z + 1) * TILE, :] = spread
+        term += lax.dot_general(
+            aggregate, grad_pre, (((0,), (0,)), ((), ())), preferred_element_type=F32
+        )
+        bias_term += jnp.sum(grad_pre.astype(F32), axis=0, keepdims=True)
+    bias_rows = split_rows(bias_term)
+    for y in range(4):
+        out[y, 4 * TILE : 4 * TILE + PIECE, :] = term[PIECE * y : PIECE * (y + 1)].astype(BF)
+        out[y, 4 * TILE + PIECE :, :] = bias_rows
 
 
 def tail_sum(total):
@@ -124,42 +157,41 @@
     return jnp.concatenate([total[0:PIECE].astype(BF), ends], axis=0)
 
 
-def sum_zh_kernel(recv, out):
-    tail = tail_sum(sum_ref(recv, 4, slice(TILE, TILE + TAIL)))
-    for y in range(4):
-        for z in range(4):
-            out[y, z * TILE : (z + 1) * TILE, :] = recv[z, 0:TILE, :]
-        out[y, 4 * TILE :, :] = tail
-
-
-def backward_kernel(rows, cols, count, core, tiles, spread, keep, send, acc):
-    acc[...] = jnp.zeros_like(acc)
+def backward_kernel(rows, cols, count, core, tiles, spread, keep, send, acc, seen):
+    clear(seen, 32)
 
     def step(t):
         c, r = cols[0, t], rows[0, t]
         block = spread[lax.rem(r, 4), pl.ds(pl.multiple_of((r // 4) * TILE, TILE), TILE), :]
-        acc[c] += lax.dot_general(
+        product = lax.dot_general(
             tiles[t], block, (((0,), (0,)), ((), ())), preferred_element_type=F32
         )
+        add_block(acc, seen, c, product)
 
     each_slot(count[0, 0], step)
     me = core[0]
     for i in range(16):
-        keep[i * TILE : (i + 1) * TILE, :] = acc[2 * i + me].astype(BF)
-        send[i * TILE : (i + 1) * TILE, :] = acc[2 * i + 1 - me].astype(BF)
+        mine, others = 2 * i + me, 2 * i + 1 - me
+        here = slice(i * TILE, (i + 1) * TILE)
+        keep[here, :] = jnp.where(seen[mine] == 1, acc[mine], 0.0).astype(BF)
+        send[here, :] = jnp.where(seen[others] == 1, acc[others], 0.0).astype(BF)
     tail = tail_sum(sum_ref(spread, 4, slice(4 * TILE, 4 * TILE + TAIL)))
     keep[16 * TILE :, :] = tail
     send[16 * TILE :, :] = tail
 
 
-def sum_k_kernel(keep, recv, out):
+def sum_k_kernel(core, keep, recv, out):
     def both(rows):
         return keep[rows, :].astype(F32) + recv[rows, :].astype(F32)
 
     tail = tail_sum(both(slice(16 * TILE, 16 * TILE + TAIL)))
-    for x in range(4):
-        out[x, 0 : 4 * TILE, :] = both(slice(4 * TILE * x, 4 * TILE * (x + 1))).astype(BF)
-        out[x, 4 * TILE :, :] = tail
+    first = core[0] == 0
+    for d in range(4):
+        for e in range(4):
+            i = jnp.where(first, 4 * d + e, 4 * e + d)
+            rows = pl.ds(pl.multiple_of(i * TILE, TILE), TILE)
+            out[d, e * TILE : (e + 1) * TILE, :] = both(rows).astype(BF)
+        out[d, 4 * TILE :, :] = tail
 
 
 def sum_x_kernel(recv, out):
@@ -169,18 +201,31 @@
         out[z, TILE:, :] = tail
 
 
-def last_kernel(recv, spread, grad_features, piece, grad_bias):
+def last_kernel(recv, spread, grad_features):
     total = sum_ref(recv, 4, slice(0, TILE))
     grad_features[...] = (spread[...].astype(F32) + total).astype(BF)
+
+
+def piece_kernel(recv, piece, grad_bias):
     ends = sum_ref(recv, 4, slice(TILE, TILE + TAIL))
     part = ends[0:PIECE].astype(BF)
-    for z in range(4):
-        piece[z] = part
+    for y in range(4):
+        piece[y] = part
     grad_bias[...] = (ends[PIECE : PIECE + 1] + ends[PIECE + 1 : PIECE + 2]) * NORM
 
 
 def exchange(value, axis):
     return lax.all_to_all(value, axis, 0, 0)
+
+
+ALONG_X = [[[(x * 4 + z) * 2 + k for x in range(4)] for z in range(4)] for k in range(2)]
+ALONG_Z = [[[(x * 4 + z) * 2 + k for z in range(4)] for x in range(4)] for k in range(2)]
+FIRST = ALONG_X[0] + ALONG_Z[1]
+SECOND = ALONG_Z[0] + ALONG_X[1]
+
+
+def exchange_col(value, groups):
+    return lax.all_to_all(value, COL, 0, 0, axis_index_groups=groups)
 
 
 def copies(value):
@@ -202,7 +247,7 @@
         shape((4, 4, TILE + EXTRA, H), BF),
         4,
         3,
-        (pltpu.VMEM((16, TILE, H), F32), pltpu.VMEM((16, EXTRA, TILE), F32)),
+        (pltpu.VMEM((16, TILE, H), F32), pltpu.VMEM((16, EXTRA, TILE), F32), pltpu.SMEM((16,), jnp.int32)),
         600000000,
     )(rows, cols, tile_count, core, tiles, own, other)
     part = exchange(part, "y")
@@ -210,26 +255,29 @@
     part = exchange(part, "zh")
     node_out, spread, send = call(
         node_kernel,
-        (shape((TILE, H), BF), shape((TILE, H), BF), shape((4, TILE + TAIL, H), BF)),
+        (shape((TILE, H), BF), shape((TILE, H), BF), shape((4, 2 * TILE + EXTRA, H), BF)),
         0,
         5,
     )(part, features, grad_out, weight, bias.reshape(1, H))
     send = exchange(send, "zh")
-    send = call(sum_zh_kernel, shape((4, 4 * TILE + TAIL, H), BF), 0, 1)(send)
+    send = call(four_kernel, shape((4, 4 * TILE + TAIL, H), BF), 0, 2)(send, weight)
     send = exchange(send, "y")
     flat = shape((16 * TILE + TAIL, H), BF)
     keep, away = call(
-        backward_kernel, (flat, flat), 4, 2, (pltpu.VMEM((32, TILE, H), F32),), 600000000
+        backward_kernel, (flat, flat), 4, 2, (pltpu.VMEM((32, TILE, H), F32), pltpu.SMEM((32,), jnp.int32)), 600000000
     )(rows, cols, tile_count, core, tiles, send)
     back = lax.ppermute(away, "k", swap)
-    back = call(sum_k_kernel, shape((4, 4 * TILE + TAIL, H), BF), 0, 2)(keep, back)
-    back = exchange(back, "x")
+    back = call(sum_k_kernel, shape((4, 4 * TILE + TAIL, H), BF), 1, 2)(
+        core, keep, back
+    )
+    back = exchange_col(back, FIRST)
     back = call(sum_x_kernel, shape((4, TILE + TAIL, H), BF), 0, 1)(back)
-    back = exchange(back, "zl")
-    grad_features, piece, grad_bias = call(
-        last_kernel, (shape((TILE, H), BF), shape((4, PIECE, H), BF), shape((1, H), F32)), 0, 2
-    )(back, spread)
-    grad_weight = exchange(piece, "zh").reshape(H, H).astype(F32) * NORM
+    back = exchange_col(back, SECOND)
+    piece, grad_bias = call(
+        piece_kernel, (shape((4, PIECE, H), BF), shape((1, H), F32)), 0, 1
+    )(back)
+    grad_weight = exchange(piece, "y").reshape(H, H).astype(F32) * NORM
+    grad_features = call(last_kernel, shape((TILE, H), BF), 0, 2)(back, spread)
     return (node_out, grad_features, grad_weight, grad_bias.reshape(H))
 
 

time: 207 us -> 197 us (0.952)
  blocking collectives: 175 us -> 154 us
  starting transfers between devices: 14.1 us -> 22.8 us
  waiting for transfers between devices: 3.94 us -> 8.23 us
  Pallas kernels: 9.82 us -> 7.57 us
    all_to_all x9 -> x6, blocking collectives: 175 us -> 112 us  [exchange(): return lax.all_to_all(value, axis, 0, 0)]
    all_to_all x0 -> x2, blocking collectives: none -> 42.2 us  [exchange_col(): return lax.all_to_all(value, COL, 0, 0, axis_index_groups=groups)]
    ppermute x1, starting transfers between devices: 8.08 us -> 13.4 us  [shards(): back = lax.ppermute(away, 'k', swap)]
    all_to_all x0 -> x1, waiting for transfers between devices: none -> 4.3 us  [exchange(): return lax.all_to_all(value, axis, 0, 0)]
    all_to_all x0 -> x1, starting transfers between devices: none -> 3.33 us  [exchange(): return lax.all_to_all(value, axis, 0, 0)]
  transfers between devices with their start and end apart: 2 -> 3, of which waited for: 2 -> 3; matrix products, arithmetic and copies ran while one was open for 0% -> 0% of each run, Pallas kernels for 0% -> 0%
where the time goes in v2:
time: 197 us; the launch traced here: 196 us
  blocking collectives  154 us (78%)
  starting transfers between devices  22.8 us (12%)
  waiting for transfers between devices  8.23 us (4%)
  Pallas kernels  7.57 us (4%)
    all_to_all x6, blocking collectives, exchange(): return lax.all_to_all(value, axis, 0, 0)  112 us
    all_to_all x2, blocking collectives, exchange_col(): return lax.all_to_all(value, COL, 0, 0, axis_index_groups=groups)  42.2 us
    ppermute x1, starting transfers between devices, shards(): back = lax.ppermute(away, 'k', swap)  13.4 us
    ppermute x1, starting transfers between devices, shards(): other = lax.ppermute(own, 'k', swap)  6.04 us
    all_to_all x1, waiting for transfers between devices, exchange(): return lax.all_to_all(value, axis, 0, 0)  4.3 us
  transfers between devices with their start and end apart: 3, of which 3 were waited for; matrix products, arithmetic and copies ran while one was open for 0% of the time, Pallas kernels for 0%

profile of v2, /device:TPU:1, one launch (start us, length us, event | category | flops | bytes accessed | tf_op | source)
XLA Modules:
  0.0 195.9 jit_solution(3845256271717738782)
XLA Ops:
  0.6 0.9 broadcast_in_dim.4
  1.5 12.2 %all_to_all.45 = bf16[4,128,256]{2,1,0:T(8,128)(2,1)S(1)} all-to-all(bf16[4,128,256]{2,1,0:T(8,128)(2,1)S(1)} %broadcast_in_dim.4), channel_id=1, replica_groups=mesh['x'=4,'zl'=4,'k'=2,'zh'=4,'y'=4] {'zl'}, dimensions={0} | all-to-all | bytes 524288 | tf_op jit(solution)/shard_map/all_to_all | solution.py:218
  13.7 0.1 broadcast_in_dim.5
  13.8 0.0 copy-start
  13.8 0.0 copy-start.4
  13.8 0.0 copy-start.5
  13.9 16.8 %all_to_all.46 = bf16[4,4,128,256]{3,2,1,0:T(8,128)(2,1)S(1)} all-to-all(bf16[4,4,128,256]{3,2,1,0:T(8,128)(2,1)S(1)} %broadcast_in_dim.5), channel_id=1, replica_groups=mesh['x'=4,'zl'=4,'k'=2,'zh'=4,'y'=4] {'x'}, dimensions={0} | all-to-all | bytes 2097152 | tf_op jit(solution)/shard_map/all_to_all | solution.py:218
  30.6 6.0 %collective-permute-start = (bf16[16,128,256]{2,1,0:T(8,128)(2,1)S(1)}, bf16[16,128,256]{2,1,0:T(8,128)(2,1)S(1)}, u32[]{:S(2)}, u32[]{:S(2)}) collective-permute-start(bf16[16,128,256]{2,1,0:T(8,128)(2,1)S(1)} %bitcast.10), channel_id=1, source_target_pairs={{0,16},{16,0},{1,17},{17,1},{2,18},{18,2},{3,19},{19,3},{4,20},{20... | collective-permute-start | bytes 3145736 | tf_op jit(solution)/shard_map/ppermute | solution.py:244
  37.3 1.6 collective-permute-done.other
  38.9 0.0 copy-done
  38.9 0.0 copy-done.4
  38.9 0.0 copy-done.5
  38.9 2.0 %shard_map.111 = bf16[4,4,144,256]{3,2,1,0:T(8,128)(2,1)S(1)} custom-call(s32[1,32]{1,0:T(1,128)S(1)} %bitcast.12, s32[1,32]{1,0:T(1,128)S(1)} %bitcast.14, s32[1,1]{1,0:T(1,128)S(6)} %copy.12.count, s32[1]{0:T(128)} %bitcast.2.core, bf16[32,128,128]{2,1,0:T(8,128)(2,1)S(1)} %bitcast.8, bf16[16,128,256]{2,1,0:T(8,128)(2,1)S(1)} %bitcast.11, ...), custom_call_target="tpu_custom_call" | custom-call | flops 600000000 | bytes 4000000 | tf_op jit(solution)/shard_map/pallas_call | solution.py:245
  40.9 21.6 %all_to_all.47.recv = bf16[4,4,144,256]{3,2,1,0:T(8,128)(2,1)S(1)} all-to-all(bf16[4,4,144,256]{3,2,1,0:T(8,128)(2,1)S(1)} %shard_map.111), channel_id=1, replica_groups=mesh['x'=4,'zl'=4,'k'=2,'zh'=4,'y'=4] {'y'}, dimensions={0} | all-to-all | bytes 2359296 | tf_op jit(solution)/shard_map/all_to_all | solution.py:218
  62.5 0.0 copy-start.1
  62.5 0.0 copy-start.2
  62.5 0.0 copy-start.3
  62.5 0.0 copy-start.6
  62.5 0.2 shard_map.112
  62.6 24.8 %all_to_all.48.recv = bf16[4,144,256]{2,1,0:T(8,128)(2,1)S(1)} all-to-all(bf16[4,144,256]{2,1,0:T(8,128)(2,1)S(1)} %shard_map.112), channel_id=1, replica_groups=mesh['x'=4,'zl'=4,'k'=2,'zh'=4,'y'=4] {'zh'}, dimensions={0} | all-to-all | bytes 589824 | tf_op jit(solution)/shard_map/all_to_all | solution.py:218
  87.4 0.0 copy-done.1
  87.4 0.0 copy-done.2
  87.4 0.0 copy-done.3
  87.4 0.0 copy-done.6
  87.5 0.9 shard_map.113
  88.4 22.6 %all_to_all.49.recv = bf16[4,272,256]{2,1,0:T(8,128)(2,1)S(1)} all-to-all(bf16[4,272,256]{2,1,0:T(8,128)(2,1)S(1)} %get-tuple-element.12), channel_id=1, replica_groups=mesh['x'=4,'zl'=4,'k'=2,'zh'=4,'y'=4] {'zh'}, dimensions={0} | all-to-all | bytes 1114112 | tf_op jit(solution)/shard_map/all_to_all | solution.py:218
  110.9 0.5 shard_map.114
  111.4 14.1 %all_to_all.50.spread = bf16[4,592,256]{2,1,0:T(8,128)(2,1)S(1)} all-to-all(bf16[4,592,256]{2,1,0:T(8,128)(2,1)S(1)} %shard_map.114), channel_id=1, replica_groups=mesh['x'=4,'zl'=4,'k'=2,'zh'=4,'y'=4] {'y'}, dimensions={0} | all-to-all | bytes 2424832 | tf_op jit(solution)/shard_map/all_to_all | solution.py:218
  125.5 2.3 %shard_map.115 = (bf16[2128,256]{1,0:T(8,128)(2,1)S(1)}, bf16[2128,256]{1,0:T(8,128)(2,1)S(1)}) custom-call(s32[1,32]{1,0:T(1,128)S(1)} %bitcast.13, s32[1,32]{1,0:T(1,128)S(1)} %bitcast.15, s32[1,1]{1,0:T(1,128)S(6)} %copy.12.count, s32[1]{0:T(128)} %bitcast.2.core, bf16[32,128,128]{2,1,0:T(8,128)(2,1)S(1)} %bitcast.9, ...), custom_call_target="tpu_custom_call" | custom-call | flops 600000000 | bytes 4000000 | tf_op jit(solution)/shard_map/pallas_call | solution.py:266
  127.9 13.4 %collective-permute-start.1 = (bf16[2128,256]{1,0:T(8,128)(2,1)S(1)}, bf16[2128,256]{1,0:T(8,128)(2,1)S(1)}, u32[]{:S(2)}, u32[]{:S(2)}) collective-permute-start(bf16[2128,256]{1,0:T(8,128)(2,1)S(1)} %get-tuple-element.14), channel_id=1, source_target_pairs={{0,16},{16,0},{1,17},{17,1},{2,18},{18,2},{3,19},{19,3},{4,20},{20... | collective-permute-start | bytes 3268616 | tf_op jit(solution)/shard_map/ppermute | solution.py:269
  141.3 2.3 %collective-permute-done.1.recv = bf16[2128,256]{1,0:T(8,128)(2,1)S(1)} collective-permute-done((bf16[2128,256]{1,0:T(8,128)(2,1)S(1)}, bf16[2128,256]{1,0:T(8,128)(2,1)S(1)}, u32[]{:S(2)}, u32[]{:S(2)}) %collective-permute-start.1) | collective-permute-done | bytes 1089568 | tf_op jit(solution)/shard_map/ppermute | solution.py:269
  143.6 0.3 shard_map.116
  143.9 29.6 %all_to_all.51.recv = bf16[4,592,256]{2,1,0:T(8,128)(2,1)S(1)} all-to-all(bf16[4,592,256]{2,1,0:T(8,128)(2,1)S(1)} %shard_map.116), channel_id=1, replica_groups={{0,128,256,384},{32,160,288,416},{64,192,320,448},{96,224,352,480},{16,..., dimensions={0} | all-to-all | bytes 2424832 | tf_op jit(solution)/shard_map/all_to_all | solution.py:228
  173.5 0.2 shard_map.117
  173.6 12.6 %all_to_all.52.recv = bf16[4,208,256]{2,1,0:T(8,128)(2,1)S(1)} all-to-all(bf16[4,208,256]{2,1,0:T(8,128)(2,1)S(1)} %shard_map.117), channel_id=1, replica_groups={{0,32,64,96},{128,160,192,224},{256,288,320,352},{384,416,448,480},{16,..., dimensions={0} | all-to-all | bytes 851968 | tf_op jit(solution)/shard_map/all_to_all | solution.py:228
  186.2 0.7 shard_map.119
  186.9 3.3 %all-to-all-start.8 = ((bf16[4,64,256]{2,1,0:T(8,128)(2,1)}), bf16[4,64,256]{2,1,0:T(8,128)(2,1)S(1)}, u32[]{:S(2)}, u32[]{:S(2)}) async-start(bf16[4,64,256]{2,1,0:T(8,128)(2,1)} %get-tuple-element.16), calls=%async_computation.8 | async-start | bytes 262144 | tf_op jit(solution)/shard_map/all_to_all | solution.py:218
  190.2 0.7 shard_map.118
  190.9 4.3 %all-to-all-done.8 = bf16[4,64,256]{2,1,0:T(8,128)(2,1)S(1)} async-done(((bf16[4,64,256]{2,1,0:T(8,128)(2,1)}), bf16[4,64,256]{2,1,0:T(8,128)(2,1)S(1)}, u32[]{:S(2)}, u32[]{:S(2)}) %all-to-all-start.8) | async-done | bytes 131104 | tf_op jit(solution)/shard_map/all_to_all | solution.py:218
  195.2 0.7 convert_multiply_fusion
Async XLA Ops:
  13.8 25.1 %copy-start = (bf16[1,1,32,128,128]{4,3,2,1,0:T(8,128)(2,1)S(1)}, bf16[1,1,32,128,128]{4,3,2,1,0:T(8,128)(2,1)}, u32[]{:S(2)}) copy-start(bf16[1,1,32,128,128]{4,3,2,1,0:T(8,128)(2,1)} %param.14) | copy-start | bytes 3145732
  13.8 25.1 %copy-start.4 = (s32[1,1,32]{2,1,0:T(1,128)S(1)}, s32[1,1,32]{2,1,0:T(1,128)}, u32[]{:S(2)}) copy-start(s32[1,1,32]{2,1,0:T(1,128)} %param.12) | copy-start | bytes 388
  13.8 25.1 %copy-start.5 = (s32[1,1,32]{2,1,0:T(1,128)S(1)}, s32[1,1,32]{2,1,0:T(1,128)}, u32[]{:S(2)}) copy-start(s32[1,1,32]{2,1,0:T(1,128)} %param.13) | copy-start | bytes 388
  30.6 8.3 %collective-permute-start = (bf16[16,128,256]{2,1,0:T(8,128)(2,1)S(1)}, bf16[16,128,256]{2,1,0:T(8,128)(2,1)S(1)}, u32[]{:S(2)}, u32[]{:S(2)}) collective-permute-start(bf16[16,128,256]{2,1,0:T(8,128)(2,1)S(1)} %bitcast.10), channel_id=1, source_target_pairs={{0,16},{16,0},{1,17},{17,1},{2,18},{18,2},{3,19},{19,3},{4,20},{20... | collective-permute-start | bytes 3145736 | tf_op jit(solution)/shard_map/ppermute | solution.py:244
  62.5 25.0 %copy-start.1 = (bf16[256,256]{1,0:T(8,128)(2,1)S(1)}, bf16[256,256]{1,0:T(8,128)(2,1)}, u32[]{:S(2)}) copy-start(bf16[256,256]{1,0:T(8,128)(2,1)} %weight.3) | copy-start | bytes 393220
  62.5 25.0 %copy-start.2 = (bf16[128,256]{1,0:T(8,128)(2,1)S(1)}, bf16[128,256]{1,0:T(8,128)(2,1)}, u32[]{:S(2)}) copy-start(bf16[128,256]{1,0:T(8,128)(2,1)} %features.1) | copy-start | bytes 196612
  62.5 25.0 %copy-start.3 = (bf16[128,256]{1,0:T(8,128)(2,1)S(1)}, bf16[128,256]{1,0:T(8,128)(2,1)}, u32[]{:S(2)}) copy-start(bf16[128,256]{1,0:T(8,128)(2,1)} %grad_out.1) | copy-start | bytes 196612
  62.5 25.0 %copy-start.6 = (f32[256]{0:T(256)S(1)}, f32[256]{0:T(256)}, u32[]{:S(2)}) copy-start(f32[256]{0:T(256)} %param.11) | copy-start | bytes 3076
  127.9 15.7 %collective-permute-start.1 = (bf16[2128,256]{1,0:T(8,128)(2,1)S(1)}, bf16[2128,256]{1,0:T(8,128)(2,1)S(1)}, u32[]{:S(2)}, u32[]{:S(2)}) collective-permute-start(bf16[2128,256]{1,0:T(8,128)(2,1)S(1)} %get-tuple-element.14), channel_id=1, source_target_pairs={{0,16},{16,0},{1,17},{17,1},{2,18},{18,2},{3,19},{19,3},{4,20},{20... | collective-permute-start | bytes 3268616 | tf_op jit(solution)/shard_map/ppermute | solution.py:269
  186.9 8.3 %all-to-all-start.8 = ((bf16[4,64,256]{2,1,0:T(8,128)(2,1)}), bf16[4,64,256]{2,1,0:T(8,128)(2,1)S(1)}, u32[]{:S(2)}, u32[]{:S(2)}) async-start(bf16[4,64,256]{2,1,0:T(8,128)(2,1)} %get-tuple-element.16), calls=%async_computation.8 | async-start | bytes 262144 | tf_op jit(solution)/shard_map/all_to_all | solution.py:218

commit v3 on v2

--- a/solution.py
+++ b/solution.py
@@ -74,7 +74,9 @@
         seen[i] = 0
 
 
-def forward_kernel(rows, cols, count, core, tiles, own, other, out, acc, mass, seen):
+def forward_kernel(
+    rows, cols, count, core, zh, y, tiles, own, other, far, near1, near2, near3, mine, acc, mass, seen
+):
     clear(seen, 16)
     mass[...] = jnp.zeros_like(mass)
     ones = jnp.ones((EXTRA, TILE), BF)
@@ -87,16 +89,25 @@
         mass[r] += lax.dot_general(ones, tile, (((1,), (1,)), ((), ())), preferred_element_type=F32)
 
     each_slot(count[0, 0], step)
-    for r in range(16):
-        out[r % 4, r // 4, 0:TILE, :] = jnp.where(seen[r] == 1, acc[r], 0.0).astype(BF)
-        out[r % 4, r // 4, TILE : TILE + EXTRA, :] = mass_rows(mass[r])
-
-
-def sum_y_kernel(recv, out):
-    for z in range(4):
-        total = recv[0, z].astype(F32)
+
+    def put(out, r):
+        out[0:TILE, :] = jnp.where(seen[r] == 1, acc[r], 0.0).astype(BF)
+        out[TILE : TILE + EXTRA, :] = mass_rows(mass[r])
+
+    for d in (1, 2, 3):
+        for to in range(4):
+            put(far.at[to, d - 1], 4 * lax.rem(zh[0] + d, 4) + to)
+    for d, out in enumerate((mine, near1, near2, near3)):
+        put(out, 4 * zh[0] + lax.rem(y[0] + d, 4))
+
+
+def sum_y_kernel(zh, recv, out):
+    out[zh[0]] = jnp.zeros((TILE + EXTRA, H), BF)
+    for d in (1, 2, 3):
+        total = recv[0, d - 1].astype(F32)
         for i in range(1, 4):
-            total += recv[i, z].astype(F32)
+            total += recv[i, d - 1].astype(F32)
+        z = lax.rem(zh[0] + d, 4)
         out[z, 0:TILE, :] = total[0:TILE].astype(BF)
         ends = total[TILE:]
         out[z, TILE : TILE + EXTRA, :] = mass_rows(ends[:, 0:TILE] + ends[:, TILE:])
@@ -109,8 +120,12 @@
     return jnp.sum(jnp.where(on_diagonal, lanes, 0.0), axis=1, keepdims=True)
 
 
-def node_kernel(recv, features, grad_out, weight, bias, node_out, spread_out, send):
-    total = recv[0].astype(F32) + recv[1].astype(F32) + recv[2].astype(F32) + recv[3].astype(F32)
+def node_kernel(
+    recv, mine, near1, near2, near3, features, grad_out, weight, bias, node_out, spread_out, send
+):
+    total = mine[...].astype(F32) + recv[0].astype(F32)
+    for block in (recv[1], recv[2], recv[3], near1[...], near2[...], near3[...]):
+        total += block.astype(F32)
     ends = total[TILE:]
     degrees = 1.0 + ends[:, 0:TILE] + ends[:, TILE:]
     degree = column(degrees[0:1])
@@ -129,27 +144,33 @@
         send[z, 2 * TILE :, :] = degree_rows
 
 
-def four_kernel(recv, weight, out):
+def four_kernel(zh, recv, weight, out):
     w = weight[...]
+    for d in (1, 2, 3):
+        z = lax.rem(zh[0] + d, 4)
+        ends = recv[z, 2 * TILE :, :].astype(F32)
+        degree = column(ends[0:1, 0:TILE] + ends[0:1, TILE:])
+        back = lax.dot_general(
+            recv[z, 0:TILE, :], w, (((1,), (1,)), ((), ())), preferred_element_type=F32
+        )
+        spread = (back / degree).astype(BF)
+        for y in range(4):
+            out[y, (d - 1) * TILE : d * TILE, :] = spread
     term = jnp.zeros((H, H), F32)
     bias_term = jnp.zeros((1, H), F32)
     for z in range(4):
         grad_pre = recv[z, 0:TILE, :]
-        aggregate = recv[z, TILE : 2 * TILE, :]
-        ends = recv[z, 2 * TILE :, :].astype(F32)
-        degree = column(ends[0:1, 0:TILE] + ends[0:1, TILE:])
-        back = lax.dot_general(grad_pre, w, (((1,), (1,)), ((), ())), preferred_element_type=F32)
-        spread = (back / degree).astype(BF)
-        for y in range(4):
-            out[y, z * TILE : (z + 1) * TILE, :] = spread
         term += lax.dot_general(
-            aggregate, grad_pre, (((0,), (0,)), ((), ())), preferred_element_type=F32
+            recv[z, TILE : 2 * TILE, :],
+            grad_pre,
+            (((0,), (0,)), ((), ())),
+            preferred_element_type=F32,
         )
         bias_term += jnp.sum(grad_pre.astype(F32), axis=0, keepdims=True)
     bias_rows = split_rows(bias_term)
     for y in range(4):
-        out[y, 4 * TILE : 4 * TILE + PIECE, :] = term[PIECE * y : PIECE * (y + 1)].astype(BF)
-        out[y, 4 * TILE + PIECE :, :] = bias_rows
+        out[y, 3 * TILE : 3 * TILE + PIECE, :] = term[PIECE * y : PIECE * (y + 1)].astype(BF)
+        out[y, 3 * TILE + PIECE :, :] = bias_rows
 
 
 def tail_sum(total):
@@ -157,12 +178,19 @@
     return jnp.concatenate([total[0:PIECE].astype(BF), ends], axis=0)
 
 
-def backward_kernel(rows, cols, count, core, tiles, spread, keep, send, acc, seen):
+def backward_kernel(
+    rows, cols, count, core, zh, y, tiles, far, mine, near1, near2, near3, keep, send, near, acc, seen
+):
     clear(seen, 32)
+    for d, block in enumerate((mine, near1, near2, near3)):
+        near[lax.rem(y[0] + 4 - d, 4)] = block[...]
 
     def step(t):
         c, r = cols[0, t], rows[0, t]
-        block = spread[lax.rem(r, 4), pl.ds(pl.multiple_of((r // 4) * TILE, TILE), TILE), :]
+        d = lax.rem(r // 4 + 4 - zh[0], 4)
+        start = pl.multiple_of(jnp.maximum(d - 1, 0) * TILE, TILE)
+        at_y = lax.rem(r, 4)
+        block = jnp.where(d == 0, near[at_y], far[at_y, pl.ds(start, TILE), :])
         product = lax.dot_general(
             tiles[t], block, (((0,), (0,)), ((), ())), preferred_element_type=F32
         )
@@ -175,7 +203,7 @@
         here = slice(i * TILE, (i + 1) * TILE)
         keep[here, :] = jnp.where(seen[mine] == 1, acc[mine], 0.0).astype(BF)
         send[here, :] = jnp.where(seen[others] == 1, acc[others], 0.0).astype(BF)
-    tail = tail_sum(sum_ref(spread, 4, slice(4 * TILE, 4 * TILE + TAIL)))
+    tail = tail_sum(sum_ref(far, 4, slice(3 * TILE, 3 * TILE + TAIL)))
     keep[16 * TILE :, :] = tail
     send[16 * TILE :, :] = tail
 
@@ -228,6 +256,13 @@
     return lax.all_to_all(value, COL, 0, 0, axis_index_groups=groups)
 
 
+def along_y(*blocks):
+    return [
+        lax.ppermute(block, "y", [(i, (i + d) % 4) for i in range(4)])
+        for d, block in enumerate(blocks, 1)
+    ]
+
+
 def copies(value):
     return jnp.broadcast_to(value[None], (4,) + value.shape)
 
@@ -236,36 +271,52 @@
     shape = jax.ShapeDtypeStruct
     rows, cols = tile_rows[0], tile_cols[0]
     tiles = tile_weights[0, 0]
-    core = lax.axis_index("k").astype(jnp.int32).reshape(1)
+    core, zh, y = (lax.axis_index(a).astype(jnp.int32).reshape(1) for a in ("k", "zh", "y"))
     swap = [(0, 1), (1, 0)]
 
     own = exchange(copies(features), "zl")
     own = exchange(copies(own), "x").reshape(16, TILE, H)
     other = lax.ppermute(own, "k", swap)
-    part = call(
+    one_block = shape((TILE + EXTRA, H), BF)
+    part, near1, near2, near3, mine = call(
         forward_kernel,
-        shape((4, 4, TILE + EXTRA, H), BF),
-        4,
+        (shape((4, 3, TILE + EXTRA, H), BF),) + (one_block,) * 4,
+        6,
         3,
-        (pltpu.VMEM((16, TILE, H), F32), pltpu.VMEM((16, EXTRA, TILE), F32), pltpu.SMEM((16,), jnp.int32)),
+        (
+            pltpu.VMEM((16, TILE, H), F32),
+            pltpu.VMEM((16, EXTRA, TILE), F32),
+            pltpu.SMEM((16,), jnp.int32),
+        ),
         600000000,
-    )(rows, cols, tile_count, core, tiles, own, other)
+    )(rows, cols, tile_count, core, zh, y, tiles, own, other)
     part = exchange(part, "y")
-    part = call(sum_y_kernel, shape((4, TILE + EXTRA, H), BF), 0, 1)(part)
+    part = call(sum_y_kernel, shape((4, TILE + EXTRA, H), BF), 1, 1)(zh, part)
     part = exchange(part, "zh")
+    near = along_y(near1, near2, near3)
     node_out, spread, send = call(
         node_kernel,
         (shape((TILE, H), BF), shape((TILE, H), BF), shape((4, 2 * TILE + EXTRA, H), BF)),
         0,
-        5,
-    )(part, features, grad_out, weight, bias.reshape(1, H))
+        9,
+    )(part, mine, *near, features, grad_out, weight, bias.reshape(1, H))
     send = exchange(send, "zh")
-    send = call(four_kernel, shape((4, 4 * TILE + TAIL, H), BF), 0, 2)(send, weight)
+    send, *near = lax.optimization_barrier([send, *along_y(spread, spread, spread)])
+    send = call(four_kernel, shape((4, 3 * TILE + TAIL, H), BF), 1, 2)(zh, send, weight)
     send = exchange(send, "y")
     flat = shape((16 * TILE + TAIL, H), BF)
     keep, away = call(
-        backward_kernel, (flat, flat), 4, 2, (pltpu.VMEM((32, TILE, H), F32), pltpu.SMEM((32,), jnp.int32)), 600000000
-    )(rows, cols, tile_count, core, tiles, send)
+        backward_kernel,
+        (flat, flat),
+        6,
+        6,
+        (
+            pltpu.VMEM((4, TILE, H), BF),
+            pltpu.VMEM((32, TILE, H), F32),
+            pltpu.SMEM((32,), jnp.int32),
+        ),
+        600000000,
+    )(rows, cols, tile_count, core, zh, y, tiles, send, spread, *near)
     back = lax.ppermute(away, "k", swap)
     back = call(sum_k_kernel, shape((4, 4 * TILE + TAIL, H), BF), 1, 2)(
         core, keep, back

time: 197 us -> 194 us (0.985)
  blocking collectives: 154 us -> 89.6 us
  starting transfers between devices: 22.8 us -> 53.2 us
  waiting for transfers between devices: 8.23 us -> 38.2 us
    all_to_all x6 -> x4, blocking collectives: 112 us -> 58.9 us  [exchange(): return lax.all_to_all(value, axis, 0, 0)]
    all_to_all x1 -> x3, starting transfers between devices: 3.33 us -> 26.1 us  [exchange(): return lax.all_to_all(value, axis, 0, 0)]
    all_to_all x1 -> x3, waiting for transfers between devices: 4.3 us -> 26.2 us  [exchange(): return lax.all_to_all(value, axis, 0, 0)]
    ppermute x0 -> x6, starting transfers between devices: none -> 16.7 us  [along_y(): lax.ppermute(block, 'y', [(i, (i + d) % 4) for i in range(4)])]
    all_to_all x2, blocking collectives: 42.2 us -> 30.6 us  [exchange_col(): return lax.all_to_all(value, COL, 0, 0, axis_index_groups=groups)]
    ppermute x1, starting transfers between devices: 13.4 us -> 4.41 us  [shards(): back = lax.ppermute(away, 'k', swap)]
    ppermute x0 -> x6, waiting for transfers between devices: none -> 8.13 us  [along_y(): lax.ppermute(block, 'y', [(i, (i + d) % 4) for i in range(4)])]
  transfers between devices with their start and end apart: 3 -> 11, of which waited for: 3 -> 9; matrix products, arithmetic and copies ran while one was open for 0% -> 0% of each run, Pallas kernels for 0% -> 0%
where the time goes in v3:
time: 194 us; the launch traced here: 193 us
  blocking collectives  89.6 us (46%)
  starting transfers between devices  53.2 us (27%)
  waiting for transfers between devices  38.2 us (20%)
  Pallas kernels  8.58 us (4%)
    all_to_all x4, blocking collectives, exchange(): return lax.all_to_all(value, axis, 0, 0)  58.9 us
    all_to_all x2, blocking collectives, exchange_col(): return lax.all_to_all(value, COL, 0, 0, axis_index_groups=groups)  30.6 us
    all_to_all x3, waiting for transfers between devices, exchange(): return lax.all_to_all(value, axis, 0, 0)  26.2 us
    all_to_all x3, starting transfers between devices, exchange(): return lax.all_to_all(value, axis, 0, 0)  26.1 us
    ppermute x6, starting transfers between devices, along_y(): lax.ppermute(block, 'y', [(i, (i + d) % 4) for i in range(4)])  16.7 us
    ppermute x6, waiting for transfers between devices, along_y(): lax.ppermute(block, 'y', [(i, (i + d) % 4) for i in range(4)])  8.13 us
    ppermute x1, starting transfers between devices, shards(): other = lax.ppermute(own, 'k', swap)  6.04 us
    ppermute x1, starting transfers between devices, shards(): back = lax.ppermute(away, 'k', swap)  4.41 us
  transfers between devices with their start and end apart: 11, of which 9 were waited for; matrix products, arithmetic and copies ran while one was open for 0% of the time, Pallas kernels for 0%

profile of v3, /device:TPU:1, one launch (start us, length us, event | category | flops | bytes accessed | tf_op | source)
XLA Modules:
  0.0 192.7 jit_solution(13620792054173521803)
XLA Ops:
  0.6 0.9 broadcast_in_dim.4
  1.5 12.2 %all_to_all.45 = bf16[4,128,256]{2,1,0:T(8,128)(2,1)S(1)} all-to-all(bf16[4,128,256]{2,1,0:T(8,128)(2,1)S(1)} %broadcast_in_dim.4), channel_id=1, replica_groups=mesh['x'=4,'zl'=4,'k'=2,'zh'=4,'y'=4] {'zl'}, dimensions={0} | all-to-all | bytes 524288 | tf_op jit(solution)/shard_map/all_to_all | solution.py:246
  13.7 0.1 broadcast_in_dim.5
  13.8 0.0 copy-start
  13.8 0.0 copy-start.4
  13.8 0.0 copy-start.5
  13.9 16.8 %all_to_all.46 = bf16[4,4,128,256]{3,2,1,0:T(8,128)(2,1)S(1)} all-to-all(bf16[4,4,128,256]{3,2,1,0:T(8,128)(2,1)S(1)} %broadcast_in_dim.5), channel_id=1, replica_groups=mesh['x'=4,'zl'=4,'k'=2,'zh'=4,'y'=4] {'x'}, dimensions={0} | all-to-all | bytes 2097152 | tf_op jit(solution)/shard_map/all_to_all | solution.py:246
  30.6 6.0 %collective-permute-start = (bf16[16,128,256]{2,1,0:T(8,128)(2,1)S(1)}, bf16[16,128,256]{2,1,0:T(8,128)(2,1)S(1)}, u32[]{:S(2)}, u32[]{:S(2)}) collective-permute-start(bf16[16,128,256]{2,1,0:T(8,128)(2,1)S(1)} %bitcast.12), channel_id=1, source_target_pairs={{0,16},{16,0},{1,17},{17,1},{2,18},{18,2},{3,19},{19,3},{4,20},{20... | collective-permute-start | bytes 3145736 | tf_op jit(solution)/shard_map/ppermute | solution.py:279
  37.3 1.6 collective-permute-done.other
  38.9 0.0 copy-done
  38.9 0.0 copy-done.4
  38.9 0.0 copy-done.5
  38.9 2.1 %shard_map.111 = (bf16[4,3,144,256]{3,2,1,0:T(8,128)(2,1)S(1)}, bf16[144,256]{1,0:T(8,128)(2,1)S(1)}, bf16[144,256]{1,0:T(8,128)(2,1)S(1)}, bf16[144,256]{1,0:T(8,128)(2,1)S(1)}, bf16[144,256]{1,0:T(8,128)(2,1)S(1)}) custom-call(s32[1,32]{1,0:T(1,128)S(1)} %bitcast.14, s32[1,32]{1,0:T(1,128)S(1)} %bitcast.16, s32[1,1]{1,0:T(1,128)S(6)} %copy.12.count, ...), custom_call_target="tpu_custom_call" | custom-call | flops 600000000 | bytes 4000000 | tf_op jit(solution)/shard_map/pallas_call | solution.py:281
  41.0 15.2 %all_to_all.47.recv = bf16[4,3,144,256]{3,2,1,0:T(8,128)(2,1)S(1)} all-to-all(bf16[4,3,144,256]{3,2,1,0:T(8,128)(2,1)S(1)} %get-tuple-element.20), channel_id=1, replica_groups=mesh['x'=4,'zl'=4,'k'=2,'zh'=4,'y'=4] {'y'}, dimensions={0} | all-to-all | bytes 1769472 | tf_op jit(solution)/shard_map/all_to_all | solution.py:246
  56.2 0.0 copy-start.1
  56.2 0.0 copy-start.2
  56.2 0.0 copy-start.3
  56.2 0.0 copy-start.6
  56.2 0.8 shard_map.112
  57.0 16.2 %all-to-all-start.3 = ((bf16[4,144,256]{2,1,0:T(8,128)(2,1)}), bf16[4,144,256]{2,1,0:T(8,128)(2,1)S(1)}, u32[]{:S(2)}, u32[]{:S(2)}) async-start(bf16[4,144,256]{2,1,0:T(8,128)(2,1)} %shard_map.112), calls=%async_computation.3 | async-start | bytes 589824 | tf_op jit(solution)/shard_map/all_to_all | solution.py:246
  73.3 2.2 %collective-permute-start.1 = (bf16[144,256]{1,0:T(8,128)(2,1)S(1)}, bf16[144,256]{1,0:T(8,128)(2,1)S(1)}, u32[]{:S(2)}, u32[]{:S(2)}) collective-permute-start(bf16[144,256]{1,0:T(8,128)(2,1)S(1)} %get-tuple-element.22), channel_id=1, source_target_pairs={{0,1},{1,2},{2,3},{3,0},{4,5},{5,6},{6,7},{7,4},{8,9},{9,10},{10,1... | collective-permute-start | bytes 221192 | tf_op jit(solution)/shard_map/ppermute | solution.py:261
  75.5 3.7 %collective-permute-start.2 = (bf16[144,256]{1,0:T(8,128)(2,1)S(1)}, bf16[144,256]{1,0:T(8,128)(2,1)S(1)}, u32[]{:S(2)}, u32[]{:S(2)}) collective-permute-start(bf16[144,256]{1,0:T(8,128)(2,1)S(1)} %get-tuple-element.23), channel_id=1, source_target_pairs={{0,2},{1,3},{2,0},{3,1},{4,6},{5,7},{6,4},{7,5},{8,10},{9,11},{10,... | collective-permute-start | bytes 221192 | tf_op jit(solution)/shard_map/ppermute | solution.py:261
  79.2 2.5 %collective-permute-start.3 = (bf16[144,256]{1,0:T(8,128)(2,1)S(1)}, bf16[144,256]{1,0:T(8,128)(2,1)S(1)}, u32[]{:S(2)}, u32[]{:S(2)}) collective-permute-start(bf16[144,256]{1,0:T(8,128)(2,1)S(1)} %get-tuple-element.24), channel_id=1, source_target_pairs={{0,3},{1,0},{2,1},{3,2},{4,7},{5,4},{6,5},{7,6},{8,11},{9,8},{10,9... | collective-permute-start | bytes 221192 | tf_op jit(solution)/shard_map/ppermute | solution.py:261
  81.7 0.0 collective-permute-done.1.near1
  81.7 0.6 collective-permute-done.2.near2
  82.4 2.9 %collective-permute-done.3.near3 = bf16[144,256]{1,0:T(8,128)(2,1)S(1)} collective-permute-done((bf16[144,256]{1,0:T(8,128)(2,1)S(1)}, bf16[144,256]{1,0:T(8,128)(2,1)S(1)}, u32[]{:S(2)}, u32[]{:S(2)}) %collective-permute-start.3) | collective-permute-done | bytes 73760 | tf_op jit(solution)/shard_map/ppermute | solution.py:261
  85.3 4.6 %all-to-all-done.3.recv = bf16[4,144,256]{2,1,0:T(8,128)(2,1)S(1)} async-done(((bf16[4,144,256]{2,1,0:T(8,128)(2,1)}), bf16[4,144,256]{2,1,0:T(8,128)(2,1)S(1)}, u32[]{:S(2)}, u32[]{:S(2)}) %all-to-all-start.3) | async-done | bytes 294944 | tf_op jit(solution)/shard_map/all_to_all | solution.py:246
  89.8 0.0 copy-done.1
  89.8 0.0 copy-done.2
  89.8 0.0 copy-done.3
  89.8 0.0 copy-done.6
  89.8 1.1 shard_map.113
  90.9 6.5 %all-to-all-start.4 = ((bf16[4,272,256]{2,1,0:T(8,128)(2,1)}), bf16[4,272,256]{2,1,0:T(8,128)(2,1)S(1)}, u32[]{:S(2)}, u32[]{:S(2)}) async-start(bf16[4,272,256]{2,1,0:T(8,128)(2,1)} %get-tuple-element.26), calls=%async_computation.4 | async-start | bytes 1114112 | tf_op jit(solution)/shard_map/all_to_all | solution.py:246
  97.4 3.5 %collective-permute-start.6 = (bf16[128,256]{1,0:T(8,128)(2,1)S(1)}, bf16[128,256]{1,0:T(8,128)(2,1)S(1)}, u32[]{:S(2)}, u32[]{:S(2)}) collective-permute-start(bf16[128,256]{1,0:T(8,128)(2,1)S(1)} %get-tuple-element.27.mine.spread), channel_id=1, source_target_pairs={{0,3},{1,0},{2,1},{3,2},{4,7},{5,4},{6,5},{7,6},{8,11},{9,8},{10,9... | collective-permute-start | bytes 196616 | tf_op jit(solution)/shard_map/ppermute | solution.py:261
  100.9 2.9 %collective-permute-start.5 = (bf16[128,256]{1,0:T(8,128)(2,1)S(1)}, bf16[128,256]{1,0:T(8,128)(2,1)S(1)}, u32[]{:S(2)}, u32[]{:S(2)}) collective-permute-start(bf16[128,256]{1,0:T(8,128)(2,1)S(1)} %get-tuple-element.27.mine.spread), channel_id=1, source_target_pairs={{0,2},{1,3},{2,0},{3,1},{4,6},{5,7},{6,4},{7,5},{8,10},{9,11},{10,... | collective-permute-start | bytes 196616 | tf_op jit(solution)/shard_map/ppermute | solution.py:261
  103.8 1.9 collective-permute-start.4
  105.7 0.0 collective-permute-done.6.near3
  105.8 1.7 collective-permute-done.5.near2
  107.4 2.9 %collective-permute-done.4.near1 = bf16[128,256]{1,0:T(8,128)(2,1)S(1)} collective-permute-done((bf16[128,256]{1,0:T(8,128)(2,1)S(1)}, bf16[128,256]{1,0:T(8,128)(2,1)S(1)}, u32[]{:S(2)}, u32[]{:S(2)}) %collective-permute-start.4) | collective-permute-done | bytes 65568 | tf_op jit(solution)/shard_map/ppermute | solution.py:261
  110.3 17.5 %all-to-all-done.4.recv = bf16[4,272,256]{2,1,0:T(8,128)(2,1)S(1)} async-done(((bf16[4,272,256]{2,1,0:T(8,128)(2,1)}), bf16[4,272,256]{2,1,0:T(8,128)(2,1)S(1)}, u32[]{:S(2)}, u32[]{:S(2)}) %all-to-all-start.4) | async-done | bytes 557088 | tf_op jit(solution)/shard_map/all_to_all | solution.py:246
  127.8 0.5 shard_map.114
  128.3 14.8 %all_to_all.48.far = bf16[4,464,256]{2,1,0:T(8,128)(2,1)S(1)} all-to-all(bf16[4,464,256]{2,1,0:T(8,128)(2,1)S(1)} %shard_map.114), channel_id=1, replica_groups=mesh['x'=4,'zl'=4,'k'=2,'zh'=4,'y'=4] {'y'}, dimensions={0} | all-to-all | bytes 1900544 | tf_op jit(solution)/shard_map/all_to_all | solution.py:246
  143.1 2.4 %shard_map.115 = (bf16[2128,256]{1,0:T(8,128)(2,1)S(1)}, bf16[2128,256]{1,0:T(8,128)(2,1)S(1)}) custom-call(s32[1,32]{1,0:T(1,128)S(1)} %bitcast.15, s32[1,32]{1,0:T(1,128)S(1)} %bitcast.17, s32[1,1]{1,0:T(1,128)S(6)} %copy.12.count, s32[1]{0:T(128)} %bitcast.3.core, s32[1]{0:T(128)} %bitcast.zh, s32[1]{0:T(128)} %bitcast.4.y, ...), custom_call_target="tpu_custom_call" | custom-call | flops 600000000 | bytes 4000000 | tf_op jit(solution)/shard_map/pallas_call | solution.py:308
  145.5 4.4 %collective-permute-start.7 = (bf16[2128,256]{1,0:T(8,128)(2,1)S(1)}, bf16[2128,256]{1,0:T(8,128)(2,1)S(1)}, u32[]{:S(2)}, u32[]{:S(2)}) collective-permute-start(bf16[2128,256]{1,0:T(8,128)(2,1)S(1)} %get-tuple-element.33), channel_id=1, source_target_pairs={{0,16},{16,0},{1,17},{17,1},{2,18},{18,2},{3,19},{19,3},{4,20},{20... | collective-permute-start | bytes 3268616 | tf_op jit(solution)/shard_map/ppermute | solution.py:320
  149.9 2.3 %collective-permute-done.7.recv = bf16[2128,256]{1,0:T(8,128)(2,1)S(1)} collective-permute-done((bf16[2128,256]{1,0:T(8,128)(2,1)S(1)}, bf16[2128,256]{1,0:T(8,128)(2,1)S(1)}, u32[]{:S(2)}, u32[]{:S(2)}) %collective-permute-start.7) | collective-permute-done | bytes 1089568 | tf_op jit(solution)/shard_map/ppermute | solution.py:320
  152.2 0.3 shard_map.116
  152.5 21.8 %all_to_all.49.recv = bf16[4,592,256]{2,1,0:T(8,128)(2,1)S(1)} all-to-all(bf16[4,592,256]{2,1,0:T(8,128)(2,1)S(1)} %shard_map.116), channel_id=1, replica_groups={{0,128,256,384},{32,160,288,416},{64,192,320,448},{96,224,352,480},{16,..., dimensions={0} | all-to-all | bytes 2424832 | tf_op jit(solution)/shard_map/all_to_all | solution.py:256
  174.3 0.2 shard_map.117
  174.4 8.8 %all_to_all.50.recv = bf16[4,208,256]{2,1,0:T(8,128)(2,1)S(1)} all-to-all(bf16[4,208,256]{2,1,0:T(8,128)(2,1)S(1)} %shard_map.117), channel_id=1, replica_groups={{0,32,64,96},{128,160,192,224},{256,288,320,352},{384,416,448,480},{16,..., dimensions={0} | all-to-all | bytes 851968 | tf_op jit(solution)/shard_map/all_to_all | solution.py:256
  183.2 0.7 shard_map.119
  183.9 3.3 %all-to-all-start.8 = ((bf16[4,64,256]{2,1,0:T(8,128)(2,1)}), bf16[4,64,256]{2,1,0:T(8,128)(2,1)S(1)}, u32[]{:S(2)}, u32[]{:S(2)}) async-start(bf16[4,64,256]{2,1,0:T(8,128)(2,1)} %get-tuple-element.34), calls=%async_computation.8 | async-start | bytes 262144 | tf_op jit(solution)/shard_map/all_to_all | solution.py:246
  187.2 0.7 shard_map.118
  187.9 4.1 %all-to-all-done.8 = bf16[4,64,256]{2,1,0:T(8,128)(2,1)S(1)} async-done(((bf16[4,64,256]{2,1,0:T(8,128)(2,1)}), bf16[4,64,256]{2,1,0:T(8,128)(2,1)S(1)}, u32[]{:S(2)}, u32[]{:S(2)}) %all-to-all-start.8) | async-done | bytes 131104 | tf_op jit(solution)/shard_map/all_to_all | solution.py:246
  192.0 0.7 convert_multiply_fusion
Async XLA Ops:
  13.8 25.1 %copy-start = (bf16[1,1,32,128,128]{4,3,2,1,0:T(8,128)(2,1)S(1)}, bf16[1,1,32,128,128]{4,3,2,1,0:T(8,128)(2,1)}, u32[]{:S(2)}) copy-start(bf16[1,1,32,128,128]{4,3,2,1,0:T(8,128)(2,1)} %param.14) | copy-start | bytes 3145732
  13.8 25.1 %copy-start.4 = (s32[1,1,32]{2,1,0:T(1,128)S(1)}, s32[1,1,32]{2,1,0:T(1,128)}, u32[]{:S(2)}) copy-start(s32[1,1,32]{2,1,0:T(1,128)} %param.12) | copy-start | bytes 388
  13.8 25.1 %copy-start.5 = (s32[1,1,32]{2,1,0:T(1,128)S(1)}, s32[1,1,32]{2,1,0:T(1,128)}, u32[]{:S(2)}) copy-start(s32[1,1,32]{2,1,0:T(1,128)} %param.13) | copy-start | bytes 388
  30.6 8.3 %collective-permute-start = (bf16[16,128,256]{2,1,0:T(8,128)(2,1)S(1)}, bf16[16,128,256]{2,1,0:T(8,128)(2,1)S(1)}, u32[]{:S(2)}, u32[]{:S(2)}) collective-permute-start(bf16[16,128,256]{2,1,0:T(8,128)(2,1)S(1)} %bitcast.12), channel_id=1, source_target_pairs={{0,16},{16,0},{1,17},{17,1},{2,18},{18,2},{3,19},{19,3},{4,20},{20... | collective-permute-start | bytes 3145736 | tf_op jit(solution)/shard_map/ppermute | solution.py:279
  56.2 33.6 %copy-start.1 = (bf16[256,256]{1,0:T(8,128)(2,1)S(1)}, bf16[256,256]{1,0:T(8,128)(2,1)}, u32[]{:S(2)}) copy-start(bf16[256,256]{1,0:T(8,128)(2,1)} %weight.3) | copy-start | bytes 393220
  56.2 33.6 %copy-start.2 = (bf16[128,256]{1,0:T(8,128)(2,1)S(1)}, bf16[128,256]{1,0:T(8,128)(2,1)}, u32[]{:S(2)}) copy-start(bf16[128,256]{1,0:T(8,128)(2,1)} %features.1) | copy-start | bytes 196612
  56.2 33.6 %copy-start.3 = (bf16[128,256]{1,0:T(8,128)(2,1)S(1)}, bf16[128,256]{1,0:T(8,128)(2,1)}, u32[]{:S(2)}) copy-start(bf16[128,256]{1,0:T(8,128)(2,1)} %grad_out.1) | copy-start | bytes 196612
  56.2 33.6 %copy-start.6 = (f32[256]{0:T(256)S(1)}, f32[256]{0:T(256)}, u32[]{:S(2)}) copy-start(f32[256]{0:T(256)} %param.11) | copy-start | bytes 3076
  57.0 32.8 %all-to-all-start.3 = ((bf16[4,144,256]{2,1,0:T(8,128)(2,1)}), bf16[4,144,256]{2,1,0:T(8,128)(2,1)S(1)}, u32[]{:S(2)}, u32[]{:S(2)}) async-start(bf16[4,144,256]{2,1,0:T(8,128)(2,1)} %shard_map.112), calls=%async_computation.3 | async-start | bytes 589824 | tf_op jit(solution)/shard_map/all_to_all | solution.py:246
  73.3 8.4 %collective-permute-start.1 = (bf16[144,256]{1,0:T(8,128)(2,1)S(1)}, bf16[144,256]{1,0:T(8,128)(2,1)S(1)}, u32[]{:S(2)}, u32[]{:S(2)}) collective-permute-start(bf16[144,256]{1,0:T(8,128)(2,1)S(1)} %get-tuple-element.22), channel_id=1, source_target_pairs={{0,1},{1,2},{2,3},{3,0},{4,5},{5,6},{6,7},{7,4},{8,9},{9,10},{10,1... | collective-permute-start | bytes 221192 | tf_op jit(solution)/shard_map/ppermute | solution.py:261
  75.5 6.9 %collective-permute-start.2 = (bf16[144,256]{1,0:T(8,128)(2,1)S(1)}, bf16[144,256]{1,0:T(8,128)(2,1)S(1)}, u32[]{:S(2)}, u32[]{:S(2)}) collective-permute-start(bf16[144,256]{1,0:T(8,128)(2,1)S(1)} %get-tuple-element.23), channel_id=1, source_target_pairs={{0,2},{1,3},{2,0},{3,1},{4,6},{5,7},{6,4},{7,5},{8,10},{9,11},{10,... | collective-permute-start | bytes 221192 | tf_op jit(solution)/shard_map/ppermute | solution.py:261
  79.2 6.1 %collective-permute-start.3 = (bf16[144,256]{1,0:T(8,128)(2,1)S(1)}, bf16[144,256]{1,0:T(8,128)(2,1)S(1)}, u32[]{:S(2)}, u32[]{:S(2)}) collective-permute-start(bf16[144,256]{1,0:T(8,128)(2,1)S(1)} %get-tuple-element.24), channel_id=1, source_target_pairs={{0,3},{1,0},{2,1},{3,2},{4,7},{5,4},{6,5},{7,6},{8,11},{9,8},{10,9... | collective-permute-start | bytes 221192 | tf_op jit(solution)/shard_map/ppermute | solution.py:261
  90.9 36.9 %all-to-all-start.4 = ((bf16[4,272,256]{2,1,0:T(8,128)(2,1)}), bf16[4,272,256]{2,1,0:T(8,128)(2,1)S(1)}, u32[]{:S(2)}, u32[]{:S(2)}) async-start(bf16[4,272,256]{2,1,0:T(8,128)(2,1)} %get-tuple-element.26), calls=%async_computation.4 | async-start | bytes 1114112 | tf_op jit(solution)/shard_map/all_to_all | solution.py:246
  97.4 8.3 %collective-permute-start.6 = (bf16[128,256]{1,0:T(8,128)(2,1)S(1)}, bf16[128,256]{1,0:T(8,128)(2,1)S(1)}, u32[]{:S(2)}, u32[]{:S(2)}) collective-permute-start(bf16[128,256]{1,0:T(8,128)(2,1)S(1)} %get-tuple-element.27.mine.spread), channel_id=1, source_target_pairs={{0,3},{1,0},{2,1},{3,2},{4,7},{5,4},{6,5},{7,6},{8,11},{9,8},{10,9... | collective-permute-start | bytes 196616 | tf_op jit(solution)/shard_map/ppermute | solution.py:261
  100.9 6.5 %collective-permute-start.5 = (bf16[128,256]{1,0:T(8,128)(2,1)S(1)}, bf16[128,256]{1,0:T(8,128)(2,1)S(1)}, u32[]{:S(2)}, u32[]{:S(2)}) collective-permute-start(bf16[128,256]{1,0:T(8,128)(2,1)S(1)} %get-tuple-element.27.mine.spread), channel_id=1, source_target_pairs={{0,2},{1,3},{2,0},{3,1},{4,6},{5,7},{6,4},{7,5},{8,10},{9,11},{10,... | collective-permute-start | bytes 196616 | tf_op jit(solution)/shard_map/ppermute | solution.py:261
  103.8 6.5 %collective-permute-start.4 = (bf16[128,256]{1,0:T(8,128)(2,1)S(1)}, bf16[128,256]{1,0:T(8,128)(2,1)S(1)}, u32[]{:S(2)}, u32[]{:S(2)}) collective-permute-start(bf16[128,256]{1,0:T(8,128)(2,1)S(1)} %get-tuple-element.27.mine.spread), channel_id=1, source_target_pairs={{0,1},{1,2},{2,3},{3,0},{4,5},{5,6},{6,7},{7,4},{8,9},{9,10},{10,1... | collective-permute-start | bytes 196616 | tf_op jit(solution)/shard_map/ppermute | solution.py:261
  145.5 6.7 %collective-permute-start.7 = (bf16[2128,256]{1,0:T(8,128)(2,1)S(1)}, bf16[2128,256]{1,0:T(8,128)(2,1)S(1)}, u32[]{:S(2)}, u32[]{:S(2)}) collective-permute-start(bf16[2128,256]{1,0:T(8,128)(2,1)S(1)} %get-tuple-element.33), channel_id=1, source_target_pairs={{0,16},{16,0},{1,17},{17,1},{2,18},{18,2},{3,19},{19,3},{4,20},{20... | collective-permute-start | bytes 3268616 | tf_op jit(solution)/shard_map/ppermute | solution.py:320
  183.9 8.1 %all-to-all-start.8 = ((bf16[4,64,256]{2,1,0:T(8,128)(2,1)}), bf16[4,64,256]{2,1,0:T(8,128)(2,1)S(1)}, u32[]{:S(2)}, u32[]{:S(2)}) async-start(bf16[4,64,256]{2,1,0:T(8,128)(2,1)} %get-tuple-element.34), calls=%async_computation.8 | async-start | bytes 262144 | tf_op jit(solution)/shard_map/all_to_all | solution.py:246

commit v4 on v3

--- a/solution.py
+++ b/solution.py
@@ -64,34 +64,68 @@
         step(count - 1)
 
 
-def add_block(acc, seen, i, product):
-    acc[i] = jnp.where(seen[i] == 1, acc[i], 0.0) + product
-    seen[i] = 1
-
-
 def clear(seen, count):
     for i in range(count):
         seen[i] = 0
 
 
-def forward_kernel(
-    rows, cols, count, core, zh, y, tiles, own, other, far, near1, near2, near3, mine, acc, mass, seen
-):
+def slots_of(cols, count, parity, order):
+    def put(t, n):
+        order[n] = t
+        return n + jnp.where(lax.rem(cols[0, t], 2) == parity, 1, 0)
+
+    return lax.fori_loop(0, count, put, 0)
+
+
+def row_sums(ones, tile):
+    return lax.dot_general(ones, tile, (((1,), (1,)), ((), ())), preferred_element_type=F32)
+
+
+def own_kernel(rows, cols, count, core, tiles, own, begun, mass, seen, order):
     clear(seen, 16)
     mass[...] = jnp.zeros_like(mass)
     ones = jnp.ones((EXTRA, TILE), BF)
 
-    def step(t):
+    def step(i):
+        t = order[i]
+        r = rows[0, t]
         tile = tiles[t]
-        c, r = cols[0, t], rows[0, t]
-        block = jnp.where(lax.rem(c, 2) == core[0], own[c // 2], other[c // 2])
-        add_block(acc, seen, r, jnp.dot(tile, block, preferred_element_type=F32))
-        mass[r] += lax.dot_general(ones, tile, (((1,), (1,)), ((), ())), preferred_element_type=F32)
-
-    each_slot(count[0, 0], step)
+        product = jnp.dot(tile, own[cols[0, t] // 2], preferred_element_type=F32)
+        begun[r] = jnp.where(seen[r] == 1, begun[r], 0.0) + product
+        mass[r] += row_sums(ones, tile)
+        seen[r] = 1
+
+    each_slot(slots_of(cols, count[0, 0], core[0], order), step)
+
+
+def forward_kernel(
+    rows, cols, count, core, zh, y, tiles, other, begun, masses, far, near1, near2, near3, mine, acc, mass, seen, order
+):
+    clear(seen, 16)
+    mass[...] = masses[...]
+    ones = jnp.ones((EXTRA, TILE), BF)
+
+    def mark(i, carry):
+        seen[rows[0, order[i]]] = 1
+        return carry
+
+    lax.fori_loop(0, slots_of(cols, count[0, 0], core[0], order), mark, 0)
+
+    def so_far(r):
+        return jnp.where(seen[r] == 2, acc[r], jnp.where(seen[r] == 1, begun[r], 0.0))
+
+    def step(i):
+        t = order[i]
+        r = rows[0, t]
+        tile = tiles[t]
+        acc[r] = so_far(r) + jnp.dot(tile, other[cols[0, t] // 2], preferred_element_type=F32)
+        mass[r] += row_sums(ones, tile)
+        seen[r] = 2
+
+    each_slot(slots_of(cols, count[0, 0], 1 - core[0], order), step)
 
     def put(out, r):
-        out[0:TILE, :] = jnp.where(seen[r] == 1, acc[r], 0.0).astype(BF)
+        out[0:TILE, :] = so_far(r).astype(BF)
         out[TILE : TILE + EXTRA, :] = mass_rows(mass[r])
 
     for d in (1, 2, 3):
@@ -179,14 +213,16 @@
 
 
 def backward_kernel(
-    rows, cols, count, core, zh, y, tiles, far, mine, near1, near2, near3, keep, send, near, acc, seen
+    flip, rows, cols, count, core, zh, y, tiles, far, mine, near1, near2, near3, out, near, acc, seen, order
 ):
-    clear(seen, 32)
+    clear(seen, 16)
     for d, block in enumerate((mine, near1, near2, near3)):
         near[lax.rem(y[0] + 4 - d, 4)] = block[...]
-
-    def step(t):
-        c, r = cols[0, t], rows[0, t]
+    parity = 1 - core[0] if flip else core[0]
+
+    def step(i):
+        t = order[i]
+        c, r = cols[0, t] // 2, rows[0, t]
         d = lax.rem(r // 4 + 4 - zh[0], 4)
         start = pl.multiple_of(jnp.maximum(d - 1, 0) * TILE, TILE)
         at_y = lax.rem(r, 4)
@@ -194,18 +230,13 @@
         product = lax.dot_general(
             tiles[t], block, (((0,), (0,)), ((), ())), preferred_element_type=F32
         )
-        add_block(acc, seen, c, product)
-
-    each_slot(count[0, 0], step)
-    me = core[0]
+        acc[c] = jnp.where(seen[c] == 1, acc[c], 0.0) + product
+        seen[c] = 1
+
+    each_slot(slots_of(cols, count[0, 0], parity, order), step)
     for i in range(16):
-        mine, others = 2 * i + me, 2 * i + 1 - me
-        here = slice(i * TILE, (i + 1) * TILE)
-        keep[here, :] = jnp.where(seen[mine] == 1, acc[mine], 0.0).astype(BF)
-        send[here, :] = jnp.where(seen[others] == 1, acc[others], 0.0).astype(BF)
-    tail = tail_sum(sum_ref(far, 4, slice(3 * TILE, 3 * TILE + TAIL)))
-    keep[16 * TILE :, :] = tail
-    send[16 * TILE :, :] = tail
+        out[i * TILE : (i + 1) * TILE, :] = jnp.where(seen[i] == 1, acc[i], 0.0).astype(BF)
+    out[16 * TILE :, :] = tail_sum(sum_ref(far, 4, slice(3 * TILE, 3 * TILE + TAIL)))
 
 
 def sum_k_kernel(core, keep, recv, out):
@@ -229,12 +260,9 @@
         out[z, TILE:, :] = tail
 
 
-def last_kernel(recv, spread, grad_features):
+def last_kernel(recv, spread, grad_features, piece, grad_bias):
     total = sum_ref(recv, 4, slice(0, TILE))
     grad_features[...] = (spread[...].astype(F32) + total).astype(BF)
-
-
-def piece_kernel(recv, piece, grad_bias):
     ends = sum_ref(recv, 4, slice(TILE, TILE + TAIL))
     part = ends[0:PIECE].astype(BF)
     for y in range(4):
@@ -277,19 +305,25 @@
     own = exchange(copies(features), "zl")
     own = exchange(copies(own), "x").reshape(16, TILE, H)
     other = lax.ppermute(own, "k", swap)
+    flags = (pltpu.SMEM((16,), jnp.int32), pltpu.SMEM((32,), jnp.int32))
+    scratch = (pltpu.VMEM((16, TILE, H), F32),) + flags
+    begun, mass = call(
+        own_kernel,
+        (shape((16, TILE, H), F32), shape((16, EXTRA, TILE), F32)),
+        4,
+        2,
+        flags,
+        300000000,
+    )(rows, cols, tile_count, core, tiles, own)
     one_block = shape((TILE + EXTRA, H), BF)
     part, near1, near2, near3, mine = call(
         forward_kernel,
         (shape((4, 3, TILE + EXTRA, H), BF),) + (one_block,) * 4,
         6,
-        3,
-        (
-            pltpu.VMEM((16, TILE, H), F32),
-            pltpu.VMEM((16, EXTRA, TILE), F32),
-            pltpu.SMEM((16,), jnp.int32),
-        ),
-        600000000,
-    )(rows, cols, tile_count, core, zh, y, tiles, own, other)
+        4,
+        (pltpu.VMEM((16, TILE, H), F32), pltpu.VMEM((16, EXTRA, TILE), F32)) + flags,
+        300000000,
+    )(rows, cols, tile_count, core, zh, y, tiles, other, begun, mass)
     part = exchange(part, "y")
     part = call(sum_y_kernel, shape((4, TILE + EXTRA, H), BF), 1, 1)(zh, part)
     part = exchange(part, "zh")
@@ -305,30 +339,28 @@
     send = call(four_kernel, shape((4, 3 * TILE + TAIL, H), BF), 1, 2)(zh, send, weight)
     send = exchange(send, "y")
     flat = shape((16 * TILE + TAIL, H), BF)
-    keep, away = call(
-        backward_kernel,
-        (flat, flat),
-        6,
-        6,
-        (
-            pltpu.VMEM((4, TILE, H), BF),
-            pltpu.VMEM((32, TILE, H), F32),
-            pltpu.SMEM((32,), jnp.int32),
-        ),
-        600000000,
-    )(rows, cols, tile_count, core, zh, y, tiles, send, spread, *near)
-    back = lax.ppermute(away, "k", swap)
+    def terms(flip):
+        return call(
+            functools.partial(backward_kernel, flip),
+            flat,
+            6,
+            6,
+            (pltpu.VMEM((4, TILE, H), BF),) + scratch,
+            300000000,
+        )(rows, cols, tile_count, core, zh, y, tiles, send, spread, *near)
+
+    back = lax.ppermute(terms(1), "k", swap)
+    keep = terms(0)
     back = call(sum_k_kernel, shape((4, 4 * TILE + TAIL, H), BF), 1, 2)(
         core, keep, back
     )
     back = exchange_col(back, FIRST)
     back = call(sum_x_kernel, shape((4, TILE + TAIL, H), BF), 0, 1)(back)
     back = exchange_col(back, SECOND)
-    piece, grad_bias = call(
-        piece_kernel, (shape((4, PIECE, H), BF), shape((1, H), F32)), 0, 1
-    )(back)
+    grad_features, piece, grad_bias = call(
+        last_kernel, (shape((TILE, H), BF), shape((4, PIECE, H), BF), shape((1, H), F32)), 0, 2
+    )(back, spread)
     grad_weight = exchange(piece, "y").reshape(H, H).astype(F32) * NORM
-    grad_features = call(last_kernel, shape((TILE, H), BF), 0, 2)(back, spread)
     return (node_out, grad_features, grad_weight, grad_bias.reshape(H))
 
 

time: 194 us -> 191 us (0.985)
  starting transfers between devices: 53.2 us -> 42.9 us
  blocking collectives: 89.6 us -> 98.9 us
  waiting for transfers between devices: 38.2 us -> 32 us
  Pallas kernels: 8.58 us -> 13.4 us
    all_to_all x4 -> x5, blocking collectives: 58.9 us -> 69.7 us  [exchange(): return lax.all_to_all(value, axis, 0, 0)]
    all_to_all x3 -> x2, starting transfers between devices: 26.1 us -> 17 us  [exchange(): return lax.all_to_all(value, axis, 0, 0)]
    pallas_call x3 -> x4, Pallas kernels: 3.72 us -> 7.83 us  [the longest x2 4.84 us: terms(): call(functools.partial(backward_kernel, flip), flat, 6, 6, (pltpu.VMEM((4...]
    ppermute x1, waiting for transfers between devices: 2.32 us -> 0.01 us  [shards(): back = lax.ppermute(terms(1), 'k', swap)]
    all_to_all x3 -> x2, waiting for transfers between devices: 26.2 us -> 24 us  [exchange(): return lax.all_to_all(value, axis, 0, 0)]
  transfers between devices with their start and end apart: 11 -> 10, of which waited for: 9 -> 6; matrix products, arithmetic and copies ran while one was open for 0% -> 0% of each run, Pallas kernels for 0% -> 3%
where the time goes in v4:
time: 191 us; the launch traced here: 190 us
  blocking collectives  98.9 us (52%)
  starting transfers between devices  42.9 us (22%)
  waiting for transfers between devices  32 us (17%)
  Pallas kernels  13.4 us (7%)
    all_to_all x5, blocking collectives, exchange(): return lax.all_to_all(value, axis, 0, 0)  69.7 us
    all_to_all x2, blocking collectives, exchange_col(): return lax.all_to_all(value, COL, 0, 0, axis_index_groups=groups)  29.2 us
    all_to_all x2, waiting for transfers between devices, exchange(): return lax.all_to_all(value, axis, 0, 0)  24 us
    all_to_all x2, starting transfers between devices, exchange(): return lax.all_to_all(value, axis, 0, 0)  17 us
    ppermute x6, starting transfers between devices, along_y(): lax.ppermute(block, 'y', [(i, (i + d) % 4) for i in range(4)])  16.4 us
    ppermute x6, waiting for transfers between devices, along_y(): lax.ppermute(block, 'y', [(i, (i + d) % 4) for i in range(4)])  8.01 us
    ppermute x1, starting transfers between devices, shards(): other = lax.ppermute(own, 'k', swap)  6.04 us
    pallas_call x2, Pallas kernels, terms(): call(functools.partial(backward_kernel, flip), flat, 6, 6, (pltpu.VMEM((4...  4.84 us
  transfers between devices with their start and end apart: 10, of which 6 were waited for; matrix products, arithmetic and copies ran while one was open for 0% of the time, Pallas kernels for 3%

profile of v4, /device:TPU:1, one launch (start us, length us, event | category | flops | bytes accessed | tf_op | source)
XLA Modules:
  0.0 190.4 jit_solution(15620283169373376984)
XLA Ops:
  0.6 0.9 broadcast_in_dim.4
  1.5 12.2 %all_to_all.45 = bf16[4,128,256]{2,1,0:T(8,128)(2,1)S(1)} all-to-all(bf16[4,128,256]{2,1,0:T(8,128)(2,1)S(1)} %broadcast_in_dim.4), channel_id=1, replica_groups=mesh['x'=4,'zl'=4,'k'=2,'zh'=4,'y'=4] {'zl'}, dimensions={0} | all-to-all | bytes 524288 | tf_op jit(solution)/shard_map/all_to_all | solution.py:274
  13.7 0.1 broadcast_in_dim.5
  13.8 0.0 copy-start
  13.8 0.0 copy-start.4
  13.8 0.0 copy-start.5
  13.9 16.8 %all_to_all.46 = bf16[4,4,128,256]{3,2,1,0:T(8,128)(2,1)S(1)} all-to-all(bf16[4,4,128,256]{3,2,1,0:T(8,128)(2,1)S(1)} %broadcast_in_dim.5), channel_id=1, replica_groups=mesh['x'=4,'zl'=4,'k'=2,'zh'=4,'y'=4] {'x'}, dimensions={0} | all-to-all | bytes 2097152 | tf_op jit(solution)/shard_map/all_to_all | solution.py:274
  30.6 6.0 %collective-permute-start = (bf16[16,128,256]{2,1,0:T(8,128)(2,1)S(1)}, bf16[16,128,256]{2,1,0:T(8,128)(2,1)S(1)}, u32[]{:S(2)}, u32[]{:S(2)}) collective-permute-start(bf16[16,128,256]{2,1,0:T(8,128)(2,1)S(1)} %bitcast.14), channel_id=1, source_target_pairs={{0,16},{16,0},{1,17},{17,1},{2,18},{18,2},{3,19},{19,3},{4,20},{20... | collective-permute-start | bytes 3145736 | tf_op jit(solution)/shard_map/ppermute | solution.py:307
  37.3 0.0 copy-done
  37.3 0.0 copy-done.4
  37.3 0.0 copy-done.5
  37.3 2.3 %shard_map.111 = (f32[16,128,256]{2,1,0:T(8,128)S(1)}, f32[16,16,128]{2,1,0:T(8,128)S(1)}) custom-call(s32[1,32]{1,0:T(1,128)S(1)} %bitcast.16, s32[1,32]{1,0:T(1,128)S(1)} %bitcast.20, s32[1,1]{1,0:T(1,128)S(6)} %copy.12.count, s32[1]{0:T(128)} %bitcast.3.core, bf16[32,128,128]{2,1,0:T(8,128)(2,1)S(1)} %bitcast.10, bf16[16,128,256]{2,1,0:T(8,128)(2,1)S(1)} %bitcast.15), custom_call_target="tpu_custom_call" | custom-call | flops 300000000 | bytes 4000000 | tf_op jit(solution)/shard_map/pallas_call | solution.py:310
  39.7 0.0 collective-permute-done.other
  39.7 2.7 %shard_map.112 = (bf16[4,3,144,256]{3,2,1,0:T(8,128)(2,1)S(1)}, bf16[144,256]{1,0:T(8,128)(2,1)S(1)}, bf16[144,256]{1,0:T(8,128)(2,1)S(1)}, bf16[144,256]{1,0:T(8,128)(2,1)S(1)}, bf16[144,256]{1,0:T(8,128)(2,1)S(1)}) custom-call(s32[1,32]{1,0:T(1,128)S(1)} %bitcast.17, s32[1,32]{1,0:T(1,128)S(1)} %bitcast.21, s32[1,1]{1,0:T(1,128)S(6)} %copy.12.count, ...), custom_call_target="tpu_custom_call" | custom-call | flops 300000000 | bytes 4000000 | tf_op jit(solution)/shard_map/pallas_call | solution.py:319
  42.4 17.1 %all_to_all.47.recv = bf16[4,3,144,256]{3,2,1,0:T(8,128)(2,1)S(1)} all-to-all(bf16[4,3,144,256]{3,2,1,0:T(8,128)(2,1)S(1)} %get-tuple-element.23), channel_id=1, replica_groups=mesh['x'=4,'zl'=4,'k'=2,'zh'=4,'y'=4] {'y'}, dimensions={0} | all-to-all | bytes 1769472 | tf_op jit(solution)/shard_map/all_to_all | solution.py:274
  59.5 0.0 copy-start.1
  59.5 0.0 copy-start.2
  59.5 0.0 copy-start.3
  59.5 0.0 copy-start.6
  59.5 0.8 shard_map.113
  60.3 12.3 %all-to-all-start.3 = ((bf16[4,144,256]{2,1,0:T(8,128)(2,1)}), bf16[4,144,256]{2,1,0:T(8,128)(2,1)S(1)}, u32[]{:S(2)}, u32[]{:S(2)}) async-start(bf16[4,144,256]{2,1,0:T(8,128)(2,1)} %shard_map.113), calls=%async_computation.3 | async-start | bytes 589824 | tf_op jit(solution)/shard_map/all_to_all | solution.py:274
  72.6 2.2 %collective-permute-start.1 = (bf16[144,256]{1,0:T(8,128)(2,1)S(1)}, bf16[144,256]{1,0:T(8,128)(2,1)S(1)}, u32[]{:S(2)}, u32[]{:S(2)}) collective-permute-start(bf16[144,256]{1,0:T(8,128)(2,1)S(1)} %get-tuple-element.25), channel_id=1, source_target_pairs={{0,1},{1,2},{2,3},{3,0},{4,5},{5,6},{6,7},{7,4},{8,9},{9,10},{10,1... | collective-permute-start | bytes 221192 | tf_op jit(solution)/shard_map/ppermute | solution.py:289
  74.8 3.7 %collective-permute-start.2 = (bf16[144,256]{1,0:T(8,128)(2,1)S(1)}, bf16[144,256]{1,0:T(8,128)(2,1)S(1)}, u32[]{:S(2)}, u32[]{:S(2)}) collective-permute-start(bf16[144,256]{1,0:T(8,128)(2,1)S(1)} %get-tuple-element.26), channel_id=1, source_target_pairs={{0,2},{1,3},{2,0},{3,1},{4,6},{5,7},{6,4},{7,5},{8,10},{9,11},{10,... | collective-permute-start | bytes 221192 | tf_op jit(solution)/shard_map/ppermute | solution.py:289
  78.5 2.5 %collective-permute-start.3 = (bf16[144,256]{1,0:T(8,128)(2,1)S(1)}, bf16[144,256]{1,0:T(8,128)(2,1)S(1)}, u32[]{:S(2)}, u32[]{:S(2)}) collective-permute-start(bf16[144,256]{1,0:T(8,128)(2,1)S(1)} %get-tuple-element.27), channel_id=1, source_target_pairs={{0,3},{1,0},{2,1},{3,2},{4,7},{5,4},{6,5},{7,6},{8,11},{9,8},{10,9... | collective-permute-start | bytes 221192 | tf_op jit(solution)/shard_map/ppermute | solution.py:289
  81.1 0.0 collective-permute-done.1.near1
  81.1 0.8 collective-permute-done.2.near2
  81.9 2.0 %collective-permute-done.3.near3 = bf16[144,256]{1,0:T(8,128)(2,1)S(1)} collective-permute-done((bf16[144,256]{1,0:T(8,128)(2,1)S(1)}, bf16[144,256]{1,0:T(8,128)(2,1)S(1)}, u32[]{:S(2)}, u32[]{:S(2)}) %collective-permute-start.3) | collective-permute-done | bytes 73760 | tf_op jit(solution)/shard_map/ppermute | solution.py:289
  83.9 7.2 %all-to-all-done.3.recv = bf16[4,144,256]{2,1,0:T(8,128)(2,1)S(1)} async-done(((bf16[4,144,256]{2,1,0:T(8,128)(2,1)}), bf16[4,144,256]{2,1,0:T(8,128)(2,1)S(1)}, u32[]{:S(2)}, u32[]{:S(2)}) %all-to-all-start.3) | async-done | bytes 294944 | tf_op jit(solution)/shard_map/all_to_all | solution.py:274
  91.1 0.0 copy-done.1
  91.1 0.0 copy-done.2
  91.1 0.0 copy-done.3
  91.1 0.0 copy-done.6
  91.1 1.1 shard_map.114
  92.2 4.7 %all-to-all-start.4 = ((bf16[4,272,256]{2,1,0:T(8,128)(2,1)}), bf16[4,272,256]{2,1,0:T(8,128)(2,1)S(1)}, u32[]{:S(2)}, u32[]{:S(2)}) async-start(bf16[4,272,256]{2,1,0:T(8,128)(2,1)} %get-tuple-element.29), calls=%async_computation.4 | async-start | bytes 1114112 | tf_op jit(solution)/shard_map/all_to_all | solution.py:274
  96.9 3.1 %collective-permute-start.6 = (bf16[128,256]{1,0:T(8,128)(2,1)S(1)}, bf16[128,256]{1,0:T(8,128)(2,1)S(1)}, u32[]{:S(2)}, u32[]{:S(2)}) collective-permute-start(bf16[128,256]{1,0:T(8,128)(2,1)S(1)} %get-tuple-element.30.mine.spread), channel_id=1, source_target_pairs={{0,3},{1,0},{2,1},{3,2},{4,7},{5,4},{6,5},{7,6},{8,11},{9,8},{10,9... | collective-permute-start | bytes 196616 | tf_op jit(solution)/shard_map/ppermute | solution.py:289
  100.0 3.0 %collective-permute-start.5 = (bf16[128,256]{1,0:T(8,128)(2,1)S(1)}, bf16[128,256]{1,0:T(8,128)(2,1)S(1)}, u32[]{:S(2)}, u32[]{:S(2)}) collective-permute-start(bf16[128,256]{1,0:T(8,128)(2,1)S(1)} %get-tuple-element.30.mine.spread), channel_id=1, source_target_pairs={{0,2},{1,3},{2,0},{3,1},{4,6},{5,7},{6,4},{7,5},{8,10},{9,11},{10,... | collective-permute-start | bytes 196616 | tf_op jit(solution)/shard_map/ppermute | solution.py:289
  103.0 1.9 %collective-permute-start.4 = (bf16[128,256]{1,0:T(8,128)(2,1)S(1)}, bf16[128,256]{1,0:T(8,128)(2,1)S(1)}, u32[]{:S(2)}, u32[]{:S(2)}) collective-permute-start(bf16[128,256]{1,0:T(8,128)(2,1)S(1)} %get-tuple-element.30.mine.spread), channel_id=1, source_target_pairs={{0,1},{1,2},{2,3},{3,0},{4,5},{5,6},{6,7},{7,4},{8,9},{9,10},{10,1... | collective-permute-start | bytes 196616 | tf_op jit(solution)/shard_map/ppermute | solution.py:289
  105.0 0.0 collective-permute-done.6.near3
  105.0 1.9 collective-permute-done.5.near2
  106.8 3.3 %collective-permute-done.4.near1 = bf16[128,256]{1,0:T(8,128)(2,1)S(1)} collective-permute-done((bf16[128,256]{1,0:T(8,128)(2,1)S(1)}, bf16[128,256]{1,0:T(8,128)(2,1)S(1)}, u32[]{:S(2)}, u32[]{:S(2)}) %collective-permute-start.4) | collective-permute-done | bytes 65568 | tf_op jit(solution)/shard_map/ppermute | solution.py:289
  110.1 16.9 %all-to-all-done.4.recv = bf16[4,272,256]{2,1,0:T(8,128)(2,1)S(1)} async-done(((bf16[4,272,256]{2,1,0:T(8,128)(2,1)}), bf16[4,272,256]{2,1,0:T(8,128)(2,1)S(1)}, u32[]{:S(2)}, u32[]{:S(2)}) %all-to-all-start.4) | async-done | bytes 557088 | tf_op jit(solution)/shard_map/all_to_all | solution.py:274
  127.0 0.5 shard_map.115
  127.4 15.7 %all_to_all.48.far = bf16[4,464,256]{2,1,0:T(8,128)(2,1)S(1)} all-to-all(bf16[4,464,256]{2,1,0:T(8,128)(2,1)S(1)} %shard_map.115), channel_id=1, replica_groups=mesh['x'=4,'zl'=4,'k'=2,'zh'=4,'y'=4] {'y'}, dimensions={0} | all-to-all | bytes 1900544 | tf_op jit(solution)/shard_map/all_to_all | solution.py:274
  143.2 2.3 %shard_map.117 = bf16[2128,256]{1,0:T(8,128)(2,1)S(1)} custom-call(s32[1,32]{1,0:T(1,128)S(1)} %bitcast.18, s32[1,32]{1,0:T(1,128)S(1)} %bitcast.22, s32[1,1]{1,0:T(1,128)S(6)} %copy.12.count, s32[1]{0:T(128)} %bitcast.3.core, s32[1]{0:T(128)} %bitcast.zh, s32[1]{0:T(128)} %bitcast.4.y, bf16[32,128,128]{2,1,0:T(8,128)(2,1)S(1)} %bitcast.12, ...), custom_call_target="tpu_custom_call" | custom-call | flops 300000000 | bytes 4000000 | tf_op jit(solution)/shard_map/pallas_call | solution.py:343
  145.5 3.5 %collective-permute-start.7 = (bf16[2128,256]{1,0:T(8,128)(2,1)S(1)}, bf16[2128,256]{1,0:T(8,128)(2,1)S(1)}, u32[]{:S(2)}, u32[]{:S(2)}) collective-permute-start(bf16[2128,256]{1,0:T(8,128)(2,1)S(1)} %shard_map.117), channel_id=1, source_target_pairs={{0,16},{16,0},{1,17},{17,1},{2,18},{18,2},{3,19},{19,3},{4,20},{20... | collective-permute-start | bytes 3268616 | tf_op jit(solution)/shard_map/ppermute | solution.py:352
  148.9 2.5 %shard_map.116.keep = bf16[2128,256]{1,0:T(8,128)(2,1)S(1)} custom-call(s32[1,32]{1,0:T(1,128)S(1)} %bitcast.19, s32[1,32]{1,0:T(1,128)S(1)} %bitcast.23, s32[1,1]{1,0:T(1,128)S(6)} %copy.12.count, s32[1]{0:T(128)} %bitcast.3.core, s32[1]{0:T(128)} %bitcast.zh, s32[1]{0:T(128)} %bitcast.4.y, bf16[32,128,128]{2,1,0:T(8,128)(2,1)S(1)} %bitcast.13, ...), custom_call_target="tpu_custom_call" | custom-call | flops 300000000 | bytes 4000000 | tf_op jit(solution)/shard_map/pallas_call | solution.py:343
  151.5 0.0 collective-permute-done.7.recv
  151.5 0.3 shard_map.118
  151.8 19.5 %all_to_all.49.recv = bf16[4,592,256]{2,1,0:T(8,128)(2,1)S(1)} all-to-all(bf16[4,592,256]{2,1,0:T(8,128)(2,1)S(1)} %shard_map.118), channel_id=1, replica_groups={{0,128,256,384},{32,160,288,416},{64,192,320,448},{96,224,352,480},{16,..., dimensions={0} | all-to-all | bytes 2424832 | tf_op jit(solution)/shard_map/all_to_all | solution.py:284
  171.2 0.2 shard_map.119
  171.4 9.8 %all_to_all.50.recv = bf16[4,208,256]{2,1,0:T(8,128)(2,1)S(1)} all-to-all(bf16[4,208,256]{2,1,0:T(8,128)(2,1)S(1)} %shard_map.119), channel_id=1, replica_groups={{0,32,64,96},{128,160,192,224},{256,288,320,352},{384,416,448,480},{16,..., dimensions={0} | all-to-all | bytes 851968 | tf_op jit(solution)/shard_map/all_to_all | solution.py:284
  181.1 0.7 shard_map.120
  181.8 7.9 %all_to_all.51 = bf16[4,64,256]{2,1,0:T(8,128)(2,1)S(1)} all-to-all(bf16[4,64,256]{2,1,0:T(8,128)(2,1)S(1)} %get-tuple-element.36), channel_id=1, replica_groups=mesh['x'=4,'zl'=4,'k'=2,'zh'=4,'y'=4] {'y'}, dimensions={0} | all-to-all | bytes 262144 | tf_op jit(solution)/shard_map/all_to_all | solution.py:274
  189.7 0.7 convert_multiply_fusion
Async XLA Ops:
  13.8 23.5 %copy-start = (bf16[1,1,32,128,128]{4,3,2,1,0:T(8,128)(2,1)S(1)}, bf16[1,1,32,128,128]{4,3,2,1,0:T(8,128)(2,1)}, u32[]{:S(2)}) copy-start(bf16[1,1,32,128,128]{4,3,2,1,0:T(8,128)(2,1)} %param.14) | copy-start | bytes 3145732
  13.8 23.5 %copy-start.4 = (s32[1,1,32]{2,1,0:T(1,128)S(1)}, s32[1,1,32]{2,1,0:T(1,128)}, u32[]{:S(2)}) copy-start(s32[1,1,32]{2,1,0:T(1,128)} %param.12) | copy-start | bytes 388
  13.8 23.5 %copy-start.5 = (s32[1,1,32]{2,1,0:T(1,128)S(1)}, s32[1,1,32]{2,1,0:T(1,128)}, u32[]{:S(2)}) copy-start(s32[1,1,32]{2,1,0:T(1,128)} %param.13) | copy-start | bytes 388
  30.6 9.1 %collective-permute-start = (bf16[16,128,256]{2,1,0:T(8,128)(2,1)S(1)}, bf16[16,128,256]{2,1,0:T(8,128)(2,1)S(1)}, u32[]{:S(2)}, u32[]{:S(2)}) collective-permute-start(bf16[16,128,256]{2,1,0:T(8,128)(2,1)S(1)} %bitcast.14), channel_id=1, source_target_pairs={{0,16},{16,0},{1,17},{17,1},{2,18},{18,2},{3,19},{19,3},{4,20},{20... | collective-permute-start | bytes 3145736 | tf_op jit(solution)/shard_map/ppermute | solution.py:307
  59.5 31.6 %copy-start.1 = (bf16[256,256]{1,0:T(8,128)(2,1)S(1)}, bf16[256,256]{1,0:T(8,128)(2,1)}, u32[]{:S(2)}) copy-start(bf16[256,256]{1,0:T(8,128)(2,1)} %weight.3) | copy-start | bytes 393220
  59.5 31.6 %copy-start.2 = (bf16[128,256]{1,0:T(8,128)(2,1)S(1)}, bf16[128,256]{1,0:T(8,128)(2,1)}, u32[]{:S(2)}) copy-start(bf16[128,256]{1,0:T(8,128)(2,1)} %features.1) | copy-start | bytes 196612
  59.5 31.6 %copy-start.3 = (bf16[128,256]{1,0:T(8,128)(2,1)S(1)}, bf16[128,256]{1,0:T(8,128)(2,1)}, u32[]{:S(2)}) copy-start(bf16[128,256]{1,0:T(8,128)(2,1)} %grad_out.1) | copy-start | bytes 196612
  59.5 31.6 %copy-start.6 = (f32[256]{0:T(256)S(1)}, f32[256]{0:T(256)}, u32[]{:S(2)}) copy-start(f32[256]{0:T(256)} %param.11) | copy-start | bytes 3076
  60.3 30.8 %all-to-all-start.3 = ((bf16[4,144,256]{2,1,0:T(8,128)(2,1)}), bf16[4,144,256]{2,1,0:T(8,128)(2,1)S(1)}, u32[]{:S(2)}, u32[]{:S(2)}) async-start(bf16[4,144,256]{2,1,0:T(8,128)(2,1)} %shard_map.113), calls=%async_computation.3 | async-start | bytes 589824 | tf_op jit(solution)/shard_map/all_to_all | solution.py:274
  72.6 8.4 %collective-permute-start.1 = (bf16[144,256]{1,0:T(8,128)(2,1)S(1)}, bf16[144,256]{1,0:T(8,128)(2,1)S(1)}, u32[]{:S(2)}, u32[]{:S(2)}) collective-permute-start(bf16[144,256]{1,0:T(8,128)(2,1)S(1)} %get-tuple-element.25), channel_id=1, source_target_pairs={{0,1},{1,2},{2,3},{3,0},{4,5},{5,6},{6,7},{7,4},{8,9},{9,10},{10,1... | collective-permute-start | bytes 221192 | tf_op jit(solution)/shard_map/ppermute | solution.py:289
  74.8 7.1 %collective-permute-start.2 = (bf16[144,256]{1,0:T(8,128)(2,1)S(1)}, bf16[144,256]{1,0:T(8,128)(2,1)S(1)}, u32[]{:S(2)}, u32[]{:S(2)}) collective-permute-start(bf16[144,256]{1,0:T(8,128)(2,1)S(1)} %get-tuple-element.26), channel_id=1, source_target_pairs={{0,2},{1,3},{2,0},{3,1},{4,6},{5,7},{6,4},{7,5},{8,10},{9,11},{10,... | collective-permute-start | bytes 221192 | tf_op jit(solution)/shard_map/ppermute | solution.py:289
  78.5 5.4 %collective-permute-start.3 = (bf16[144,256]{1,0:T(8,128)(2,1)S(1)}, bf16[144,256]{1,0:T(8,128)(2,1)S(1)}, u32[]{:S(2)}, u32[]{:S(2)}) collective-permute-start(bf16[144,256]{1,0:T(8,128)(2,1)S(1)} %get-tuple-element.27), channel_id=1, source_target_pairs={{0,3},{1,0},{2,1},{3,2},{4,7},{5,4},{6,5},{7,6},{8,11},{9,8},{10,9... | collective-permute-start | bytes 221192 | tf_op jit(solution)/shard_map/ppermute | solution.py:289
  92.2 34.8 %all-to-all-start.4 = ((bf16[4,272,256]{2,1,0:T(8,128)(2,1)}), bf16[4,272,256]{2,1,0:T(8,128)(2,1)S(1)}, u32[]{:S(2)}, u32[]{:S(2)}) async-start(bf16[4,272,256]{2,1,0:T(8,128)(2,1)} %get-tuple-element.29), calls=%async_computation.4 | async-start | bytes 1114112 | tf_op jit(solution)/shard_map/all_to_all | solution.py:274
  96.9 8.0 %collective-permute-start.6 = (bf16[128,256]{1,0:T(8,128)(2,1)S(1)}, bf16[128,256]{1,0:T(8,128)(2,1)S(1)}, u32[]{:S(2)}, u32[]{:S(2)}) collective-permute-start(bf16[128,256]{1,0:T(8,128)(2,1)S(1)} %get-tuple-element.30.mine.spread), channel_id=1, source_target_pairs={{0,3},{1,0},{2,1},{3,2},{4,7},{5,4},{6,5},{7,6},{8,11},{9,8},{10,9... | collective-permute-start | bytes 196616 | tf_op jit(solution)/shard_map/ppermute | solution.py:289
  100.0 6.8 %collective-permute-start.5 = (bf16[128,256]{1,0:T(8,128)(2,1)S(1)}, bf16[128,256]{1,0:T(8,128)(2,1)S(1)}, u32[]{:S(2)}, u32[]{:S(2)}) collective-permute-start(bf16[128,256]{1,0:T(8,128)(2,1)S(1)} %get-tuple-element.30.mine.spread), channel_id=1, source_target_pairs={{0,2},{1,3},{2,0},{3,1},{4,6},{5,7},{6,4},{7,5},{8,10},{9,11},{10,... | collective-permute-start | bytes 196616 | tf_op jit(solution)/shard_map/ppermute | solution.py:289
  103.0 7.1 %collective-permute-start.4 = (bf16[128,256]{1,0:T(8,128)(2,1)S(1)}, bf16[128,256]{1,0:T(8,128)(2,1)S(1)}, u32[]{:S(2)}, u32[]{:S(2)}) collective-permute-start(bf16[128,256]{1,0:T(8,128)(2,1)S(1)} %get-tuple-element.30.mine.spread), channel_id=1, source_target_pairs={{0,1},{1,2},{2,3},{3,0},{4,5},{5,6},{6,7},{7,4},{8,9},{9,10},{10,1... | collective-permute-start | bytes 196616 | tf_op jit(solution)/shard_map/ppermute | solution.py:289
  145.5 6.0 %collective-permute-start.7 = (bf16[2128,256]{1,0:T(8,128)(2,1)S(1)}, bf16[2128,256]{1,0:T(8,128)(2,1)S(1)}, u32[]{:S(2)}, u32[]{:S(2)}) collective-permute-start(bf16[2128,256]{1,0:T(8,128)(2,1)S(1)} %shard_map.117), channel_id=1, source_target_pairs={{0,16},{16,0},{1,17},{17,1},{2,18},{18,2},{3,19},{19,3},{4,20},{20... | collective-permute-start | bytes 3268616 | tf_op jit(solution)/shard_map/ppermute | solution.py:352

commit v5 on v4

--- a/solution.py
+++ b/solution.py
@@ -124,27 +124,33 @@
 
     each_slot(slots_of(cols, count[0, 0], 1 - core[0], order), step)
 
-    def put(out, r):
+    for to in range(4):
+        blocks = [4 * lax.rem(zh[0] + d, 4) + to for d in (1, 2, 3)]
+        for d, r in enumerate(blocks):
+            far[to, d * TILE : (d + 1) * TILE, :] = so_far(r).astype(BF)
+        one, two, three = (mass[r] for r in blocks)
+        row = lax.broadcasted_iota(jnp.int32, (EXTRA, TILE), 0)
+        far[to, 3 * TILE :, :] = mass_rows(
+            jnp.where(row == 0, one, jnp.where(row == 1, two, three))
+        )
+    for d, out in enumerate((mine, near1, near2, near3)):
+        r = 4 * zh[0] + lax.rem(y[0] + d, 4)
         out[0:TILE, :] = so_far(r).astype(BF)
-        out[TILE : TILE + EXTRA, :] = mass_rows(mass[r])
-
-    for d in (1, 2, 3):
-        for to in range(4):
-            put(far.at[to, d - 1], 4 * lax.rem(zh[0] + d, 4) + to)
-    for d, out in enumerate((mine, near1, near2, near3)):
-        put(out, 4 * zh[0] + lax.rem(y[0] + d, 4))
-
-
-def sum_y_kernel(zh, recv, out):
-    out[zh[0]] = jnp.zeros((TILE + EXTRA, H), BF)
-    for d in (1, 2, 3):
-        total = recv[0, d - 1].astype(F32)
-        for i in range(1, 4):
-            total += recv[i, d - 1].astype(F32)
-        z = lax.rem(zh[0] + d, 4)
-        out[z, 0:TILE, :] = total[0:TILE].astype(BF)
-        ends = total[TILE:]
-        out[z, TILE : TILE + EXTRA, :] = mass_rows(ends[:, 0:TILE] + ends[:, TILE:])
+        out[TILE:, :] = mass_rows(mass[r])
+
+
+def zh_rank(core, z):
+    return jnp.where(core[0] == 0, z, 3 - z)
+
+
+def sum_y_kernel(core, zh, recv, out):
+    out[zh_rank(core, zh[0])] = jnp.zeros((TILE + EXTRA, H), BF)
+    ends = sum_ref(recv, 4, slice(3 * TILE, 3 * TILE + EXTRA))
+    masses = ends[:, 0:TILE] + ends[:, TILE:]
+    for d in range(3):
+        z = zh_rank(core, lax.rem(zh[0] + d + 1, 4))
+        out[z, 0:TILE, :] = sum_ref(recv, 4, slice(d * TILE, (d + 1) * TILE)).astype(BF)
+        out[z, TILE:, :] = mass_rows(jnp.broadcast_to(masses[d : d + 1], (EXTRA, TILE)))
 
 
 def column(lanes):
@@ -172,28 +178,23 @@
     back = lax.dot_general(grad_pre, w, (((1,), (1,)), ((), ())), preferred_element_type=F32)
     spread_out[...] = (back / degree).astype(BF)
     degree_rows = mass_rows(degrees)
-    for z in range(4):
-        send[z, 0:TILE, :] = grad_pre
-        send[z, TILE : 2 * TILE, :] = aggregate
-        send[z, 2 * TILE :, :] = degree_rows
-
-
-def four_kernel(zh, recv, weight, out):
+    send[0:TILE, :] = grad_pre
+    send[TILE : 2 * TILE, :] = aggregate
+    send[2 * TILE :, :] = degree_rows
+
+
+def four_kernel(recv, weight, out):
     w = weight[...]
-    for d in (1, 2, 3):
-        z = lax.rem(zh[0] + d, 4)
-        ends = recv[z, 2 * TILE :, :].astype(F32)
-        degree = column(ends[0:1, 0:TILE] + ends[0:1, TILE:])
-        back = lax.dot_general(
-            recv[z, 0:TILE, :], w, (((1,), (1,)), ((), ())), preferred_element_type=F32
-        )
-        spread = (back / degree).astype(BF)
-        for y in range(4):
-            out[y, (d - 1) * TILE : d * TILE, :] = spread
     term = jnp.zeros((H, H), F32)
     bias_term = jnp.zeros((1, H), F32)
     for z in range(4):
         grad_pre = recv[z, 0:TILE, :]
+        ends = recv[z, 2 * TILE :, :].astype(F32)
+        degree = column(ends[0:1, 0:TILE] + ends[0:1, TILE:])
+        back = lax.dot_general(grad_pre, w, (((1,), (1,)), ((), ())), preferred_element_type=F32)
+        spread = (back / degree).astype(BF)
+        for y in range(4):
+            out[y, z * TILE : (z + 1) * TILE, :] = spread
         term += lax.dot_general(
             recv[z, TILE : 2 * TILE, :],
             grad_pre,
@@ -203,8 +204,8 @@
         bias_term += jnp.sum(grad_pre.astype(F32), axis=0, keepdims=True)
     bias_rows = split_rows(bias_term)
     for y in range(4):
-        out[y, 3 * TILE : 3 * TILE + PIECE, :] = term[PIECE * y : PIECE * (y + 1)].astype(BF)
-        out[y, 3 * TILE + PIECE :, :] = bias_rows
+        out[y, 4 * TILE : 4 * TILE + PIECE, :] = term[PIECE * y : PIECE * (y + 1)].astype(BF)
+        out[y, 4 * TILE + PIECE :, :] = bias_rows
 
 
 def tail_sum(total):
@@ -212,21 +213,15 @@
     return jnp.concatenate([total[0:PIECE].astype(BF), ends], axis=0)
 
 
-def backward_kernel(
-    flip, rows, cols, count, core, zh, y, tiles, far, mine, near1, near2, near3, out, near, acc, seen, order
-):
+def backward_kernel(flip, rows, cols, count, core, tiles, spread, out, acc, seen, order):
     clear(seen, 16)
-    for d, block in enumerate((mine, near1, near2, near3)):
-        near[lax.rem(y[0] + 4 - d, 4)] = block[...]
     parity = 1 - core[0] if flip else core[0]
 
     def step(i):
         t = order[i]
         c, r = cols[0, t] // 2, rows[0, t]
-        d = lax.rem(r // 4 + 4 - zh[0], 4)
-        start = pl.multiple_of(jnp.maximum(d - 1, 0) * TILE, TILE)
-        at_y = lax.rem(r, 4)
-        block = jnp.where(d == 0, near[at_y], far[at_y, pl.ds(start, TILE), :])
+        start = pl.multiple_of((r // 4) * TILE, TILE)
+        block = spread[lax.rem(r, 4), pl.ds(start, TILE), :]
         product = lax.dot_general(
             tiles[t], block, (((0,), (0,)), ((), ())), preferred_element_type=F32
         )
@@ -236,7 +231,7 @@
     each_slot(slots_of(cols, count[0, 0], parity, order), step)
     for i in range(16):
         out[i * TILE : (i + 1) * TILE, :] = jnp.where(seen[i] == 1, acc[i], 0.0).astype(BF)
-    out[16 * TILE :, :] = tail_sum(sum_ref(far, 4, slice(3 * TILE, 3 * TILE + TAIL)))
+    out[16 * TILE :, :] = tail_sum(sum_ref(spread, 4, slice(4 * TILE, 4 * TILE + TAIL)))
 
 
 def sum_k_kernel(core, keep, recv, out):
@@ -282,6 +277,11 @@
 
 def exchange_col(value, groups):
     return lax.all_to_all(value, COL, 0, 0, axis_index_groups=groups)
+
+
+def exchange_zh(value):
+    groups = [[0, 1, 2, 3], [7, 6, 5, 4]]
+    return lax.all_to_all(value, ("k", "zh"), 0, 0, axis_index_groups=groups)
 
 
 def along_y(*blocks):
@@ -318,36 +318,35 @@
     one_block = shape((TILE + EXTRA, H), BF)
     part, near1, near2, near3, mine = call(
         forward_kernel,
-        (shape((4, 3, TILE + EXTRA, H), BF),) + (one_block,) * 4,
+        (shape((4, 3 * TILE + EXTRA, H), BF),) + (one_block,) * 4,
         6,
         4,
         (pltpu.VMEM((16, TILE, H), F32), pltpu.VMEM((16, EXTRA, TILE), F32)) + flags,
         300000000,
     )(rows, cols, tile_count, core, zh, y, tiles, other, begun, mass)
     part = exchange(part, "y")
-    part = call(sum_y_kernel, shape((4, TILE + EXTRA, H), BF), 1, 1)(zh, part)
-    part = exchange(part, "zh")
+    part = call(sum_y_kernel, shape((4, TILE + EXTRA, H), BF), 2, 1)(core, zh, part)
+    part = exchange_zh(part)
     near = along_y(near1, near2, near3)
     node_out, spread, send = call(
         node_kernel,
-        (shape((TILE, H), BF), shape((TILE, H), BF), shape((4, 2 * TILE + EXTRA, H), BF)),
+        (shape((TILE, H), BF), shape((TILE, H), BF), shape((2 * TILE + EXTRA, H), BF)),
         0,
         9,
     )(part, mine, *near, features, grad_out, weight, bias.reshape(1, H))
-    send = exchange(send, "zh")
-    send, *near = lax.optimization_barrier([send, *along_y(spread, spread, spread)])
-    send = call(four_kernel, shape((4, 3 * TILE + TAIL, H), BF), 1, 2)(zh, send, weight)
+    send = lax.all_gather(send, "zh")
+    send = call(four_kernel, shape((4, 4 * TILE + TAIL, H), BF), 0, 2)(send, weight)
     send = exchange(send, "y")
     flat = shape((16 * TILE + TAIL, H), BF)
     def terms(flip):
         return call(
             functools.partial(backward_kernel, flip),
             flat,
-            6,
-            6,
-            (pltpu.VMEM((4, TILE, H), BF),) + scratch,
+            4,
+            2,
+            scratch,
             300000000,
-        )(rows, cols, tile_count, core, zh, y, tiles, send, spread, *near)
+        )(rows, cols, tile_count, core, tiles, send)
 
     back = lax.ppermute(terms(1), "k", swap)
     keep = terms(0)

time: 191 us -> 184 us (0.963)
  blocking collectives: 98.9 us -> 135 us
  waiting for transfers between devices: 32 us -> 5.57 us
  starting transfers between devices: 42.9 us -> 30.3 us
  Pallas kernels: 13.4 us -> 10.3 us
    all_gather x0 -> x1, blocking collectives: none -> 31.5 us  [shards(): send = lax.all_gather(send, 'zh')]
    all_to_all x2 -> x1, waiting for transfers between devices: 24 us -> 1.68 us  [exchange_zh(): return lax.all_to_all(value, ('k', 'zh'), 0, 0, axis_index_groups=groups)]
    ppermute x6 -> x3, starting transfers between devices: 16.4 us -> 8.5 us  [along_y(): lax.ppermute(block, 'y', [(i, (i + d) % 4) for i in range(4)])]
    all_to_all x2 -> x1, starting transfers between devices: 17 us -> 11.9 us  [exchange_zh(): return lax.all_to_all(value, ('k', 'zh'), 0, 0, axis_index_groups=groups)]
    all_to_all x5, blocking collectives: 69.7 us -> 74.7 us  [exchange(): return lax.all_to_all(value, axis, 0, 0)]
    ppermute x6 -> x3, waiting for transfers between devices: 8.01 us -> 3.29 us  [along_y(): lax.ppermute(block, 'y', [(i, (i + d) % 4) for i in range(4)])]
    pallas_call x6, Pallas kernels: 9.98 us -> 7.61 us  [the longest x2 3.42 us: terms(): call(functools.partial(backward_kernel, flip), flat, 4, 2, scratch, 30000...]
  transfers between devices with their start and end apart: 10 -> 6, of which waited for: 6 -> 4; matrix products, arithmetic and copies ran while one was open for 0% -> 0% of each run, Pallas kernels for 3% -> 2%
where the time goes in v5:
time: 184 us
  blocking collectives  135 us (73%)
  starting transfers between devices  30.3 us (16%)
  Pallas kernels  10.3 us (6%)
  waiting for transfers between devices  5.57 us (3%)
    all_to_all x5, blocking collectives, exchange(): return lax.all_to_all(value, axis, 0, 0)  74.7 us
    all_gather x1, blocking collectives, shards(): send = lax.all_gather(send, 'zh')  31.5 us
    all_to_all x2, blocking collectives, exchange_col(): return lax.all_to_all(value, COL, 0, 0, axis_index_groups=groups)  28.4 us
    all_to_all x1, starting transfers between devices, exchange_zh(): return lax.all_to_all(value, ('k', 'zh'), 0, 0, axis_index_groups=groups)  11.9 us
    ppermute x3, starting transfers between devices, along_y(): lax.ppermute(block, 'y', [(i, (i + d) % 4) for i in range(4)])  8.5 us
    ppermute x1, starting transfers between devices, shards(): other = lax.ppermute(own, 'k', swap)  6.04 us
    ppermute x1, starting transfers between devices, shards(): back = lax.ppermute(terms(1), 'k', swap)  3.84 us
  transfers between devices with their start and end apart: 6, of which 4 were waited for; matrix products, arithmetic and copies ran while one was open for 0% of the time, Pallas kernels for 2%

profile of v5, /device:TPU:1, one launch (start us, length us, event | category | flops | bytes accessed | tf_op | source)
XLA Modules:
  0.0 183.9 jit_solution(10762808864895917972)
XLA Ops:
  0.6 0.9 broadcast_in_dim.4
  1.5 12.2 %all_to_all.40 = bf16[4,128,256]{2,1,0:T(8,128)(2,1)S(1)} all-to-all(bf16[4,128,256]{2,1,0:T(8,128)(2,1)S(1)} %broadcast_in_dim.4), channel_id=1, replica_groups=mesh['x'=4,'zl'=4,'k'=2,'zh'=4,'y'=4] {'zl'}, dimensions={0} | all-to-all | bytes 524288 | tf_op jit(solution)/shard_map/all_to_all | solution.py:269
  13.7 0.1 broadcast_in_dim.5
  13.8 0.0 copy-start
  13.8 0.0 copy-start.4
  13.8 0.0 copy-start.5
  13.9 16.8 %all_to_all.41 = bf16[4,4,128,256]{3,2,1,0:T(8,128)(2,1)S(1)} all-to-all(bf16[4,4,128,256]{3,2,1,0:T(8,128)(2,1)S(1)} %broadcast_in_dim.5), channel_id=1, replica_groups=mesh['x'=4,'zl'=4,'k'=2,'zh'=4,'y'=4] {'x'}, dimensions={0} | all-to-all | bytes 2097152 | tf_op jit(solution)/shard_map/all_to_all | solution.py:269
  30.6 6.0 %collective-permute-start = (bf16[16,128,256]{2,1,0:T(8,128)(2,1)S(1)}, bf16[16,128,256]{2,1,0:T(8,128)(2,1)S(1)}, u32[]{:S(2)}, u32[]{:S(2)}) collective-permute-start(bf16[16,128,256]{2,1,0:T(8,128)(2,1)S(1)} %bitcast.15), channel_id=1, source_target_pairs={{0,16},{16,0},{1,17},{17,1},{2,18},{18,2},{3,19},{19,3},{4,20},{20... | collective-permute-start | bytes 3145736 | tf_op jit(solution)/shard_map/ppermute | solution.py:307
  37.3 0.0 copy-done
  37.3 0.0 copy-done.4
  37.3 0.0 copy-done.5
  37.3 1.6 shard_map.111
  38.9 0.0 collective-permute-done.other
  38.9 2.0 %shard_map.112 = (bf16[4,400,256]{2,1,0:T(8,128)(2,1)S(1)}, bf16[144,256]{1,0:T(8,128)(2,1)S(1)}, bf16[144,256]{1,0:T(8,128)(2,1)S(1)}, bf16[144,256]{1,0:T(8,128)(2,1)S(1)}, bf16[144,256]{1,0:T(8,128)(2,1)S(1)}) custom-call(s32[1,32]{1,0:T(1,128)S(1)} %bitcast.19, s32[1,32]{1,0:T(1,128)S(1)} %bitcast.23, s32[1,1]{1,0:T(1,128)S(6)} %copy.12.count, ...), custom_call_target="tpu_custom_call" | custom-call | flops 300000000 | bytes 4000000 | tf_op jit(solution)/shard_map/pallas_call | solution.py:319
  40.9 19.0 %all_to_all.42.recv = bf16[4,400,256]{2,1,0:T(8,128)(2,1)S(1)} all-to-all(bf16[4,400,256]{2,1,0:T(8,128)(2,1)S(1)} %get-tuple-element.19), channel_id=1, replica_groups=mesh['x'=4,'zl'=4,'k'=2,'zh'=4,'y'=4] {'y'}, dimensions={0} | all-to-all | bytes 1638400 | tf_op jit(solution)/shard_map/all_to_all | solution.py:269
  60.0 0.0 copy-start.1
  60.0 0.0 copy-start.2
  60.0 0.0 copy-start.3
  60.0 0.0 copy-start.6
  60.0 0.8 shard_map.113
  60.8 11.9 %all-to-all-start.3 = ((bf16[4,144,256]{2,1,0:T(8,128)(2,1)}), bf16[4,144,256]{2,1,0:T(8,128)(2,1)S(1)}, u32[]{:S(2)}, u32[]{:S(2)}) async-start(bf16[4,144,256]{2,1,0:T(8,128)(2,1)} %shard_map.113), calls=%async_computation.3 | async-start | bytes 589824 | tf_op jit(solution)/shard_map/all_to_all | solution.py:284
  72.8 2.2 %collective-permute-start.1 = (bf16[144,256]{1,0:T(8,128)(2,1)S(1)}, bf16[144,256]{1,0:T(8,128)(2,1)S(1)}, u32[]{:S(2)}, u32[]{:S(2)}) collective-permute-start(bf16[144,256]{1,0:T(8,128)(2,1)S(1)} %get-tuple-element.21), channel_id=1, source_target_pairs={{0,1},{1,2},{2,3},{3,0},{4,5},{5,6},{6,7},{7,4},{8,9},{9,10},{10,1... | collective-permute-start | bytes 221192 | tf_op jit(solution)/shard_map/ppermute | solution.py:289
  74.9 3.7 %collective-permute-start.2 = (bf16[144,256]{1,0:T(8,128)(2,1)S(1)}, bf16[144,256]{1,0:T(8,128)(2,1)S(1)}, u32[]{:S(2)}, u32[]{:S(2)}) collective-permute-start(bf16[144,256]{1,0:T(8,128)(2,1)S(1)} %get-tuple-element.22), channel_id=1, source_target_pairs={{0,2},{1,3},{2,0},{3,1},{4,6},{5,7},{6,4},{7,5},{8,10},{9,11},{10,... | collective-permute-start | bytes 221192 | tf_op jit(solution)/shard_map/ppermute | solution.py:289
  78.6 2.6 %collective-permute-start.3 = (bf16[144,256]{1,0:T(8,128)(2,1)S(1)}, bf16[144,256]{1,0:T(8,128)(2,1)S(1)}, u32[]{:S(2)}, u32[]{:S(2)}) collective-permute-start(bf16[144,256]{1,0:T(8,128)(2,1)S(1)} %get-tuple-element.23), channel_id=1, source_target_pairs={{0,3},{1,0},{2,1},{3,2},{4,7},{5,4},{6,5},{7,6},{8,11},{9,8},{10,9... | collective-permute-start | bytes 221192 | tf_op jit(solution)/shard_map/ppermute | solution.py:289
  81.3 0.0 collective-permute-done.1.near1
  81.3 0.8 collective-permute-done.2.near2
  82.1 2.5 %collective-permute-done.3.near3 = bf16[144,256]{1,0:T(8,128)(2,1)S(1)} collective-permute-done((bf16[144,256]{1,0:T(8,128)(2,1)S(1)}, bf16[144,256]{1,0:T(8,128)(2,1)S(1)}, u32[]{:S(2)}, u32[]{:S(2)}) %collective-permute-start.3) | collective-permute-done | bytes 73760 | tf_op jit(solution)/shard_map/ppermute | solution.py:289
  84.6 1.7 all-to-all-done.3.recv
  86.3 0.0 copy-done.1
  86.3 0.0 copy-done.2
  86.3 0.0 copy-done.3
  86.3 0.0 copy-done.6
  86.3 0.9 shard_map.114
  87.2 31.5 %all-gather = bf16[1088,256]{1,0:T(8,128)(2,1)S(1)} all-gather(bf16[272,256]{1,0:T(8,128)(2,1)S(1)} %get-tuple-element.25), channel_id=2, replica_groups=mesh['x'=4,'zl'=4,'k'=2,'zh'=4,'y'=4] {'zh'}, dimensions={0}, use_global_device_ids=true | all-gather | bytes 696320 | tf_op jit(solution)/shard_map/all_gather | solution.py:337
  118.7 0.5 shard_map.115
  119.1 19.2 %all_to_all.43.spread = bf16[4,592,256]{2,1,0:T(8,128)(2,1)S(1)} all-to-all(bf16[4,592,256]{2,1,0:T(8,128)(2,1)S(1)} %shard_map.115), channel_id=1, replica_groups=mesh['x'=4,'zl'=4,'k'=2,'zh'=4,'y'=4] {'y'}, dimensions={0} | all-to-all | bytes 2424832 | tf_op jit(solution)/shard_map/all_to_all | solution.py:269
  138.3 1.7 shard_map.117
  140.0 3.8 %collective-permute-start.4 = (bf16[2128,256]{1,0:T(8,128)(2,1)S(1)}, bf16[2128,256]{1,0:T(8,128)(2,1)S(1)}, u32[]{:S(2)}, u32[]{:S(2)}) collective-permute-start(bf16[2128,256]{1,0:T(8,128)(2,1)S(1)} %shard_map.117), channel_id=1, source_target_pairs={{0,16},{16,0},{1,17},{17,1},{2,18},{18,2},{3,19},{19,3},{4,20},{20... | collective-permute-start | bytes 3268616 | tf_op jit(solution)/shard_map/ppermute | solution.py:351
  143.9 1.7 shard_map.116.keep
  145.6 0.6 collective-permute-done.4.recv
  146.2 0.3 shard_map.118
  146.4 18.9 %all_to_all.44.recv = bf16[4,592,256]{2,1,0:T(8,128)(2,1)S(1)} all-to-all(bf16[4,592,256]{2,1,0:T(8,128)(2,1)S(1)} %shard_map.118), channel_id=1, replica_groups={{0,128,256,384},{32,160,288,416},{64,192,320,448},{96,224,352,480},{16,..., dimensions={0} | all-to-all | bytes 2424832 | tf_op jit(solution)/shard_map/all_to_all | solution.py:279
  165.4 0.2 shard_map.119
  165.5 9.5 %all_to_all.45.recv = bf16[4,208,256]{2,1,0:T(8,128)(2,1)S(1)} all-to-all(bf16[4,208,256]{2,1,0:T(8,128)(2,1)S(1)} %shard_map.119), channel_id=1, replica_groups={{0,32,64,96},{128,160,192,224},{256,288,320,352},{384,416,448,480},{16,..., dimensions={0} | all-to-all | bytes 851968 | tf_op jit(solution)/shard_map/all_to_all | solution.py:279
  175.0 0.7 shard_map.120
  175.7 7.4 %all_to_all.46 = bf16[4,64,256]{2,1,0:T(8,128)(2,1)S(1)} all-to-all(bf16[4,64,256]{2,1,0:T(8,128)(2,1)S(1)} %get-tuple-element.28), channel_id=1, replica_groups=mesh['x'=4,'zl'=4,'k'=2,'zh'=4,'y'=4] {'y'}, dimensions={0} | all-to-all | bytes 262144 | tf_op jit(solution)/shard_map/all_to_all | solution.py:269
  183.1 0.7 convert_multiply_fusion
Async XLA Ops:
  13.8 23.5 %copy-start = (bf16[1,1,32,128,128]{4,3,2,1,0:T(8,128)(2,1)S(1)}, bf16[1,1,32,128,128]{4,3,2,1,0:T(8,128)(2,1)}, u32[]{:S(2)}) copy-start(bf16[1,1,32,128,128]{4,3,2,1,0:T(8,128)(2,1)} %param.14) | copy-start | bytes 3145732
  13.8 23.5 %copy-start.4 = (s32[1,1,32]{2,1,0:T(1,128)S(1)}, s32[1,1,32]{2,1,0:T(1,128)}, u32[]{:S(2)}) copy-start(s32[1,1,32]{2,1,0:T(1,128)} %param.12) | copy-start | bytes 388
  13.8 23.5 %copy-start.5 = (s32[1,1,32]{2,1,0:T(1,128)S(1)}, s32[1,1,32]{2,1,0:T(1,128)}, u32[]{:S(2)}) copy-start(s32[1,1,32]{2,1,0:T(1,128)} %param.13) | copy-start | bytes 388
  30.6 8.3 %collective-permute-start = (bf16[16,128,256]{2,1,0:T(8,128)(2,1)S(1)}, bf16[16,128,256]{2,1,0:T(8,128)(2,1)S(1)}, u32[]{:S(2)}, u32[]{:S(2)}) collective-permute-start(bf16[16,128,256]{2,1,0:T(8,128)(2,1)S(1)} %bitcast.15), channel_id=1, source_target_pairs={{0,16},{16,0},{1,17},{17,1},{2,18},{18,2},{3,19},{19,3},{4,20},{20... | collective-permute-start | bytes 3145736 | tf_op jit(solution)/shard_map/ppermute | solution.py:307
  60.0 26.3 %copy-start.1 = (bf16[256,256]{1,0:T(8,128)(2,1)S(1)}, bf16[256,256]{1,0:T(8,128)(2,1)}, u32[]{:S(2)}) copy-start(bf16[256,256]{1,0:T(8,128)(2,1)} %weight.3) | copy-start | bytes 393220
  60.0 26.3 %copy-start.2 = (bf16[128,256]{1,0:T(8,128)(2,1)S(1)}, bf16[128,256]{1,0:T(8,128)(2,1)}, u32[]{:S(2)}) copy-start(bf16[128,256]{1,0:T(8,128)(2,1)} %features.1) | copy-start | bytes 196612
  60.0 26.3 %copy-start.3 = (bf16[128,256]{1,0:T(8,128)(2,1)S(1)}, bf16[128,256]{1,0:T(8,128)(2,1)}, u32[]{:S(2)}) copy-start(bf16[128,256]{1,0:T(8,128)(2,1)} %grad_out.1) | copy-start | bytes 196612
  60.0 26.3 %copy-start.6 = (f32[256]{0:T(256)S(1)}, f32[256]{0:T(256)}, u32[]{:S(2)}) copy-start(f32[256]{0:T(256)} %param.11) | copy-start | bytes 3076
  60.8 25.4 %all-to-all-start.3 = ((bf16[4,144,256]{2,1,0:T(8,128)(2,1)}), bf16[4,144,256]{2,1,0:T(8,128)(2,1)S(1)}, u32[]{:S(2)}, u32[]{:S(2)}) async-start(bf16[4,144,256]{2,1,0:T(8,128)(2,1)} %shard_map.113), calls=%async_computation.3 | async-start | bytes 589824 | tf_op jit(solution)/shard_map/all_to_all | solution.py:284
  72.8 8.5 %collective-permute-start.1 = (bf16[144,256]{1,0:T(8,128)(2,1)S(1)}, bf16[144,256]{1,0:T(8,128)(2,1)S(1)}, u32[]{:S(2)}, u32[]{:S(2)}) collective-permute-start(bf16[144,256]{1,0:T(8,128)(2,1)S(1)} %get-tuple-element.21), channel_id=1, source_target_pairs={{0,1},{1,2},{2,3},{3,0},{4,5},{5,6},{6,7},{7,4},{8,9},{9,10},{10,1... | collective-permute-start | bytes 221192 | tf_op jit(solution)/shard_map/ppermute | solution.py:289
  74.9 7.2 %collective-permute-start.2 = (bf16[144,256]{1,0:T(8,128)(2,1)S(1)}, bf16[144,256]{1,0:T(8,128)(2,1)S(1)}, u32[]{:S(2)}, u32[]{:S(2)}) collective-permute-start(bf16[144,256]{1,0:T(8,128)(2,1)S(1)} %get-tuple-element.22), channel_id=1, source_target_pairs={{0,2},{1,3},{2,0},{3,1},{4,6},{5,7},{6,4},{7,5},{8,10},{9,11},{10,... | collective-permute-start | bytes 221192 | tf_op jit(solution)/shard_map/ppermute | solution.py:289
  78.6 5.9 %collective-permute-start.3 = (bf16[144,256]{1,0:T(8,128)(2,1)S(1)}, bf16[144,256]{1,0:T(8,128)(2,1)S(1)}, u32[]{:S(2)}, u32[]{:S(2)}) collective-permute-start(bf16[144,256]{1,0:T(8,128)(2,1)S(1)} %get-tuple-element.23), channel_id=1, source_target_pairs={{0,3},{1,0},{2,1},{3,2},{4,7},{5,4},{6,5},{7,6},{8,11},{9,8},{10,9... | collective-permute-start | bytes 221192 | tf_op jit(solution)/shard_map/ppermute | solution.py:289
  140.0 6.2 %collective-permute-start.4 = (bf16[2128,256]{1,0:T(8,128)(2,1)S(1)}, bf16[2128,256]{1,0:T(8,128)(2,1)S(1)}, u32[]{:S(2)}, u32[]{:S(2)}) collective-permute-start(bf16[2128,256]{1,0:T(8,128)(2,1)S(1)} %shard_map.117), channel_id=1, source_target_pairs={{0,16},{16,0},{1,17},{17,1},{2,18},{18,2},{3,19},{19,3},{4,20},{20... | collective-permute-start | bytes 3268616 | tf_op jit(solution)/shard_map/ppermute | solution.py:351

commit v6 on v5

--- a/solution.py
+++ b/solution.py
@@ -128,15 +128,13 @@
         blocks = [4 * lax.rem(zh[0] + d, 4) + to for d in (1, 2, 3)]
         for d, r in enumerate(blocks):
             far[to, d * TILE : (d + 1) * TILE, :] = so_far(r).astype(BF)
-        one, two, three = (mass[r] for r in blocks)
         row = lax.broadcasted_iota(jnp.int32, (EXTRA, TILE), 0)
-        far[to, 3 * TILE :, :] = mass_rows(
-            jnp.where(row == 0, one, jnp.where(row == 1, two, three))
-        )
+        masses = mass[to]
+        for z in (1, 2, 3):
+            masses = jnp.where(row == z, mass[4 * z + to], masses)
+        far[to, 3 * TILE :, :] = mass_rows(masses)
     for d, out in enumerate((mine, near1, near2, near3)):
-        r = 4 * zh[0] + lax.rem(y[0] + d, 4)
-        out[0:TILE, :] = so_far(r).astype(BF)
-        out[TILE:, :] = mass_rows(mass[r])
+        out[...] = so_far(4 * zh[0] + lax.rem(y[0] + d, 4)).astype(BF)
 
 
 def zh_rank(core, z):
@@ -144,13 +142,14 @@
 
 
 def sum_y_kernel(core, zh, recv, out):
-    out[zh_rank(core, zh[0])] = jnp.zeros((TILE + EXTRA, H), BF)
     ends = sum_ref(recv, 4, slice(3 * TILE, 3 * TILE + EXTRA))
-    masses = ends[:, 0:TILE] + ends[:, TILE:]
+    masses = mass_rows(ends[:, 0:TILE] + ends[:, TILE:])
+    for z in range(4):
+        out[z, TILE:, :] = masses
+    out[zh_rank(core, zh[0]), 0:TILE, :] = jnp.zeros((TILE, H), BF)
     for d in range(3):
         z = zh_rank(core, lax.rem(zh[0] + d + 1, 4))
         out[z, 0:TILE, :] = sum_ref(recv, 4, slice(d * TILE, (d + 1) * TILE)).astype(BF)
-        out[z, TILE:, :] = mass_rows(jnp.broadcast_to(masses[d : d + 1], (EXTRA, TILE)))
 
 
 def column(lanes):
@@ -161,14 +160,17 @@
 
 
 def node_kernel(
-    recv, mine, near1, near2, near3, features, grad_out, weight, bias, node_out, spread_out, send
+    zh, recv, mine, near1, near2, near3, features, grad_out, weight, bias, node_out, spread_out, send, degrees
 ):
-    total = mine[...].astype(F32) + recv[0].astype(F32)
-    for block in (recv[1], recv[2], recv[3], near1[...], near2[...], near3[...]):
+    parts = [recv[z, 0:TILE, :] for z in range(4)] + [near1[...], near2[...], near3[...]]
+    total = mine[...].astype(F32)
+    for block in parts:
         total += block.astype(F32)
-    ends = total[TILE:]
-    degrees = 1.0 + ends[:, 0:TILE] + ends[:, TILE:]
-    degree = column(degrees[0:1])
+    ends = sum_ref(recv, 4, slice(TILE, TILE + EXTRA))
+    rows = 1.0 + ends[:, 0:TILE] + ends[:, TILE:]
+    degrees[...] = rows
+    here = lax.broadcasted_iota(jnp.int32, (EXTRA, TILE), 0) == zh[0]
+    degree = column(jnp.sum(jnp.where(here, rows, 0.0), axis=0, keepdims=True))
     aggregate = ((features[...].astype(F32) + total[0:TILE]) / degree).astype(BF)
     w = weight[...]
     pre = jnp.dot(aggregate, w, preferred_element_type=F32) + bias[...]
@@ -177,20 +179,17 @@
     grad_pre = (grad_out[...].astype(F32) * (sig * (1.0 + pre * (1.0 - sig)))).astype(BF)
     back = lax.dot_general(grad_pre, w, (((1,), (1,)), ((), ())), preferred_element_type=F32)
     spread_out[...] = (back / degree).astype(BF)
-    degree_rows = mass_rows(degrees)
     send[0:TILE, :] = grad_pre
     send[TILE : 2 * TILE, :] = aggregate
-    send[2 * TILE :, :] = degree_rows
-
-
-def four_kernel(recv, weight, out):
+
+
+def four_kernel(recv, degrees, weight, out):
     w = weight[...]
     term = jnp.zeros((H, H), F32)
     bias_term = jnp.zeros((1, H), F32)
     for z in range(4):
         grad_pre = recv[z, 0:TILE, :]
-        ends = recv[z, 2 * TILE :, :].astype(F32)
-        degree = column(ends[0:1, 0:TILE] + ends[0:1, TILE:])
+        degree = column(degrees[z : z + 1, :])
         back = lax.dot_general(grad_pre, w, (((1,), (1,)), ((), ())), preferred_element_type=F32)
         spread = (back / degree).astype(BF)
         for y in range(4):
@@ -315,7 +314,7 @@
         flags,
         300000000,
     )(rows, cols, tile_count, core, tiles, own)
-    one_block = shape((TILE + EXTRA, H), BF)
+    one_block = shape((TILE, H), BF)
     part, near1, near2, near3, mine = call(
         forward_kernel,
         (shape((4, 3 * TILE + EXTRA, H), BF),) + (one_block,) * 4,
@@ -328,14 +327,21 @@
     part = call(sum_y_kernel, shape((4, TILE + EXTRA, H), BF), 2, 1)(core, zh, part)
     part = exchange_zh(part)
     near = along_y(near1, near2, near3)
-    node_out, spread, send = call(
+    node_out, spread, send, degrees = call(
         node_kernel,
-        (shape((TILE, H), BF), shape((TILE, H), BF), shape((2 * TILE + EXTRA, H), BF)),
-        0,
+        (
+            shape((TILE, H), BF),
+            shape((TILE, H), BF),
+            shape((2 * TILE, H), BF),
+            shape((EXTRA, TILE), F32),
+        ),
+        1,
         9,
-    )(part, mine, *near, features, grad_out, weight, bias.reshape(1, H))
+    )(zh, part, mine, *near, features, grad_out, weight, bias.reshape(1, H))
     send = lax.all_gather(send, "zh")
-    send = call(four_kernel, shape((4, 4 * TILE + TAIL, H), BF), 0, 2)(send, weight)
+    send = call(four_kernel, shape((4, 4 * TILE + TAIL, H), BF), 0, 3)(
+        send, degrees, weight
+    )
     send = exchange(send, "y")
     flat = shape((16 * TILE + TAIL, H), BF)
     def terms(flip):

time: 184 us -> 184 us (level); the launches traced: 184 us -> 181 us
  blocking collectives: 135 us -> 123 us
  starting transfers between devices: 30.3 us -> 38.7 us
  Pallas kernels: 10.3 us -> 13.4 us
  waiting for transfers between devices: 5.57 us -> 3.1 us
    all_gather x1, blocking collectives: 31.5 us -> 20.4 us  [shards(): send = lax.all_gather(send, 'zh')]
    ppermute x1, starting transfers between devices: 3.84 us -> 11.6 us  [shards(): back = lax.ppermute(terms(1), 'k', swap)]
    all_to_all x5, blocking collectives: 74.7 us -> 67.6 us  [exchange(): return lax.all_to_all(value, axis, 0, 0)]
    all_to_all x2, blocking collectives: 28.4 us -> 34.6 us  [exchange_col(): return lax.all_to_all(value, COL, 0, 0, axis_index_groups=groups)]
  transfers between devices with their start and end apart: 6 -> 6, of which waited for: 4 -> 2; matrix products, arithmetic and copies ran while one was open for 0% -> 0% of each run, Pallas kernels for 2% -> 3%
where the time goes in v6:
time: 184 us; the launch traced here: 181 us
  blocking collectives  123 us (67%)
  starting transfers between devices  38.7 us (21%)
  Pallas kernels  13.4 us (7%)
  waiting for transfers between devices  3.1 us (2%)
    all_to_all x5, blocking collectives, exchange(): return lax.all_to_all(value, axis, 0, 0)  67.6 us
    all_to_all x2, blocking collectives, exchange_col(): return lax.all_to_all(value, COL, 0, 0, axis_index_groups=groups)  34.6 us
    all_gather x1, blocking collectives, shards(): send = lax.all_gather(send, 'zh')  20.4 us
    all_to_all x1, starting transfers between devices, exchange_zh(): return lax.all_to_all(value, ('k', 'zh'), 0, 0, axis_index_groups=groups)  12.3 us
    ppermute x1, starting transfers between devices, shards(): back = lax.ppermute(terms(1), 'k', swap)  11.6 us
    ppermute x3, starting transfers between devices, along_y(): lax.ppermute(block, 'y', [(i, (i + d) % 4) for i in range(4)])  8.67 us
    ppermute x1, starting transfers between devices, shards(): other = lax.ppermute(own, 'k', swap)  6.04 us
    pallas_call x2, Pallas kernels, terms(): call(functools.partial(backward_kernel, flip), flat, 4, 2, scratch, 30000...  4.94 us
  transfers between devices with their start and end apart: 6, of which 2 were waited for; matrix products, arithmetic and copies ran while one was open for 0% of the time, Pallas kernels for 3%

profile of v6, /device:TPU:1, one launch (start us, length us, event | category | flops | bytes accessed | tf_op | source)
XLA Modules:
  0.0 181.0 jit_solution(5905966510069604318)
XLA Ops:
  0.6 0.9 broadcast_in_dim.4
  1.5 12.2 %all_to_all.40 = bf16[4,128,256]{2,1,0:T(8,128)(2,1)S(1)} all-to-all(bf16[4,128,256]{2,1,0:T(8,128)(2,1)S(1)} %broadcast_in_dim.4), channel_id=1, replica_groups=mesh['x'=4,'zl'=4,'k'=2,'zh'=4,'y'=4] {'zl'}, dimensions={0} | all-to-all | bytes 524288 | tf_op jit(solution)/shard_map/all_to_all | solution.py:268
  13.7 0.1 broadcast_in_dim.5
  13.8 0.0 copy-start
  13.8 0.0 copy-start.4
  13.8 0.0 copy-start.5
  13.9 16.8 %all_to_all.41 = bf16[4,4,128,256]{3,2,1,0:T(8,128)(2,1)S(1)} all-to-all(bf16[4,4,128,256]{3,2,1,0:T(8,128)(2,1)S(1)} %broadcast_in_dim.5), channel_id=1, replica_groups=mesh['x'=4,'zl'=4,'k'=2,'zh'=4,'y'=4] {'x'}, dimensions={0} | all-to-all | bytes 2097152 | tf_op jit(solution)/shard_map/all_to_all | solution.py:268
  30.6 6.0 %collective-permute-start = (bf16[16,128,256]{2,1,0:T(8,128)(2,1)S(1)}, bf16[16,128,256]{2,1,0:T(8,128)(2,1)S(1)}, u32[]{:S(2)}, u32[]{:S(2)}) collective-permute-start(bf16[16,128,256]{2,1,0:T(8,128)(2,1)S(1)} %bitcast.15), channel_id=1, source_target_pairs={{0,16},{16,0},{1,17},{17,1},{2,18},{18,2},{3,19},{19,3},{4,20},{20... | collective-permute-start | bytes 3145736 | tf_op jit(solution)/shard_map/ppermute | solution.py:306
  37.3 0.0 copy-done
  37.3 0.0 copy-done.4
  37.3 0.0 copy-done.5
  37.3 2.3 %shard_map.111 = (f32[16,128,256]{2,1,0:T(8,128)S(1)}, f32[16,16,128]{2,1,0:T(8,128)S(1)}) custom-call(s32[1,32]{1,0:T(1,128)S(1)} %bitcast.18, s32[1,32]{1,0:T(1,128)S(1)} %bitcast.22, s32[1,1]{1,0:T(1,128)S(6)} %copy.12.count, s32[1]{0:T(128)} %bitcast.1.core, bf16[32,128,128]{2,1,0:T(8,128)(2,1)S(1)} %bitcast.11, bf16[16,128,256]{2,1,0:T(8,128)(2,1)S(1)} %bitcast.16), custom_call_target="tpu_custom_call" | custom-call | flops 300000000 | bytes 4000000 | tf_op jit(solution)/shard_map/pallas_call | solution.py:309
  39.6 0.0 collective-permute-done.other
  39.6 2.9 %shard_map.112 = (bf16[4,400,256]{2,1,0:T(8,128)(2,1)S(1)}, bf16[128,256]{1,0:T(8,128)(2,1)S(1)}, bf16[128,256]{1,0:T(8,128)(2,1)S(1)}, bf16[128,256]{1,0:T(8,128)(2,1)S(1)}, bf16[128,256]{1,0:T(8,128)(2,1)S(1)}) custom-call(s32[1,32]{1,0:T(1,128)S(1)} %bitcast.19, s32[1,32]{1,0:T(1,128)S(1)} %bitcast.23, s32[1,1]{1,0:T(1,128)S(6)} %copy.12.count, ...), custom_call_target="tpu_custom_call" | custom-call | flops 300000000 | bytes 4000000 | tf_op jit(solution)/shard_map/pallas_call | solution.py:318
  42.5 15.0 %all_to_all.42.recv = bf16[4,400,256]{2,1,0:T(8,128)(2,1)S(1)} all-to-all(bf16[4,400,256]{2,1,0:T(8,128)(2,1)S(1)} %get-tuple-element.20), channel_id=1, replica_groups=mesh['x'=4,'zl'=4,'k'=2,'zh'=4,'y'=4] {'y'}, dimensions={0} | all-to-all | bytes 1638400 | tf_op jit(solution)/shard_map/all_to_all | solution.py:268
  57.5 0.0 copy-start.1
  57.5 0.0 copy-start.2
  57.5 0.0 copy-start.3
  57.5 0.0 copy-start.6
  57.5 0.8 shard_map.113
  58.4 12.3 %all-to-all-start.3 = ((bf16[4,144,256]{2,1,0:T(8,128)(2,1)}), bf16[4,144,256]{2,1,0:T(8,128)(2,1)S(1)}, u32[]{:S(2)}, u32[]{:S(2)}) async-start(bf16[4,144,256]{2,1,0:T(8,128)(2,1)} %shard_map.113), calls=%async_computation.3 | async-start | bytes 589824 | tf_op jit(solution)/shard_map/all_to_all | solution.py:283
  70.7 2.2 %collective-permute-start.1 = (bf16[128,256]{1,0:T(8,128)(2,1)S(1)}, bf16[128,256]{1,0:T(8,128)(2,1)S(1)}, u32[]{:S(2)}, u32[]{:S(2)}) collective-permute-start(bf16[128,256]{1,0:T(8,128)(2,1)S(1)} %get-tuple-element.22), channel_id=1, source_target_pairs={{0,1},{1,2},{2,3},{3,0},{4,5},{5,6},{6,7},{7,4},{8,9},{9,10},{10,1... | collective-permute-start | bytes 196616 | tf_op jit(solution)/shard_map/ppermute | solution.py:288
  72.9 3.7 %collective-permute-start.2 = (bf16[128,256]{1,0:T(8,128)(2,1)S(1)}, bf16[128,256]{1,0:T(8,128)(2,1)S(1)}, u32[]{:S(2)}, u32[]{:S(2)}) collective-permute-start(bf16[128,256]{1,0:T(8,128)(2,1)S(1)} %get-tuple-element.23), channel_id=1, source_target_pairs={{0,2},{1,3},{2,0},{3,1},{4,6},{5,7},{6,4},{7,5},{8,10},{9,11},{10,... | collective-permute-start | bytes 196616 | tf_op jit(solution)/shard_map/ppermute | solution.py:288
  76.6 2.8 %collective-permute-start.3 = (bf16[128,256]{1,0:T(8,128)(2,1)S(1)}, bf16[128,256]{1,0:T(8,128)(2,1)S(1)}, u32[]{:S(2)}, u32[]{:S(2)}) collective-permute-start(bf16[128,256]{1,0:T(8,128)(2,1)S(1)} %get-tuple-element.24), channel_id=1, source_target_pairs={{0,3},{1,0},{2,1},{3,2},{4,7},{5,4},{6,5},{7,6},{8,11},{9,8},{10,9... | collective-permute-start | bytes 196616 | tf_op jit(solution)/shard_map/ppermute | solution.py:288
  79.4 0.0 collective-permute-done.1.near1
  79.4 0.3 collective-permute-done.2.near2
  79.7 2.8 %collective-permute-done.3.near3 = bf16[128,256]{1,0:T(8,128)(2,1)S(1)} collective-permute-done((bf16[128,256]{1,0:T(8,128)(2,1)S(1)}, bf16[128,256]{1,0:T(8,128)(2,1)S(1)}, u32[]{:S(2)}, u32[]{:S(2)}) %collective-permute-start.3) | collective-permute-done | bytes 65568 | tf_op jit(solution)/shard_map/ppermute | solution.py:288
  82.5 0.0 all-to-all-done.3.recv
  82.5 0.0 copy-done.1
  82.5 0.0 copy-done.2
  82.5 0.0 copy-done.3
  82.5 0.0 copy-done.6
  82.5 0.9 shard_map.114
  83.4 20.4 %all-gather = bf16[1024,256]{1,0:T(8,128)(2,1)S(1)} all-gather(bf16[256,256]{1,0:T(8,128)(2,1)S(1)} %get-tuple-element.26), channel_id=2, replica_groups=mesh['x'=4,'zl'=4,'k'=2,'zh'=4,'y'=4] {'zh'}, dimensions={0}, use_global_device_ids=true | all-gather | bytes 655360 | tf_op jit(solution)/shard_map/all_gather | solution.py:341
  103.9 0.5 shard_map.115
  104.3 16.1 %all_to_all.43.spread = bf16[4,592,256]{2,1,0:T(8,128)(2,1)S(1)} all-to-all(bf16[4,592,256]{2,1,0:T(8,128)(2,1)S(1)} %shard_map.115), channel_id=1, replica_groups=mesh['x'=4,'zl'=4,'k'=2,'zh'=4,'y'=4] {'y'}, dimensions={0} | all-to-all | bytes 2424832 | tf_op jit(solution)/shard_map/all_to_all | solution.py:268
  120.4 2.5 %shard_map.117 = bf16[2128,256]{1,0:T(8,128)(2,1)S(1)} custom-call(s32[1,32]{1,0:T(1,128)S(1)} %bitcast.20, s32[1,32]{1,0:T(1,128)S(1)} %bitcast.24, s32[1,1]{1,0:T(1,128)S(6)} %copy.12.count, s32[1]{0:T(128)} %bitcast.1.core, bf16[32,128,128]{2,1,0:T(8,128)(2,1)S(1)} %bitcast.13, bf16[4,592,256]{2,1,0:T(8,128)(2,1)S(1)} %all_to_all.43.spread), custom_call_target="tpu_custom_call" | custom-call | flops 300000000 | bytes 4000000 | tf_op jit(solution)/shard_map/pallas_call | solution.py:348
  122.9 11.6 %collective-permute-start.4 = (bf16[2128,256]{1,0:T(8,128)(2,1)S(1)}, bf16[2128,256]{1,0:T(8,128)(2,1)S(1)}, u32[]{:S(2)}, u32[]{:S(2)}) collective-permute-start(bf16[2128,256]{1,0:T(8,128)(2,1)S(1)} %shard_map.117), channel_id=1, source_target_pairs={{0,16},{16,0},{1,17},{17,1},{2,18},{18,2},{3,19},{19,3},{4,20},{20... | collective-permute-start | bytes 3268616 | tf_op jit(solution)/shard_map/ppermute | solution.py:357
  134.5 2.5 %shard_map.116.keep = bf16[2128,256]{1,0:T(8,128)(2,1)S(1)} custom-call(s32[1,32]{1,0:T(1,128)S(1)} %bitcast.21, s32[1,32]{1,0:T(1,128)S(1)} %bitcast.25, s32[1,1]{1,0:T(1,128)S(6)} %copy.12.count, s32[1]{0:T(128)} %bitcast.1.core, bf16[32,128,128]{2,1,0:T(8,128)(2,1)S(1)} %bitcast.14, bf16[4,592,256]{2,1,0:T(8,128)(2,1)S(1)} %all_to_all.43.spread), custom_call_target="tpu_custom_call" | custom-call | flops 300000000 | bytes 4000000 | tf_op jit(solution)/shard_map/pallas_call | solution.py:348
  137.0 0.0 collective-permute-done.4.recv
  137.0 0.3 shard_map.118
  137.3 25.8 %all_to_all.44.recv = bf16[4,592,256]{2,1,0:T(8,128)(2,1)S(1)} all-to-all(bf16[4,592,256]{2,1,0:T(8,128)(2,1)S(1)} %shard_map.118), channel_id=1, replica_groups={{0,128,256,384},{32,160,288,416},{64,192,320,448},{96,224,352,480},{16,..., dimensions={0} | all-to-all | bytes 2424832 | tf_op jit(solution)/shard_map/all_to_all | solution.py:278
  163.1 0.2 shard_map.119
  163.3 8.8 %all_to_all.45.recv = bf16[4,208,256]{2,1,0:T(8,128)(2,1)S(1)} all-to-all(bf16[4,208,256]{2,1,0:T(8,128)(2,1)S(1)} %shard_map.119), channel_id=1, replica_groups={{0,32,64,96},{128,160,192,224},{256,288,320,352},{384,416,448,480},{16,..., dimensions={0} | all-to-all | bytes 851968 | tf_op jit(solution)/shard_map/all_to_all | solution.py:278
  172.0 0.7 shard_map.120
  172.7 7.5 %all_to_all.46 = bf16[4,64,256]{2,1,0:T(8,128)(2,1)S(1)} all-to-all(bf16[4,64,256]{2,1,0:T(8,128)(2,1)S(1)} %get-tuple-element.30), channel_id=1, replica_groups=mesh['x'=4,'zl'=4,'k'=2,'zh'=4,'y'=4] {'y'}, dimensions={0} | all-to-all | bytes 262144 | tf_op jit(solution)/shard_map/all_to_all | solution.py:268
  180.2 0.7 convert_multiply_fusion
Async XLA Ops:
  13.8 23.5 %copy-start = (bf16[1,1,32,128,128]{4,3,2,1,0:T(8,128)(2,1)S(1)}, bf16[1,1,32,128,128]{4,3,2,1,0:T(8,128)(2,1)}, u32[]{:S(2)}) copy-start(bf16[1,1,32,128,128]{4,3,2,1,0:T(8,128)(2,1)} %param.14) | copy-start | bytes 3145732
  13.8 23.5 %copy-start.4 = (s32[1,1,32]{2,1,0:T(1,128)S(1)}, s32[1,1,32]{2,1,0:T(1,128)}, u32[]{:S(2)}) copy-start(s32[1,1,32]{2,1,0:T(1,128)} %param.12) | copy-start | bytes 388
  13.8 23.5 %copy-start.5 = (s32[1,1,32]{2,1,0:T(1,128)S(1)}, s32[1,1,32]{2,1,0:T(1,128)}, u32[]{:S(2)}) copy-start(s32[1,1,32]{2,1,0:T(1,128)} %param.13) | copy-start | bytes 388
  30.6 9.0 %collective-permute-start = (bf16[16,128,256]{2,1,0:T(8,128)(2,1)S(1)}, bf16[16,128,256]{2,1,0:T(8,128)(2,1)S(1)}, u32[]{:S(2)}, u32[]{:S(2)}) collective-permute-start(bf16[16,128,256]{2,1,0:T(8,128)(2,1)S(1)} %bitcast.15), channel_id=1, source_target_pairs={{0,16},{16,0},{1,17},{17,1},{2,18},{18,2},{3,19},{19,3},{4,20},{20... | collective-permute-start | bytes 3145736 | tf_op jit(solution)/shard_map/ppermute | solution.py:306
  57.5 25.0 %copy-start.1 = (bf16[256,256]{1,0:T(8,128)(2,1)S(1)}, bf16[256,256]{1,0:T(8,128)(2,1)}, u32[]{:S(2)}) copy-start(bf16[256,256]{1,0:T(8,128)(2,1)} %weight.3) | copy-start | bytes 393220
  57.5 25.0 %copy-start.2 = (bf16[128,256]{1,0:T(8,128)(2,1)S(1)}, bf16[128,256]{1,0:T(8,128)(2,1)}, u32[]{:S(2)}) copy-start(bf16[128,256]{1,0:T(8,128)(2,1)} %features.1) | copy-start | bytes 196612
  57.5 25.0 %copy-start.3 = (bf16[128,256]{1,0:T(8,128)(2,1)S(1)}, bf16[128,256]{1,0:T(8,128)(2,1)}, u32[]{:S(2)}) copy-start(bf16[128,256]{1,0:T(8,128)(2,1)} %grad_out.1) | copy-start | bytes 196612
  57.5 25.0 %copy-start.6 = (f32[256]{0:T(256)S(1)}, f32[256]{0:T(256)}, u32[]{:S(2)}) copy-start(f32[256]{0:T(256)} %param.11) | copy-start | bytes 3076
  58.4 24.1 %all-to-all-start.3 = ((bf16[4,144,256]{2,1,0:T(8,128)(2,1)}), bf16[4,144,256]{2,1,0:T(8,128)(2,1)S(1)}, u32[]{:S(2)}, u32[]{:S(2)}) async-start(bf16[4,144,256]{2,1,0:T(8,128)(2,1)} %shard_map.113), calls=%async_computation.3 | async-start | bytes 589824 | tf_op jit(solution)/shard_map/all_to_all | solution.py:283
  70.7 8.7 %collective-permute-start.1 = (bf16[128,256]{1,0:T(8,128)(2,1)S(1)}, bf16[128,256]{1,0:T(8,128)(2,1)S(1)}, u32[]{:S(2)}, u32[]{:S(2)}) collective-permute-start(bf16[128,256]{1,0:T(8,128)(2,1)S(1)} %get-tuple-element.22), channel_id=1, source_target_pairs={{0,1},{1,2},{2,3},{3,0},{4,5},{5,6},{6,7},{7,4},{8,9},{9,10},{10,1... | collective-permute-start | bytes 196616 | tf_op jit(solution)/shard_map/ppermute | solution.py:288
  72.9 6.8 %collective-permute-start.2 = (bf16[128,256]{1,0:T(8,128)(2,1)S(1)}, bf16[128,256]{1,0:T(8,128)(2,1)S(1)}, u32[]{:S(2)}, u32[]{:S(2)}) collective-permute-start(bf16[128,256]{1,0:T(8,128)(2,1)S(1)} %get-tuple-element.23), channel_id=1, source_target_pairs={{0,2},{1,3},{2,0},{3,1},{4,6},{5,7},{6,4},{7,5},{8,10},{9,11},{10,... | collective-permute-start | bytes 196616 | tf_op jit(solution)/shard_map/ppermute | solution.py:288
  76.6 5.9 %collective-permute-start.3 = (bf16[128,256]{1,0:T(8,128)(2,1)S(1)}, bf16[128,256]{1,0:T(8,128)(2,1)S(1)}, u32[]{:S(2)}, u32[]{:S(2)}) collective-permute-start(bf16[128,256]{1,0:T(8,128)(2,1)S(1)} %get-tuple-element.24), channel_id=1, source_target_pairs={{0,3},{1,0},{2,1},{3,2},{4,7},{5,4},{6,5},{7,6},{8,11},{9,8},{10,9... | collective-permute-start | bytes 196616 | tf_op jit(solution)/shard_map/ppermute | solution.py:288
  122.9 14.1 %collective-permute-start.4 = (bf16[2128,256]{1,0:T(8,128)(2,1)S(1)}, bf16[2128,256]{1,0:T(8,128)(2,1)S(1)}, u32[]{:S(2)}, u32[]{:S(2)}) collective-permute-start(bf16[2128,256]{1,0:T(8,128)(2,1)S(1)} %shard_map.117), channel_id=1, source_target_pairs={{0,16},{16,0},{1,17},{17,1},{2,18},{18,2},{3,19},{19,3},{4,20},{20... | collective-permute-start | bytes 3268616 | tf_op jit(solution)/shard_map/ppermute | solution.py:357
